TPU v7x, 512 devices: a whole 4x4x16 slice. The times are simulated.
512 devices in a mesh: dp: 128 (over z, y, core), fsdp: 4 (over x).
Axes of the slice: x: 4, y: 4, z: 16, core: 2. Of those that a mesh axis runs over, the one named last changes fastest.
Arguments:
- tiles: bfloat16 [768, 65536], P('fsdp', 'dp'), may hold values from -6 to 6
- kernel: bfloat16 [49, 768], P(None, 'fsdp'), may hold values from -0.875 to 0.875
- norm_gain: bfloat16 [768], P('fsdp'), may hold values from 0.099609375 to 1.8984375
- w_up: bfloat16 [768, 1536], P('dp', 'fsdp'), may hold values from -0.21875 to 0.21875
- w_down: bfloat16 [768, 1536], P('dp', 'fsdp'), may hold values from -0.15625 to 0.15625
- layer_scale: bfloat16 [768], P('fsdp'), may hold values from 0.5 to 2
- neighbors: int32 [1024, 4, 2], P('dp'), may hold values from -1 to 1023, as said below
- shifts: int32 [1024, 4, 2], P('dp'), may hold values from -8 to 7, as said below
- halo_widths: int32 [1024, 4], P('dp'), may hold values from 1 to 3
- land: int32 [1024, 8, 8], P('dp'), may hold values 0 or 1
- cotangent: bfloat16 [768, 65536], P('fsdp', 'dp'), may hold values from -6 to 6
Outputs:
- block_out: bfloat16 [768, 65536], P('fsdp', 'dp')
- tile_grad: bfloat16 [768, 65536], P('fsdp', 'dp')
- up_grad: float32 [768, 1536], P('dp', 'fsdp')
- down_grad: float32 [768, 1536], P('dp', 'fsdp')
Inputs may be any that keep to these rules, and one draw needn't show every extreme that they name: `neighbors`: faces are north, south, west, east. Tile t is held by index t // 8 of dp. A named north or south neighbour is held by the same index of dp as the tile, a west one by the index before, an east one by the index after. Adjacency is symmetric: a cell taken from a neighbour's edge belongs to the tile that takes the facing cell of it. Entry 0 of a face holds shifts 0 to 7, entry 1 shifts -8 to -1; an entry that names no tile has shift 0, and north and south shifts are 0.
All inputs are finite; a program needn't handle non-finite values. No bound on the sum of `land` on one device may be relied on, other than what follows from the above.
Results may differ from a plain program's by a relative error of at most 0.0095.
Values may be sent and summed in bfloat16 or wider, within the bound.
A program may use at most 64 MiB of HBM per device.

v0:
```python
import math

import jax
import jax.numpy as jnp
from jax import lax
from jax.sharding import PartitionSpec as P

root_half = 1.0 / math.sqrt(2.0)
root_tau = 1.0 / math.sqrt(2.0 * math.pi)


def padded_2(block, sides, width):
    for axis, dim in sides:
        count = lax.axis_size(axis)
        forward = [(i, i + 1) for i in range(count - 1)]
        backward = [(target, source) for source, target in forward]
        low = lax.ppermute(
            lax.slice_in_dim(block, block.shape[dim] - width, None, axis=dim), axis, forward
        )
        high = lax.ppermute(lax.slice_in_dim(block, 0, width, axis=dim), axis, backward)
        block = jnp.concatenate([low, block, high], axis=dim)
    return block


def gelu_value(hidden):
    return 0.5 * hidden * (1.0 + jax.scipy.special.erf(hidden * root_half))


def gelu_slope(hidden):
    return (
        0.5 * (1.0 + jax.scipy.special.erf(hidden * root_half))
        + hidden * jnp.exp(-0.5 * hidden * hidden) * root_tau
    )


def depth_keep(widths_face, far_first):
    layer_index = jnp.arange(3, dtype=jnp.int32)
    if far_first:
        depth_value = 3 - layer_index
    else:
        depth_value = layer_index + 1
    return depth_value[None, :] <= widths_face[:, None]


def depthwise_flat(padded, kernel):
    channels, tile_count, wide, _ = padded.shape
    total = tile_count * wide * wide
    flat = jnp.pad(padded.reshape(channels, total), ((0, 0), (0, 6 * wide + 6)))
    taps = kernel.astype(jnp.float32)
    summed = jnp.zeros((channels, total), jnp.float32)
    for row_tap in range(7):
        for col_tap in range(7):
            offset = row_tap * wide + col_tap
            summed = (
                summed
                + flat[:, offset : offset + total].astype(jnp.float32)
                * taps[row_tap * 7 + col_tap][:, None]
            )
    side_len = wide - 6
    return summed.reshape(channels, tile_count, wide, wide)[:, :, :side_len, :side_len]


def depthwise_back_flat(grad_grid, kernel):
    channels, tile_count, side_len, _ = grad_grid.shape
    wide = side_len + 6
    total = tile_count * wide * wide
    lead = 6 * wide + 6
    placed = jnp.pad(grad_grid.astype(jnp.float32), ((0, 0), (0, 0), (0, 6), (0, 6))).reshape(
        channels, total
    )
    placed = jnp.pad(placed, ((0, 0), (lead, 0)))
    taps = kernel.astype(jnp.float32)
    summed = jnp.zeros((channels, total), jnp.float32)
    for row_tap in range(7):
        for col_tap in range(7):
            offset = row_tap * wide + col_tap
            summed = (
                summed
                + placed[:, lead - offset : lead - offset + total]
                * taps[row_tap * 7 + col_tap][:, None]
            )
    return summed.reshape(channels, tile_count, wide, wide)


def selection(neighbor_ids, shift_values, tile_count, side_len):
    position = jnp.arange(side_len, dtype=jnp.int32)
    source_tile = jnp.arange(tile_count, dtype=jnp.int32)
    summed = jnp.zeros((tile_count, side_len, tile_count, side_len), jnp.float32)
    for which_entry in range(2):
        owner_tile = neighbor_ids[:, which_entry]
        slot_index = jnp.where(owner_tile >= 0, owner_tile % tile_count, -1)
        along_edge = position[None, :] + shift_values[:, which_entry][:, None]
        tile_hit = slot_index[:, None] == source_tile[None, :]
        row_hit = along_edge[:, :, None] == position[None, None, :]
        summed = summed + (tile_hit[:, None, :, None] & row_hit[:, :, None, :]).astype(jnp.float32)
    return summed.reshape(tile_count * side_len, tile_count * side_len)


def per_device(
    tiles,
    kernel,
    norm_gain,
    w_up,
    w_down,
    layer_scale,
    neighbors,
    shifts,
    halo_widths,
    land,
    cotangent,
):
    channels = tiles.shape[0]
    tile_count, side_len = (land.shape[0], land.shape[1])
    row_count = tile_count * side_len * side_len
    face_cols = tile_count * side_len
    full_width = channels * lax.axis_size("fsdp")
    grid_in = tiles.reshape(channels, tile_count, side_len, side_len)
    north_src = jnp.transpose(grid_in[:, :, side_len - 3 :, :], (2, 0, 1, 3))
    south_src = jnp.transpose(grid_in[:, :, :3, :], (2, 0, 1, 3))
    west_src = jnp.transpose(grid_in[:, :, :, side_len - 3 :], (3, 0, 1, 2))
    east_src = jnp.transpose(grid_in[:, :, :, :3], (3, 0, 1, 2))
    edges = padded_2(jnp.stack([east_src, west_src]), (("dp", 0),), 1)
    faces = (north_src, south_src, edges[0], edges[3])
    selectors = []
    masks = []
    halos = []
    for face_index in range(4):
        selector = selection(neighbors[:, face_index], shifts[:, face_index], tile_count, side_len)
        keep = depth_keep(halo_widths[:, face_index], face_index in (0, 2))
        keep_mask = jnp.transpose(keep)[:, None, :, None]
        picked = jnp.dot(
            faces[face_index].reshape(3 * channels, face_cols),
            selector.T.astype(jnp.bfloat16),
            preferred_element_type=jnp.float32,
        )
        halos.append(
            jnp.where(keep_mask, picked.reshape(3, channels, tile_count, side_len), 0.0).astype(
                jnp.bfloat16
            )
        )
        selectors.append(selector)
        masks.append(keep_mask)
    up_full, down_full = (
        lax.all_gather(w_up, "dp", axis=0, tiled=True),
        lax.all_gather(w_down, "dp", axis=0, tiled=True),
    )
    corner = jnp.zeros((channels, tile_count, 3, 3), jnp.bfloat16)
    upper = jnp.concatenate([corner, jnp.transpose(halos[0], (1, 2, 0, 3)), corner], axis=3)
    lower = jnp.concatenate([corner, jnp.transpose(halos[1], (1, 2, 0, 3)), corner], axis=3)
    middle = jnp.concatenate(
        [jnp.transpose(halos[2], (1, 2, 3, 0)), grid_in, jnp.transpose(halos[3], (1, 2, 3, 0))],
        axis=3,
    )
    padded = jnp.concatenate([upper, middle, lower], axis=2)
    conv = depthwise_flat(padded, kernel)
    conv_rows = conv.reshape(channels, row_count).astype(jnp.bfloat16)
    gain_f = norm_gain.astype(jnp.float32)[:, None]
    values = lax.optimization_barrier(conv_rows).astype(jnp.float32)
    row_total, row_squares = lax.psum(
        (jnp.sum(values, axis=0), jnp.sum(values * values, axis=0)), "fsdp"
    )
    row_mean = row_total / full_width
    inv_scale = lax.rsqrt(row_squares / full_width - row_mean * row_mean + 1e-06)
    centered = (values - row_mean[None, :]) * inv_scale[None, :]
    normed = lax.all_gather((centered * gain_f).astype(jnp.bfloat16), "fsdp", axis=0, tiled=True)
    pre_act = lax.dot_general(
        normed, up_full, (((0,), (0,)), ((), ())), preferred_element_type=jnp.float32
    )
    hidden = gelu_value(pre_act).astype(jnp.bfloat16)
    partial_out = lax.dot_general(
        down_full, hidden, (((1,), (1,)), ((), ())), preferred_element_type=jnp.float32
    )
    mixed = lax.psum_scatter(
        partial_out.astype(jnp.bfloat16), "fsdp", scatter_dimension=0, tiled=True
    ).astype(jnp.float32)
    scale_f = layer_scale.astype(jnp.float32)[:, None]
    block_out = (tiles.astype(jnp.float32) + scale_f * mixed).astype(jnp.bfloat16)
    grad_out = cotangent * land.reshape(row_count)[None, :].astype(jnp.bfloat16)
    grad_mixed = (scale_f * grad_out.astype(jnp.float32)).astype(jnp.bfloat16)
    grad_mixed_all = lax.all_gather(grad_mixed, "fsdp", axis=0, tiled=True)
    down_local = jnp.dot(grad_mixed_all, hidden, preferred_element_type=jnp.float32)
    grad_hidden = lax.dot_general(
        grad_mixed_all, down_full, (((0,), (0,)), ((), ())), preferred_element_type=jnp.float32
    )
    grad_pre = (grad_hidden * gelu_slope(pre_act)).astype(jnp.bfloat16)
    partial_grad = lax.dot_general(
        up_full, grad_pre, (((1,), (1,)), ((), ())), preferred_element_type=jnp.float32
    )
    grad_normed = lax.psum_scatter(
        partial_grad.astype(jnp.bfloat16), "fsdp", scatter_dimension=0, tiled=True
    ).astype(jnp.float32)
    up_local = jnp.dot(normed, grad_pre, preferred_element_type=jnp.float32)
    grad_centered = grad_normed * gain_f
    first_sum, second_sum = lax.psum(
        (jnp.sum(grad_centered, axis=0), jnp.sum(grad_centered * centered, axis=0)), "fsdp"
    )
    grad_conv = (
        inv_scale[None, :]
        * (
            grad_centered
            - first_sum[None, :] / full_width
            - centered * (second_sum[None, :] / full_width)
        )
    ).astype(jnp.bfloat16)
    grad_pad = depthwise_back_flat(
        grad_conv.reshape(channels, tile_count, side_len, side_len), kernel
    )
    inner = slice(3, 3 + side_len)

    def returned(face_index, grad_face):
        masked = jnp.where(masks[face_index], grad_face, 0.0).reshape(3 * channels, face_cols)
        moved = jnp.dot(
            masked,
            selectors[face_index],
            precision=lax.Precision.HIGHEST,
            preferred_element_type=jnp.float32,
        )
        return moved.reshape(3, channels, tile_count, side_len)

    tile_grad = (
        grad_out.astype(jnp.float32).reshape(channels, tile_count, side_len, side_len)
        + grad_pad[:, :, inner, inner]
    )
    edge_north = returned(0, jnp.transpose(grad_pad[:, :, 0:3, inner], (2, 0, 1, 3)))
    tile_grad = tile_grad + jnp.pad(
        jnp.transpose(edge_north, (1, 2, 0, 3)), ((0, 0), (0, 0), (side_len - 3, 0), (0, 0))
    )
    edge_south = returned(1, jnp.transpose(grad_pad[:, :, side_len + 3 :, inner], (2, 0, 1, 3)))
    tile_grad = tile_grad + jnp.pad(
        jnp.transpose(edge_south, (1, 2, 0, 3)), ((0, 0), (0, 0), (0, side_len - 3), (0, 0))
    )
    edge_west = returned(2, jnp.transpose(grad_pad[:, :, inner, 0:3], (3, 0, 1, 2)))
    edge_east = returned(3, jnp.transpose(grad_pad[:, :, inner, side_len + 3 :], (3, 0, 1, 2)))
    coming = padded_2(
        jnp.stack([edge_west, edge_east]).astype(jnp.bfloat16), (("dp", 0),), 1
    ).astype(jnp.float32)
    tile_grad = tile_grad + jnp.pad(
        jnp.transpose(coming[0], (1, 2, 3, 0)), ((0, 0), (0, 0), (0, 0), (0, side_len - 3))
    )
    tile_grad = tile_grad + jnp.pad(
        jnp.transpose(coming[3], (1, 2, 3, 0)), ((0, 0), (0, 0), (0, 0), (side_len - 3, 0))
    )
    up_grad, down_grad = (
        lax.psum_scatter(up_local, "dp", scatter_dimension=0, tiled=True),
        lax.psum_scatter(down_local, "dp", scatter_dimension=0, tiled=True),
    )
    return (
        block_out,
        tile_grad.reshape(channels, row_count).astype(jnp.bfloat16),
        up_grad,
        down_grad,
    )


def solution(mesh):
    return jax.shard_map(
        per_device,
        mesh=mesh,
        in_specs=(
            P("fsdp", "dp"),
            P(None, "fsdp"),
            P("fsdp"),
            P("dp", "fsdp"),
            P("dp", "fsdp"),
            P("fsdp"),
            P("dp", None, None),
            P("dp", None, None),
            P("dp", None),
            P("dp", None, None),
            P("fsdp", "dp"),
        ),
        out_specs=(P("fsdp", "dp"), P("fsdp", "dp"), P("dp", "fsdp"), P("dp", "fsdp")),
        check_vma=False,
    )
```

profile of v0, /device:TPU:1, one launch (start us, length us, event | category | flops | bytes accessed | tf_op | source)
XLA Modules:
  0.0 737.8 jit_solution(6048609424690734368)
XLA Ops:
  7.2 1.1 copy.110
  8.4 4.6 collective-permute-start
  13.0 5.5 collective-permute-start.1
  18.5 1.0 fusion.72
  19.6 1.0 fusion.71
  20.8 1.7 fusion.70
  22.5 0.7 convert_element_type.380
  23.2 0.8 slice_bitcast_fusion.25
  24.0 0.7 slice_bitcast_fusion.13
  24.9 0.7 slice_bitcast_fusion.12
  27.6 0.2 convolution_bitcast_fusion.5
  28.1 0.2 convolution_bitcast_fusion.2
  28.4 99.4 %all-gather = bf16[128,6,384]{2,1,0:T(8,128)(2,1)S(1)} all-gather(bf16[1,6,384]{2,1,0:T(8,128)(2,1)S(1)} %bitcast.415), channel_id=1, replica_groups=mesh['dp'=128,'fsdp'=4] {'dp'}, dimensions={0}, use_global_device_ids=true | all-gather | bytes 594432 | tf_op jit(solution)/shard_map/all_gather | solution.py:144
  127.8 0.2 reshape.696
  128.4 96.6 %all-gather.1 = bf16[128,6,384]{2,1,0:T(8,128)(2,1)S(1)} all-gather(bf16[1,6,384]{2,1,0:T(8,128)(2,1)S(1)} %bitcast.416), channel_id=1, replica_groups=mesh['dp'=128,'fsdp'=4] {'dp'}, dimensions={0}, use_global_device_ids=true | all-gather | bytes 594432 | tf_op jit(solution)/shard_map/all_gather | solution.py:145
  225.0 0.2 reshape.698
  225.3 0.2 convolution_bitcast_fusion.4
  226.5 0.6 maximum_maximum_fusion
  227.1 0.4 reshape.685
  227.8 16.6 %add_convert_fusion = bf16[192,1568]{0,1:T(8,128)(2,1)S(1)} fusion(bf16[192,1568]{0,1:T(8,128)(2,1)S(1)} %reshape.685, f32[192]{0:T(256)S(1)} %bitcast.375, f32[192]{0:T(256)S(1)} %bitcast.373, f32[192]{0:T(256)S(1)} %bitcast.371, f32[192]{0:T(256)S(1)} %bitcast.369, f32[192]{0:T(256)S(1)} %bitcast.367, f32[192]{0:T(256)S(1)} %bitcast.365, ...), kind=kLoop, calls=%fused_computation.4 | loop fusion | flops 44255232 | bytes 1241856 | tf_op jit(solution)/shard_map/convert.9
  244.4 0.3 reshape.686
  244.7 0.2 convert_reduce_fusion
  244.9 8.5 %all-reduce.11 = (f32[512]{0:T(512)S(1)}, f32[512]{0:T(512)S(1)}) all-reduce(f32[512]{0:T(512)S(1)} %get-tuple-element.27, f32[512]{0:T(512)S(1)} %get-tuple-element.26), channel_id=1, replica_groups=mesh['dp'=128,'fsdp'=4] {'fsdp'}, use_global_device_ids=true, to_apply=%region_3.4 | all-reduce | flops 1024 | bytes 8192 | tf_op jit(solution)/shard_map/psum | solution.py:159
  253.4 0.2 fusion.13
  253.8 10.8 %all_gather.12 = bf16[768,512]{1,0:T(8,128)(2,1)S(1)} all-gather(bf16[192,512]{1,0:T(8,128)(2,1)S(1)} %copy.119), channel_id=1, replica_groups=mesh['dp'=128,'fsdp'=4] {'fsdp'}, dimensions={0}, use_global_device_ids=true | all-gather | bytes 983040 | tf_op jit(solution)/shard_map/all_gather | solution.py:165
  264.6 1.5 multiply_convert_fusion
  266.1 0.6 fusion.2
  266.7 1.2 copy.138
  268.1 24.0 %reduce-scatter.7.cloned.1.call-done = bf16[192,512]{1,0:T(8,128)(2,1)} async-done(((bf16[768,512]{1,0:T(8,128)(2,1)}), bf16[192,512]{1,0:T(8,128)(2,1)}) %reduce-scatter.7.cloned.1.call-update) | async-done | bytes 196624 | tf_op jit(solution)/shard_map/reduce_scatter | solution.py:173
  292.2 1.9 multiply_convert_fusion.1
  294.1 11.3 %all_gather.15 = bf16[768,512]{1,0:T(8,128)(2,1)S(1)} all-gather(bf16[192,512]{1,0:T(8,128)(2,1)S(1)} %get-tuple-element.107), channel_id=1, replica_groups=mesh['dp'=128,'fsdp'=4] {'fsdp'}, dimensions={0}, use_global_device_ids=true | all-gather | bytes 983040 | tf_op jit(solution)/shard_map/all_gather | solution.py:180
  305.4 1.6 fusion.82
  307.0 0.7 fusion.4
  307.7 1.6 fusion.81
  309.4 0.3 reduce-scatter.9.cloned.1.call-start
  309.6 0.6 fusion.3
  310.2 1.2 copy.140
  311.5 1.0 copy.121
  312.5 1.3 dynamic-slice
  314.4 348.2 %all-reduce.14.cloned.1.call-done = (f32[768,384]{1,0:T(8,128)}, f32[768,384]{1,0:T(8,128)}) async-done(((f32[768,384]{1,0:T(8,128)}, f32[768,384]{1,0:T(8,128)}), (f32[768,384]{1,0:T(8,128)}, f32[768,384]{1,0:T(8,128)})) %all-reduce.14.cloned.1.call-update) | async-done | bytes 2359312
  662.6 1.3 constant_dynamic-slice_fusion.1
  664.0 1.3 constant_dynamic-slice_fusion
  665.3 27.3 %reduce-scatter.9.cloned.1.call-done = bf16[192,512]{1,0:T(8,128)(2,1)} async-done(((bf16[768,512]{1,0:T(8,128)(2,1)}), bf16[192,512]{1,0:T(8,128)(2,1)}) %reduce-scatter.9.cloned.1.call-update) | async-done | bytes 196624
  692.6 1.1 copy.141
  693.7 0.4 fusion.24
  694.1 6.0 all-reduce.10
  700.1 0.3 fusion.17
  700.5 0.2 pad_convert_fusion
  701.0 0.2 reshape.694
  701.2 0.2 copy-done.22
  701.6 14.7 %multiply_add_fusion = f32[192,1568]{0,1:T(8,128)S(1)} fusion(f32[192,1568]{0,1:T(8,128)S(1)} %reshape.694, f32[192]{0:T(256)S(1)} %bitcast.376, f32[192]{0:T(256)S(1)} %bitcast.374, f32[192]{0:T(256)S(1)} %bitcast.372, f32[192]{0:T(256)S(1)} %bitcast.370, f32[192]{0:T(256)S(1)} %bitcast.368, f32[192]{0:T(256)S(1)} %bitcast.366, f32[192]{0:T(256)S(1)} %bitcast.364, ...), kind=kLoop, calls=%fused_computation | loop fusion | flops 29202432 | bytes 2446080 | tf_op jit(solution)/shard_map/add | solution.py:78
  716.4 0.2 reshape.690
  716.6 0.4 copy-done.16
  717.3 0.5 copy-done.9
  717.8 0.3 convolution_bitcast_fusion.1
  718.1 0.4 convolution_convert_fusion.3
  718.7 0.4 convolution_convert_fusion.2
  719.2 6.1 collective-permute-start.3
  725.3 2.8 collective-permute-start.2
  728.1 0.3 convolution_bitcast_fusion
  728.4 0.4 collective-permute-done.3
  728.8 1.2 collective-permute-done.2
  730.2 0.2 fusion.23
  730.5 0.8 copy.133
  (245 shorter events, 5.3 us)
Async XLA Ops:
  7.2 285.0 %reduce-scatter.7.cloned.1.call-start = ((), (), s32[]{:S(2)}) async-start(), calls=%async_computation.2 | async-start | bytes 983040 | tf_op jit(solution)/shard_map/reduce_scatter | solution.py:173
  8.4 216.8 %collective-permute-start = (bf16[1,3,192,8,8]{2,1,4,3,0:T(4,128)(2,1)S(1)}, bf16[1,3,192,8,8]{2,1,4,3,0:T(4,128)(2,1)S(1)}, u32[]{:S(2)}, u32[]{:S(2)}) collective-permute-start(bf16[1,3,192,8,8]{2,1,4,3,0:T(4,128)(2,1)S(1)} %get-tuple-element.42), channel_id=1, source_target_pairs={{0,4},{4,8},{8,12},{12,16},{16,20},{20,24},{24,28},{28,32},{32,36}... | collective-permute-start | bytes 221192 | tf_op jit(solution)/shard_map/ppermute | solution.py:17
  13.0 212.8 %collective-permute-start.1 = (bf16[1,3,192,8,8]{2,1,4,3,0:T(4,128)(2,1)S(1)}, bf16[1,3,192,8,8]{2,1,4,3,0:T(4,128)(2,1)S(1)}, u32[]{:S(2)}, u32[]{:S(2)}) collective-permute-start(bf16[1,3,192,8,8]{2,1,4,3,0:T(4,128)(2,1)S(1)} %get-tuple-element.43), channel_id=1, source_target_pairs={{4,0},{8,4},{12,8},{16,12},{20,16},{24,20},{28,24},{32,28},{36,32}... | collective-permute-start | bytes 221192 | tf_op jit(solution)/shard_map/ppermute | solution.py:20
  19.5 208.0 %copy-start.21 = (f32[1,192]{1,0:T(1,128)}, f32[1,192]{1,0:T(1,128)S(1)}, u32[]{:S(2)}) copy-start(f32[1,192]{1,0:T(1,128)S(1)} %get-tuple-element.82) | copy-start | bytes 2308
  19.5 208.0 %copy-start.23 = (f32[1,192]{1,0:T(1,128)}, f32[1,192]{1,0:T(1,128)S(1)}, u32[]{:S(2)}) copy-start(f32[1,192]{1,0:T(1,128)S(1)} %get-tuple-element.83) | copy-start | bytes 2308
  19.5 208.0 %copy-start.25 = (f32[1,192]{1,0:T(1,128)}, f32[1,192]{1,0:T(1,128)S(1)}, u32[]{:S(2)}) copy-start(f32[1,192]{1,0:T(1,128)S(1)} %get-tuple-element.84) | copy-start | bytes 2308
  19.5 208.0 %copy-start.27 = (f32[1,192]{1,0:T(1,128)}, f32[1,192]{1,0:T(1,128)S(1)}, u32[]{:S(2)}) copy-start(f32[1,192]{1,0:T(1,128)S(1)} %get-tuple-element.85) | copy-start | bytes 2308
  19.6 208.0 %copy-start.29 = (f32[1,192]{1,0:T(1,128)}, f32[1,192]{1,0:T(1,128)S(1)}, u32[]{:S(2)}) copy-start(f32[1,192]{1,0:T(1,128)S(1)} %get-tuple-element.86) | copy-start | bytes 2308
  19.6 208.0 %copy-start.31 = (f32[1,192]{1,0:T(1,128)}, f32[1,192]{1,0:T(1,128)S(1)}, u32[]{:S(2)}) copy-start(f32[1,192]{1,0:T(1,128)S(1)} %get-tuple-element.87) | copy-start | bytes 2308
  19.6 208.0 %copy-start.33 = (f32[1,192]{1,0:T(1,128)}, f32[1,192]{1,0:T(1,128)S(1)}, u32[]{:S(2)}) copy-start(f32[1,192]{1,0:T(1,128)S(1)} %get-tuple-element.88) | copy-start | bytes 2308
  19.6 208.0 %copy-start.35 = (f32[1,192]{1,0:T(1,128)}, f32[1,192]{1,0:T(1,128)S(1)}, u32[]{:S(2)}) copy-start(f32[1,192]{1,0:T(1,128)S(1)} %get-tuple-element.89) | copy-start | bytes 2308
  19.6 208.0 %copy-start.37 = (f32[1,192]{1,0:T(1,128)}, f32[1,192]{1,0:T(1,128)S(1)}, u32[]{:S(2)}) copy-start(f32[1,192]{1,0:T(1,128)S(1)} %get-tuple-element.90) | copy-start | bytes 2308
  19.6 208.0 %copy-start.39 = (f32[1,192]{1,0:T(1,128)}, f32[1,192]{1,0:T(1,128)S(1)}, u32[]{:S(2)}) copy-start(f32[1,192]{1,0:T(1,128)S(1)} %get-tuple-element.91) | copy-start | bytes 2308
  19.6 208.0 %copy-start.41 = (f32[1,192]{1,0:T(1,128)}, f32[1,192]{1,0:T(1,128)S(1)}, u32[]{:S(2)}) copy-start(f32[1,192]{1,0:T(1,128)S(1)} %get-tuple-element.92) | copy-start | bytes 2308
  20.6 207.0 %copy-start.43 = (f32[1,192]{1,0:T(1,128)}, f32[1,192]{1,0:T(1,128)S(1)}, u32[]{:S(2)}) copy-start(f32[1,192]{1,0:T(1,128)S(1)} %get-tuple-element.63) | copy-start | bytes 2308
  20.7 207.0 %copy-start.45 = (f32[1,192]{1,0:T(1,128)}, f32[1,192]{1,0:T(1,128)S(1)}, u32[]{:S(2)}) copy-start(f32[1,192]{1,0:T(1,128)S(1)} %get-tuple-element.64) | copy-start | bytes 2308
  20.7 207.0 %copy-start.47 = (f32[1,192]{1,0:T(1,128)}, f32[1,192]{1,0:T(1,128)S(1)}, u32[]{:S(2)}) copy-start(f32[1,192]{1,0:T(1,128)S(1)} %get-tuple-element.65) | copy-start | bytes 2308
  20.7 207.0 %copy-start.49 = (f32[1,192]{1,0:T(1,128)}, f32[1,192]{1,0:T(1,128)S(1)}, u32[]{:S(2)}) copy-start(f32[1,192]{1,0:T(1,128)S(1)} %get-tuple-element.66) | copy-start | bytes 2308
  20.7 207.0 %copy-start.51 = (f32[1,192]{1,0:T(1,128)}, f32[1,192]{1,0:T(1,128)S(1)}, u32[]{:S(2)}) copy-start(f32[1,192]{1,0:T(1,128)S(1)} %get-tuple-element.67) | copy-start | bytes 2308
  20.7 207.0 %copy-start.53 = (f32[1,192]{1,0:T(1,128)}, f32[1,192]{1,0:T(1,128)S(1)}, u32[]{:S(2)}) copy-start(f32[1,192]{1,0:T(1,128)S(1)} %get-tuple-element.68) | copy-start | bytes 2308
  20.7 207.0 %copy-start.55 = (f32[1,192]{1,0:T(1,128)}, f32[1,192]{1,0:T(1,128)S(1)}, u32[]{:S(2)}) copy-start(f32[1,192]{1,0:T(1,128)S(1)} %get-tuple-element.69) | copy-start | bytes 2308
  20.7 207.0 %copy-start.57 = (f32[1,192]{1,0:T(1,128)}, f32[1,192]{1,0:T(1,128)S(1)}, u32[]{:S(2)}) copy-start(f32[1,192]{1,0:T(1,128)S(1)} %get-tuple-element.70) | copy-start | bytes 2308
  20.7 207.0 %copy-start.59 = (f32[1,192]{1,0:T(1,128)}, f32[1,192]{1,0:T(1,128)S(1)}, u32[]{:S(2)}) copy-start(f32[1,192]{1,0:T(1,128)S(1)} %get-tuple-element.71) | copy-start | bytes 2308
  20.7 207.0 %copy-start.61 = (f32[1,192]{1,0:T(1,128)}, f32[1,192]{1,0:T(1,128)S(1)}, u32[]{:S(2)}) copy-start(f32[1,192]{1,0:T(1,128)S(1)} %get-tuple-element.72) | copy-start | bytes 2308
  20.7 207.0 %copy-start.63 = (f32[1,192]{1,0:T(1,128)}, f32[1,192]{1,0:T(1,128)S(1)}, u32[]{:S(2)}) copy-start(f32[1,192]{1,0:T(1,128)S(1)} %get-tuple-element.73) | copy-start | bytes 2308
  20.8 207.0 %copy-start.65 = (f32[1,192]{1,0:T(1,128)}, f32[1,192]{1,0:T(1,128)S(1)}, u32[]{:S(2)}) copy-start(f32[1,192]{1,0:T(1,128)S(1)} %get-tuple-element.74) | copy-start | bytes 2308
  20.8 207.0 %copy-start.67 = (f32[1,192]{1,0:T(1,128)}, f32[1,192]{1,0:T(1,128)S(1)}, u32[]{:S(2)}) copy-start(f32[1,192]{1,0:T(1,128)S(1)} %get-tuple-element.75) | copy-start | bytes 2308
  20.8 207.0 %copy-start.69 = (f32[1,192]{1,0:T(1,128)}, f32[1,192]{1,0:T(1,128)S(1)}, u32[]{:S(2)}) copy-start(f32[1,192]{1,0:T(1,128)S(1)} %get-tuple-element.76) | copy-start | bytes 2308
  20.8 207.0 %copy-start.71 = (f32[1,192]{1,0:T(1,128)}, f32[1,192]{1,0:T(1,128)S(1)}, u32[]{:S(2)}) copy-start(f32[1,192]{1,0:T(1,128)S(1)} %get-tuple-element.77) | copy-start | bytes 2308
  20.8 207.0 %copy-start.73 = (f32[1,192]{1,0:T(1,128)}, f32[1,192]{1,0:T(1,128)S(1)}, u32[]{:S(2)}) copy-start(f32[1,192]{1,0:T(1,128)S(1)} %get-tuple-element.78) | copy-start | bytes 2308
  20.8 207.0 %copy-start.75 = (f32[1,192]{1,0:T(1,128)}, f32[1,192]{1,0:T(1,128)S(1)}, u32[]{:S(2)}) copy-start(f32[1,192]{1,0:T(1,128)S(1)} %get-tuple-element.79) | copy-start | bytes 2308
  20.8 207.0 %copy-start.77 = (f32[1,192]{1,0:T(1,128)}, f32[1,192]{1,0:T(1,128)S(1)}, u32[]{:S(2)}) copy-start(f32[1,192]{1,0:T(1,128)S(1)} %get-tuple-element.80) | copy-start | bytes 2308
  20.8 207.0 %copy-start.78 = (f32[1,192]{1,0:T(1,128)}, f32[1,192]{1,0:T(1,128)S(1)}, u32[]{:S(2)}) copy-start(f32[1,192]{1,0:T(1,128)S(1)} %get-tuple-element.81) | copy-start | bytes 2308
  23.2 230.3 %copy-start.11 = (f32[192]{0:T(256)}, f32[192]{0:T(256)S(1)}, u32[]{:S(2)}) copy-start(f32[192]{0:T(256)S(1)} %convert_element_type.380) | copy-start | bytes 2308
  26.6 1.7 copy-start.8
  26.7 1.7 copy-start.79
  26.8 198.5 %copy-start.2 = (f32[64,64]{0,1:T(8,128)}, f32[64,64]{0,1:T(8,128)S(1)}, u32[]{:S(2)}) copy-start(f32[64,64]{0,1:T(8,128)S(1)} %add.564) | copy-start | bytes 49156
  27.1 198.9 %copy-start.4 = (f32[64,64]{0,1:T(8,128)}, f32[64,64]{0,1:T(8,128)S(1)}, u32[]{:S(2)}) copy-start(f32[64,64]{0,1:T(8,128)S(1)} %add.573) | copy-start | bytes 49156
  27.4 100.7 %copy-start.6 = (f32[64,64]{0,1:T(8,128)}, f32[64,64]{0,1:T(8,128)S(1)}, u32[]{:S(2)}) copy-start(f32[64,64]{0,1:T(8,128)S(1)} %add.581) | copy-start | bytes 49156
  27.9 100.4 %copy-start.80 = (bf16[6,384]{1,0:T(8,128)(2,1)S(1)}, bf16[6,384]{1,0:T(8,128)(2,1)}, u32[]{:S(2)}) copy-start(bf16[6,384]{1,0:T(8,128)(2,1)} %param.15) | copy-start | bytes 13828
  128.1 97.1 %copy-start.15 = (pred[3,8]{0,1:T(8,128)(4,1)}, pred[3,8]{0,1:T(8,128)(4,1)S(1)}, u32[]{:S(2)}) copy-start(pred[3,8]{0,1:T(8,128)(4,1)S(1)} %get-tuple-element.125) | copy-start | bytes 76
  128.1 97.6 %copy-start.13 = (pred[3,8]{0,1:T(8,128)(4,1)}, pred[3,8]{0,1:T(8,128)(4,1)S(1)}, u32[]{:S(2)}) copy-start(pred[3,8]{0,1:T(8,128)(4,1)S(1)} %get-tuple-element.126) | copy-start | bytes 76
  128.3 96.9 %copy-start.19 = (pred[3,8]{0,1:T(8,128)(4,1)}, pred[3,8]{0,1:T(8,128)(4,1)S(1)}, u32[]{:S(2)}) copy-start(pred[3,8]{0,1:T(8,128)(4,1)S(1)} %get-tuple-element.128) | copy-start | bytes 76
  128.3 98.0 %copy-start.17 = (pred[3,8]{0,1:T(8,128)(4,1)}, pred[3,8]{0,1:T(8,128)(4,1)S(1)}, u32[]{:S(2)}) copy-start(pred[3,8]{0,1:T(8,128)(4,1)S(1)} %get-tuple-element.127) | copy-start | bytes 76
  266.7 1.3 copy-start.81
  266.7 1.3 copy-start.10
  267.9 394.7 %all-reduce.14.cloned.1.call-start = ((), (), s32[]{:S(2)}) async-start(), calls=%async_computation.4 | async-start | bytes 4718592
  294.1 12.9 %copy-start.82 = (f32[512,384]{1,0:T(8,128)S(1)}, f32[512,384]{1,0:T(8,128)}, u32[]{:S(2)}) copy-start(f32[512,384]{1,0:T(8,128)} %get-tuple-element.130) | copy-start | bytes 2359300
  309.4 383.3 %reduce-scatter.9.cloned.1.call-start = ((), (), s32[]{:S(2)}) async-start(), calls=%async_computation.3 | async-start | bytes 983040
  310.2 1.2 copy-start.1
  311.4 382.3 %copy-start.12 = (f32[192]{0:T(256)S(1)}, f32[192]{0:T(256)}, u32[]{:S(2)}) copy-start(f32[192]{0:T(256)} %copy-done.11) | copy-start | bytes 2308
  700.7 0.7 copy-start.22
  700.7 0.7 copy-start.24
  700.9 0.7 copy-start.56
  716.4 0.7 copy-start.20
  717.0 0.8 copy-start.9
  717.0 1.1 copy-start.5
  717.0 1.1 copy-start.18
  717.0 1.6 copy-start.3
  717.0 1.6 copy-start.14
  717.1 11.0 %copy-start.7 = (f32[64,64]{0,1:T(8,128)S(1)}, f32[64,64]{0,1:T(8,128)}, u32[]{:S(2)}) copy-start(f32[64,64]{0,1:T(8,128)} %copy-done.6) | copy-start | bytes 49156
  717.3 12.9 %copy-start = (f32[192,512]{0,1:T(8,128)S(1)}, f32[192,512]{0,1:T(8,128)}, u32[]{:S(2)}) copy-start(f32[192,512]{0,1:T(8,128)} %copy.121) | copy-start | bytes 1179652
  719.2 9.6 %collective-permute-start.3 = (bf16[1,3,192,8,8]{2,1,3,4,0:T(4,128)(2,1)S(1)}, bf16[1,3,192,8,8]{2,1,3,4,0:T(4,128)(2,1)S(1)}, u32[]{:S(2)}, u32[]{:S(2)}) collective-permute-start(bf16[1,3,192,8,8]{2,1,3,4,0:T(4,128)(2,1)S(1)} %bitcast.353), channel_id=1, source_target_pairs={{4,0},{8,4},{12,8},{16,12},{20,16},{24,20},{28,24},{32,28},{36,32}... | collective-permute-start | bytes 221192 | tf_op jit(solution)/shard_map/ppermute | solution.py:20
  725.3 4.7 collective-permute-start.2
  (26 other events, 17.3 us)
Sparse Core Ops, SparseCore 0:
  268.1 24.0 reduce-scatter.6
  309.5 353.1 all-reduce.13
  665.5 27.0 reduce-scatter.8
where the time goes:
time: 740 us; the launch traced here: 738 us
  waiting for transfers between devices  401 us (54%)
  blocking collectives  233 us (31%)
  other arithmetic  38.2 us (5%)
  local copies, waits for them, and re-layouts  21.7 us (3%)
  starting transfers between devices  19.3 us (3%)
  between operations  16 us (2%)
  matrix products  8.83 us (1%)
    unnamed x5, waiting for transfers between devices  376 us
    all_gather x1, blocking collectives, per_device(): lax.all_gather(w_up, 'dp', axis=0, tiled=True)  99.4 us
    all_gather x1, blocking collectives, per_device(): lax.all_gather(w_down, 'dp', axis=0, tiled=True)  96.6 us
    reduce_scatter x1, waiting for transfers between devices, per_device(): lax.psum_scatter(partial_out.astype(jnp.bfloat16), 'fsdp', scatter_dimens...  24 us
    another operation x1, other arithmetic  16.6 us
  transfers between devices with their start and end apart: 7, of which 5 were waited for; matrix products, arithmetic and copies ran while one was open for 2% of the time, Pallas kernels for 0%

commit v1 on v0

--- a/solution.py
+++ b/solution.py
@@ -1,12 +1,331 @@
+import functools
 import math
 
 import jax
 import jax.numpy as jnp
 from jax import lax
+from jax.experimental import pallas as pl
+from jax.experimental.pallas import tpu as pltpu
 from jax.sharding import PartitionSpec as P
 
 root_half = 1.0 / math.sqrt(2.0)
 root_tau = 1.0 / math.sqrt(2.0 * math.pi)
+
+
+N_Z, N_Y, N_CORE = 16, 4, 2
+GROUP = N_Y * N_CORE
+MESH = pl.DeviceIdType.MESH
+RIGHT_STEPS = N_Z // 2
+LEFT_STEPS = N_Z - 1 - RIGHT_STEPS
+
+
+def dp_index(z, y, core):
+    return (z * N_Y + y) * N_CORE + core
+
+
+def own_place():
+    me = lax.axis_index("dp")
+    return me // GROUP, (me // N_CORE) % N_Y, me % N_CORE
+
+
+def remote(src, dst, send_sem, recv_sem, dp, fs):
+    return pltpu.make_async_remote_copy(
+        src_ref=src,
+        dst_ref=dst,
+        send_sem=send_sem,
+        recv_sem=recv_sem,
+        device_id=(dp, fs),
+        device_id_type=MESH,
+    )
+
+
+def weights_kernel(
+    rows, shard_ref, up_ref, down_ref, units, full,
+    unit_send, unit_recv, right_send, right_recv, left_send, left_recv, sib_send, sib_recv,
+):
+    z, y, core = own_place()
+    fs = lax.axis_index("fsdp")
+    group = y * N_CORE + core
+    right = dp_index((z + 1) % N_Z, y, core)
+    left = dp_index((z + N_Z - 1) % N_Z, y, core)
+    sibling = dp_index(z, y, 1 - core)
+
+    def mate(k):
+        other = (group + k) % GROUP
+        return dp_index(z, other // N_CORE, other % N_CORE)
+
+    barrier = pltpu.get_barrier_semaphore()
+    for k in range(1, GROUP):
+        pl.semaphore_signal(barrier, inc=1, device_id=(mate(k), fs), device_id_type=MESH)
+    for other in (right, left):
+        pl.semaphore_signal(barrier, inc=1, device_id=(other, fs), device_id_type=MESH)
+    pl.semaphore_wait(barrier, GROUP + 1)
+
+    def unit_copy(k):
+        return remote(
+            shard_ref, units.at[group], unit_send.at[k - 1], unit_recv.at[k - 1], mate(k), fs
+        )
+
+    for k in range(1, GROUP):
+        unit_copy(k).start()
+    units[group] = shard_ref[...]
+    for k in range(1, GROUP):
+        unit_copy(k).wait_recv()
+    flat = units[...].reshape(GROUP * 16, units.shape[2])
+    dense = GROUP * rows
+    row = lax.broadcasted_iota(jnp.int32, (dense, GROUP * 16), 0)
+    column = lax.broadcasted_iota(jnp.int32, (dense, GROUP * 16), 1)
+    for m in range(2):
+        pick = jnp.zeros((dense, GROUP * 16), jnp.float32)
+        for q in range(GROUP):
+            hit = (row >= q * rows) & (row < (q + 1) * rows) & (column - q * 16 - 8 * m == row - q * rows)
+            pick = jnp.where(hit, 1.0, pick)
+        full[m, z] = jnp.dot(
+            pick.astype(jnp.bfloat16), flat, preferred_element_type=jnp.float32
+        ).astype(jnp.bfloat16)
+
+    def right_copy(s):
+        block = full.at[core, (z - s + N_Z) % N_Z]
+        return remote(block, block, right_send.at[s], right_recv.at[s], right, fs)
+
+    def left_copy(s):
+        block = full.at[core, (z + s) % N_Z]
+        return remote(block, block, left_send.at[s], left_recv.at[s], left, fs)
+
+    def share(k, offset):
+        block = full.at[core, (z + offset + N_Z) % N_Z]
+        return remote(block, block, sib_send.at[k], sib_recv.at[k], sibling, fs)
+
+    def step(s, carry):
+        right_copy(s).start()
+        left_copy(s).start()
+        right_copy(s).wait_recv()
+        share(2 * s, -1 - s).start()
+        left_copy(s).wait_recv()
+        share(2 * s + 1, 1 + s).start()
+        return carry
+
+    lax.fori_loop(0, LEFT_STEPS, step, 0)
+    right_copy(LEFT_STEPS).start()
+    right_copy(LEFT_STEPS).wait_recv()
+    share(N_Z - 2, -RIGHT_STEPS).start()
+
+    for k in range(1, GROUP):
+        unit_copy(k).wait_send()
+
+    def drain(s, carry):
+        right_copy(s).wait_send()
+        left_copy(s).wait_send()
+        share(2 * s, -1 - s).wait()
+        share(2 * s + 1, 1 + s).wait()
+        return carry
+
+    lax.fori_loop(0, LEFT_STEPS, drain, 0)
+    right_copy(LEFT_STEPS).wait_send()
+    share(N_Z - 2, -RIGHT_STEPS).wait()
+
+    def emit(b, carry):
+        span = pl.ds(pl.multiple_of(b * dense, 16), dense)
+        up_ref[span, :] = full[0, b]
+        down_ref[span, :] = full[1, b]
+        return carry
+
+    lax.fori_loop(0, N_Z, emit, 0)
+
+
+def gather_weights(w_up, w_down):
+    rows, hidden = w_up.shape
+    gap = jnp.zeros((8 - rows, hidden), w_up.dtype)
+    shard = jnp.concatenate([w_up, gap, w_down, gap], axis=0)
+    total = rows * N_Z * GROUP
+    vmem = pl.BlockSpec(memory_space=pltpu.VMEM)
+    dma = pltpu.SemaphoreType.DMA
+    return pl.pallas_call(
+        functools.partial(weights_kernel, rows),
+        out_shape=[jax.ShapeDtypeStruct((total, hidden), w_up.dtype)] * 2,
+        in_specs=[vmem],
+        out_specs=[vmem, vmem],
+        scratch_shapes=[
+            pltpu.VMEM((GROUP, 16, hidden), w_up.dtype),
+            pltpu.VMEM((2, N_Z, GROUP * rows, hidden), w_up.dtype),
+            dma((GROUP - 1,)), dma((GROUP - 1,)),
+            dma((RIGHT_STEPS,)), dma((RIGHT_STEPS,)),
+            dma((LEFT_STEPS,)), dma((LEFT_STEPS,)),
+            dma((N_Z - 1,)), dma((N_Z - 1,)),
+        ],
+        compiler_params=pltpu.CompilerParams(
+            collective_id=0, has_side_effects=True, vmem_limit_bytes=48 * 1024 * 1024
+        ),
+    )(shard)
+
+
+def sums_kernel(
+    rows, up_ref, down_ref, out_ref, mats, mine, theirs, right_out, right_in, left_out, left_in,
+    block_sum, strips, strips_in, last, last_in,
+    sib_send, sib_recv, right_send, right_recv, left_send, left_recv, y_send, y_recv, end_send, end_recv,
+):
+    z, y, core = own_place()
+    fs = lax.axis_index("fsdp")
+    right = dp_index((z + 1) % N_Z, y, core)
+    left = dp_index((z + N_Z - 1) % N_Z, y, core)
+    sibling = dp_index(z, y, 1 - core)
+    dense = GROUP * rows
+
+    def column_mate(k):
+        return dp_index(z, (y + k) % N_Y, core)
+
+    barrier = pltpu.get_barrier_semaphore()
+    for other in [sibling, right, left] + [column_mate(k) for k in range(1, N_Y)]:
+        pl.semaphore_signal(barrier, inc=1, device_id=(other, fs), device_id_type=MESH)
+    pl.semaphore_wait(barrier, 2 + N_Y)
+
+    def sib_copy(k, block):
+        return remote(
+            mine.at[block], theirs.at[block], sib_send.at[k], sib_recv.at[k], sibling, fs
+        )
+
+    def span(block):
+        return pl.ds(pl.multiple_of(block * dense, 16), dense)
+
+    def pack(k, block):
+        mats[0, block] = up_ref[span(block), :]
+        mats[1, block] = down_ref[span(block), :]
+        mine[block] = mats[1 - core, block].astype(jnp.bfloat16)
+        sib_copy(k, block).start()
+
+    def right_dest(s):
+        return (z + RIGHT_STEPS - s) % N_Z
+
+    def left_dest(s):
+        return (z - LEFT_STEPS + s + N_Z) % N_Z
+
+    def pack_step(s, carry):
+        pack(2 * s, right_dest(s))
+        pack(2 * s + 1, left_dest(s))
+        return carry
+
+    lax.fori_loop(0, LEFT_STEPS, pack_step, 0)
+    pack(N_Z - 2, right_dest(LEFT_STEPS))
+    pack(N_Z - 1, z)
+
+    def own(k, block):
+        sib_copy(k, block).wait_recv()
+        return mats[core, block] + theirs[block].astype(jnp.float32)
+
+    def right_copy(s):
+        return remote(
+            right_out.at[s], right_in.at[s], right_send.at[s], right_recv.at[s], right, fs
+        )
+
+    def left_copy(s):
+        return remote(left_out.at[s], left_in.at[s], left_send.at[s], left_recv.at[s], left, fs)
+
+    right_out[0] = own(0, right_dest(0)).astype(jnp.bfloat16)
+    right_copy(0).start()
+    left_out[0] = own(1, left_dest(0)).astype(jnp.bfloat16)
+    left_copy(0).start()
+
+    def step(s, carry):
+        mixed = own(2 * s, right_dest(s))
+        right_copy(s - 1).wait_recv()
+        right_out[s] = (mixed + right_in[s - 1].astype(jnp.float32)).astype(jnp.bfloat16)
+        right_copy(s).start()
+        mixed = own(2 * s + 1, left_dest(s))
+        left_copy(s - 1).wait_recv()
+        left_out[s] = (mixed + left_in[s - 1].astype(jnp.float32)).astype(jnp.bfloat16)
+        left_copy(s).start()
+        return carry
+
+    lax.fori_loop(1, LEFT_STEPS, step, 0)
+    s = LEFT_STEPS
+    mixed = own(2 * s, right_dest(s))
+    right_copy(s - 1).wait_recv()
+    right_out[s] = (mixed + right_in[s - 1].astype(jnp.float32)).astype(jnp.bfloat16)
+    right_copy(s).start()
+    mixed = own(N_Z - 1, z)
+    left_copy(s - 1).wait_recv()
+    mixed = mixed + left_in[s - 1].astype(jnp.float32)
+    right_copy(s).wait_recv()
+    block_sum[...] = mixed + right_in[s].astype(jnp.float32)
+
+    for k in range(N_Y):
+        strips[k, 0 : N_CORE * rows] = block_sum[k * N_CORE * rows : (k + 1) * N_CORE * rows]
+
+    def strip_copy(k):
+        return remote(
+            strips.at[(y + k) % N_Y], strips_in.at[k - 1], y_send.at[k - 1], y_recv.at[k - 1],
+            column_mate(k), fs,
+        )
+
+    for k in range(1, N_Y):
+        strip_copy(k).start()
+    for k in range(1, N_Y):
+        strip_copy(k).wait_recv()
+    total = strips[y, 0 : N_CORE * rows]
+    for k in range(1, N_Y):
+        total = total + strips_in[k - 1, 0 : N_CORE * rows]
+    block_sum[0 : N_CORE * rows] = total
+    for k in range(N_CORE):
+        last[k, 0:rows] = block_sum[k * rows : (k + 1) * rows]
+    end = remote(last.at[1 - core], last_in, end_send, end_recv, sibling, fs)
+    end.start()
+    out_ref[core, 0:rows] = last[core, 0:rows]
+    end.wait_recv()
+    out_ref[1 - core, 0:rows] = last_in[0:rows]
+
+    end.wait_send()
+    for k in range(1, N_Y):
+        strip_copy(k).wait_send()
+
+    def drain(s, carry):
+        right_copy(s).wait_send()
+        left_copy(s).wait_send()
+        sib_copy(2 * s, right_dest(s)).wait_send()
+        sib_copy(2 * s + 1, left_dest(s)).wait_send()
+        return carry
+
+    lax.fori_loop(0, LEFT_STEPS, drain, 0)
+    right_copy(LEFT_STEPS).wait_send()
+    sib_copy(N_Z - 2, right_dest(LEFT_STEPS)).wait_send()
+    sib_copy(N_Z - 1, z).wait_send()
+
+
+def sum_weights(up_local, down_local):
+    total, hidden = up_local.shape
+    dense = total // N_Z
+    rows = dense // GROUP
+    vmem = pl.BlockSpec(memory_space=pltpu.VMEM)
+    dma = pltpu.SemaphoreType.DMA
+    f32, b16 = jnp.float32, jnp.bfloat16
+    both = pl.pallas_call(
+        functools.partial(sums_kernel, rows),
+        out_shape=jax.ShapeDtypeStruct((2, 8, hidden), f32),
+        in_specs=[vmem, vmem],
+        out_specs=vmem,
+        scratch_shapes=[
+            pltpu.VMEM((2, N_Z, dense, hidden), f32),
+            pltpu.VMEM((N_Z, dense, hidden), b16),
+            pltpu.VMEM((N_Z, dense, hidden), b16),
+            pltpu.VMEM((RIGHT_STEPS, dense, hidden), b16),
+            pltpu.VMEM((RIGHT_STEPS, dense, hidden), b16),
+            pltpu.VMEM((LEFT_STEPS, dense, hidden), b16),
+            pltpu.VMEM((LEFT_STEPS, dense, hidden), b16),
+            pltpu.VMEM((dense, hidden), f32),
+            pltpu.VMEM((N_Y, 16, hidden), f32),
+            pltpu.VMEM((N_Y - 1, 16, hidden), f32),
+            pltpu.VMEM((N_CORE, 8, hidden), f32),
+            pltpu.VMEM((8, hidden), f32),
+            dma((N_Z,)), dma((N_Z,)),
+            dma((RIGHT_STEPS,)), dma((RIGHT_STEPS,)),
+            dma((LEFT_STEPS,)), dma((LEFT_STEPS,)),
+            dma((N_Y - 1,)), dma((N_Y - 1,)),
+            dma, dma,
+        ],
+        compiler_params=pltpu.CompilerParams(
+            collective_id=1, has_side_effects=True, vmem_limit_bytes=48 * 1024 * 1024
+        ),
+    )(up_local, down_local)
+    return both[0, :rows], both[1, :rows]
 
 
 def padded_2(block, sides, width):
@@ -140,10 +459,7 @@
         )
         selectors.append(selector)
         masks.append(keep_mask)
-    up_full, down_full = (
-        lax.all_gather(w_up, "dp", axis=0, tiled=True),
-        lax.all_gather(w_down, "dp", axis=0, tiled=True),
-    )
+    up_full, down_full = gather_weights(w_up, w_down)
     corner = jnp.zeros((channels, tile_count, 3, 3), jnp.bfloat16)
     upper = jnp.concatenate([corner, jnp.transpose(halos[0], (1, 2, 0, 3)), corner], axis=3)
     lower = jnp.concatenate([corner, jnp.transpose(halos[1], (1, 2, 0, 3)), corner], axis=3)
@@ -240,10 +556,7 @@
     tile_grad = tile_grad + jnp.pad(
         jnp.transpose(coming[3], (1, 2, 3, 0)), ((0, 0), (0, 0), (0, 0), (side_len - 3, 0))
     )
-    up_grad, down_grad = (
-        lax.psum_scatter(up_local, "dp", scatter_dimension=0, tiled=True),
-        lax.psum_scatter(down_local, "dp", scatter_dimension=0, tiled=True),
-    )
+    up_grad, down_grad = sum_weights(up_local, down_local)
     return (
         block_out,
         tile_grad.reshape(channels, row_count).astype(jnp.bfloat16),

time: 740 us -> 252 us (0.34)
  waiting for transfers between devices: 401 us -> 31.4 us
  blocking collectives: 233 us -> 36.6 us
  Pallas kernels: 0 us -> 87.5 us
    unnamed x5 -> x2, waiting for transfers between devices: 376 us -> 0.03 us
    all_gather x2 -> x0, blocking collectives: 196 us -> none  [the longest x1 99.4 us: per_device(): lax.all_gather(w_up, 'dp', axis=0, tiled=True)]
    pallas_call x0 -> x2, Pallas kernels: none -> 87.5 us  [the longest x1 44.2 us: sum_weights(): pl.pallas_call(functools.partial(sums_kernel, rows), out_shape=jax.ShapeD...]
  transfers between devices with their start and end apart: 7 -> 6, of which waited for: 5 -> 2; matrix products, arithmetic and copies ran while one was open for 2% -> 5% of each run, Pallas kernels for 0% -> 35%
where the time goes in v1:
time: 252 us; the launch traced here: 250 us
  Pallas kernels  87.5 us (35%)
  other arithmetic  38.4 us (15%)
  blocking collectives  36.6 us (15%)
  waiting for transfers between devices  31.4 us (12%)
  starting transfers between devices  16.6 us (7%)
  between operations  15.7 us (6%)
  local copies, waits for them, and re-layouts  15.1 us (6%)
  matrix products  8.6 us (3%)
    pallas_call x1, Pallas kernels, sum_weights(): pl.pallas_call(functools.partial(sums_kernel, rows), out_shape=jax.ShapeD...  44.2 us
    pallas_call x1, Pallas kernels, gather_weights(): pl.pallas_call(functools.partial(weights_kernel, rows), out_shape=[jax.Sh...  43.2 us
    reduce_scatter x1, waiting for transfers between devices, per_device(): lax.psum_scatter(partial_out.astype(jnp.bfloat16), 'fsdp', scatter_dimens...  27.7 us
    another operation x1, other arithmetic  16.7 us
    add x1, other arithmetic, depthwise_back_flat(): summed + placed[:, lead - offset:lead - offset + total] * taps[row_tap *...  14.4 us
    all_gather x1, blocking collectives, per_device(): grad_mixed_all = lax.all_gather(grad_mixed, 'fsdp', axis=0, tiled=True)  11.3 us
    all_gather x1, blocking collectives, per_device(): lax.all_gather((centered * gain_f).astype(jnp.bfloat16), 'fsdp', axis=0,...  10.8 us
    ppermute x2, starting transfers between devices, padded_2(): lax.ppermute(lax.slice_in_dim(block, block.shape[dim] - width, None, axis...  9.15 us
  transfers between devices with their start and end apart: 6, of which 2 were waited for; matrix products, arithmetic and copies ran while one was open for 5% of the time, Pallas kernels for 35%

profile of v1, /device:TPU:1, one launch (start us, length us, event | category | flops | bytes accessed | tf_op | source)
XLA Modules:
  0.0 249.9 jit_solution(15511061884831866745)
XLA Ops:
  7.2 1.1 copy.28
  8.4 4.6 %collective-permute-start = (bf16[1,3,192,8,8]{2,1,4,3,0:T(4,128)(2,1)S(1)}, bf16[1,3,192,8,8]{2,1,4,3,0:T(4,128)(2,1)S(1)}, u32[]{:S(2)}, u32[]{:S(2)}) collective-permute-start(bf16[1,3,192,8,8]{2,1,4,3,0:T(4,128)(2,1)S(1)} %get-tuple-element.28), channel_id=1, source_target_pairs={{0,4},{4,8},{8,12},{12,16},{16,20},{20,24},{24,28},{28,32},{32,36}... | collective-permute-start | bytes 221192 | tf_op jit(solution)/shard_map/ppermute | solution.py:336
  13.0 5.5 %collective-permute-start.1 = (bf16[1,3,192,8,8]{2,1,4,3,0:T(4,128)(2,1)S(1)}, bf16[1,3,192,8,8]{2,1,4,3,0:T(4,128)(2,1)S(1)}, u32[]{:S(2)}, u32[]{:S(2)}) collective-permute-start(bf16[1,3,192,8,8]{2,1,4,3,0:T(4,128)(2,1)S(1)} %get-tuple-element.29), channel_id=1, source_target_pairs={{4,0},{8,4},{12,8},{16,12},{20,16},{24,20},{28,24},{32,28},{36,32}... | collective-permute-start | bytes 221192 | tf_op jit(solution)/shard_map/ppermute | solution.py:339
  18.6 1.0 fusion.68
  19.8 1.6 fusion.69
  21.5 1.6 fusion.70
  23.1 0.7 slice_bitcast_fusion.14
  24.0 0.7 slice_bitcast_fusion.15
  24.9 0.1 add.560
  25.5 0.1 add.569
  25.9 0.1 add.552
  26.1 0.1 reshape.679
  26.3 0.4 copy-done.9
  26.7 0.2 convolution_bitcast_fusion.5
  27.3 0.1 add.577
  27.5 0.1 reshape.683
  27.6 0.2 convolution_bitcast_fusion.2
  28.4 43.2 %shard_map.138 = (bf16[768,384]{1,0:T(8,128)(2,1)S(1)}, bf16[768,384]{1,0:T(8,128)(2,1)S(1)}) custom-call(bf16[16,384]{1,0:T(8,128)(2,1)S(1)} %pad_maximum_fusion.3.shard_ref), custom_call_target="tpu_custom_call" | custom-call | tf_op jit(solution)/shard_map/pallas_call | solution.py:143
  71.7 0.1 reshape_squeeze.6
  71.8 0.2 convolution_bitcast_fusion.4
  72.3 0.1 reshape_squeeze.7
  72.5 0.2 convolution_bitcast_fusion.3
  72.7 0.1 reshape.682
  73.0 0.6 maximum_maximum_fusion
  73.6 0.4 reshape.685
  74.3 16.7 %add_convert_fusion = bf16[192,1568]{0,1:T(8,128)(2,1)S(1)} fusion(bf16[192,1568]{0,1:T(8,128)(2,1)S(1)} %reshape.685, f32[192]{0:T(256)} %bitcast.95, f32[192]{0:T(256)} %bitcast.94, f32[192]{0:T(256)} %bitcast.93, f32[192]{0:T(256)} %bitcast.92, f32[192]{0:T(256)} %bitcast.91, f32[192]{0:T(256)} %bitcast.90, f32[192]{0:T(256)} %bitcast.89, f32[192]{0:T(256)} %bitcast.88, ...), kind=kLoop, calls=%fused_computation.4 | loop fusion | flops 44255232 | bytes 1241856 | tf_op jit(solution)/shard_map/convert.9
  91.0 0.3 reshape.686
  91.3 0.1 copy.37
  91.5 8.5 %all-reduce.8 = (f32[512]{0:T(512)S(1)}, f32[512]{0:T(512)S(1)}) all-reduce(f32[512]{0:T(512)S(1)} %get-tuple-element.15, f32[512]{0:T(512)S(1)} %get-tuple-element.14), channel_id=1, replica_groups=mesh['dp'=128,'fsdp'=4] {'fsdp'}, use_global_device_ids=true, to_apply=%region_3.4 | all-reduce | flops 1024 | bytes 8192 | tf_op jit(solution)/shard_map/psum | solution.py:475
  100.1 10.8 %all_gather.6 = bf16[768,512]{1,0:T(8,128)(2,1)S(1)} all-gather(bf16[192,512]{1,0:T(8,128)(2,1)S(1)} %fusion.16), channel_id=1, replica_groups=mesh['dp'=128,'fsdp'=4] {'fsdp'}, dimensions={0}, use_global_device_ids=true | all-gather | bytes 983040 | tf_op jit(solution)/shard_map/all_gather | solution.py:481
  111.0 1.5 multiply_convert_fusion
  112.5 1.5 convolution_convert_fusion.1
  114.2 27.7 %reduce-scatter.3.cloned.1.call-done = bf16[192,512]{1,0:T(8,128)(2,1)} async-done(((bf16[768,512]{1,0:T(8,128)(2,1)}), bf16[192,512]{1,0:T(8,128)(2,1)}) %reduce-scatter.3.cloned.1.call-update) | async-done | bytes 196624 | tf_op jit(solution)/shard_map/reduce_scatter | solution.py:489
  141.9 1.8 multiply_convert_fusion.1
  143.7 11.3 %all_gather.7 = bf16[768,512]{1,0:T(8,128)(2,1)S(1)} all-gather(bf16[192,512]{1,0:T(8,128)(2,1)S(1)} %get-tuple-element.95), channel_id=1, replica_groups=mesh['dp'=128,'fsdp'=4] {'fsdp'}, dimensions={0}, use_global_device_ids=true | all-gather | bytes 983040 | tf_op jit(solution)/shard_map/all_gather | solution.py:496
  155.0 0.7 fusion.2
  155.8 0.7 copy-done.1
  156.5 1.5 convolution_convert_fusion
  158.1 1.0 copy.38
  159.1 0.6 fusion.79.up_ref
  159.7 0.6 fusion.80.down_ref
  160.3 44.2 %shard_map.139 = f32[2,8,384]{2,1,0:T(8,128)S(1)} custom-call(f32[768,384]{1,0:T(8,128)S(1)} %fusion.79.up_ref, f32[768,384]{1,0:T(8,128)S(1)} %fusion.80.down_ref), custom_call_target="tpu_custom_call" | custom-call | tf_op jit(solution)/shard_map/pallas_call | solution.py:300
  204.5 0.6 slice_bitcast_fusion.6
  205.1 1.1 fusion.22
  206.2 6.0 %all-reduce.7 = (f32[512]{0:T(512)S(1)}, f32[512]{0:T(512)S(1)}) all-reduce(f32[512]{0:T(512)S(1)} %get-tuple-element.13, f32[512]{0:T(512)S(1)} %get-tuple-element.12), channel_id=1, replica_groups=mesh['dp'=128,'fsdp'=4] {'fsdp'}, use_global_device_ids=true, to_apply=%region_9.10 | all-reduce | flops 1024 | bytes 8192 | tf_op jit(solution)/shard_map/psum | solution.py:510
  212.2 1.1 fusion.20
  213.3 0.1 copy.39
  213.4 0.2 pad_convert_fusion
  213.9 0.2 reshape.694
  214.1 0.2 copy-done.21
  214.5 14.4 %multiply_add_fusion = f32[192,1568]{0,1:T(8,128)S(1)} fusion(f32[192,1568]{0,1:T(8,128)S(1)} %reshape.694, f32[192]{0:T(256)} %bitcast.95, f32[192]{0:T(256)} %bitcast.94, f32[192]{0:T(256)} %bitcast.93, f32[192]{0:T(256)} %bitcast.92, f32[192]{0:T(256)} %bitcast.91, f32[192]{0:T(256)} %bitcast.90, f32[192]{0:T(256)} %bitcast.89, f32[192]{0:T(256)} %bitcast.88, ...), kind=kLoop, calls=%fused_computation | loop fusion | flops 29202432 | bytes 2446080 | tf_op jit(solution)/shard_map/add | solution.py:397
  229.0 0.2 reshape.690
  229.3 0.2 copy-done.15
  229.7 0.2 copy-done.8
  229.9 0.4 convolution_convert_fusion.3
  230.4 4.6 %collective-permute-start.2 = (bf16[1,3,192,8,8]{2,1,3,4,0:T(4,128)(2,1)S(1)}, bf16[1,3,192,8,8]{2,1,3,4,0:T(4,128)(2,1)S(1)}, u32[]{:S(2)}, u32[]{:S(2)}) collective-permute-start(bf16[1,3,192,8,8]{2,1,3,4,0:T(4,128)(2,1)S(1)} %bitcast.343), channel_id=1, source_target_pairs={{0,4},{4,8},{8,12},{12,16},{16,20},{20,24},{24,28},{28,32},{32,36}... | collective-permute-start | bytes 221192 | tf_op jit(solution)/shard_map/ppermute | solution.py:336
  235.0 0.4 convolution_convert_fusion.2
  235.5 1.9 collective-permute-start.3
  237.5 0.3 convolution_bitcast_fusion
  237.8 0.3 convolution_bitcast_fusion.1
  238.1 3.7 %collective-permute-done.3 = bf16[1,3,192,8,8]{2,1,3,4,0:T(4,128)(2,1)S(1)} collective-permute-done((bf16[1,3,192,8,8]{2,1,3,4,0:T(4,128)(2,1)S(1)}, bf16[1,3,192,8,8]{2,1,3,4,0:T(4,128)(2,1)S(1)}, u32[]{:S(2)}, u32[]{:S(2)}) %collective-permute-start.3) | collective-permute-done | bytes 73760 | tf_op jit(solution)/shard_map/ppermute | solution.py:339
  241.8 0.2 convert_bitcast_fusion
  242.0 0.2 fusion.11
  242.3 0.8 copy.51
  (246 shorter events, 3.9 us)
Async XLA Ops:
  7.2 17.9 %copy-start.83 = (s32[8,4]{0,1:T(4,128)S(1)}, s32[8,4]{0,1:T(4,128)}, u32[]{:S(2)}) copy-start(s32[8,4]{0,1:T(4,128)} %param.19) | copy-start | bytes 388
  7.2 134.7 %reduce-scatter.3.cloned.1.call-start = ((), (), s32[]{:S(2)}) async-start(), calls=%async_computation.2 | async-start | bytes 983040 | tf_op jit(solution)/shard_map/reduce_scatter | solution.py:489
  8.4 63.3 %collective-permute-start = (bf16[1,3,192,8,8]{2,1,4,3,0:T(4,128)(2,1)S(1)}, bf16[1,3,192,8,8]{2,1,4,3,0:T(4,128)(2,1)S(1)}, u32[]{:S(2)}, u32[]{:S(2)}) collective-permute-start(bf16[1,3,192,8,8]{2,1,4,3,0:T(4,128)(2,1)S(1)} %get-tuple-element.28), channel_id=1, source_target_pairs={{0,4},{4,8},{8,12},{12,16},{16,20},{20,24},{24,28},{28,32},{32,36}... | collective-permute-start | bytes 221192 | tf_op jit(solution)/shard_map/ppermute | solution.py:336
  13.0 59.3 %collective-permute-start.1 = (bf16[1,3,192,8,8]{2,1,4,3,0:T(4,128)(2,1)S(1)}, bf16[1,3,192,8,8]{2,1,4,3,0:T(4,128)(2,1)S(1)}, u32[]{:S(2)}, u32[]{:S(2)}) collective-permute-start(bf16[1,3,192,8,8]{2,1,4,3,0:T(4,128)(2,1)S(1)} %get-tuple-element.29), channel_id=1, source_target_pairs={{4,0},{8,4},{12,8},{16,12},{20,16},{24,20},{28,24},{32,28},{36,32}... | collective-permute-start | bytes 221192 | tf_op jit(solution)/shard_map/ppermute | solution.py:339
  19.6 54.4 %copy-start.20 = (f32[1,192]{1,0:T(1,128)}, f32[1,192]{1,0:T(1,128)S(1)}, u32[]{:S(2)}) copy-start(f32[1,192]{1,0:T(1,128)S(1)} %get-tuple-element.30) | copy-start | bytes 2308
  19.6 54.4 %copy-start.22 = (f32[1,192]{1,0:T(1,128)}, f32[1,192]{1,0:T(1,128)S(1)}, u32[]{:S(2)}) copy-start(f32[1,192]{1,0:T(1,128)S(1)} %get-tuple-element.31) | copy-start | bytes 2308
  19.6 54.4 %copy-start.24 = (f32[1,192]{1,0:T(1,128)}, f32[1,192]{1,0:T(1,128)S(1)}, u32[]{:S(2)}) copy-start(f32[1,192]{1,0:T(1,128)S(1)} %get-tuple-element.32) | copy-start | bytes 2308
  19.6 54.4 %copy-start.26 = (f32[1,192]{1,0:T(1,128)}, f32[1,192]{1,0:T(1,128)S(1)}, u32[]{:S(2)}) copy-start(f32[1,192]{1,0:T(1,128)S(1)} %get-tuple-element.33) | copy-start | bytes 2308
  19.6 54.4 %copy-start.28 = (f32[1,192]{1,0:T(1,128)}, f32[1,192]{1,0:T(1,128)S(1)}, u32[]{:S(2)}) copy-start(f32[1,192]{1,0:T(1,128)S(1)} %get-tuple-element.34) | copy-start | bytes 2308
  19.6 54.4 %copy-start.30 = (f32[1,192]{1,0:T(1,128)}, f32[1,192]{1,0:T(1,128)S(1)}, u32[]{:S(2)}) copy-start(f32[1,192]{1,0:T(1,128)S(1)} %get-tuple-element.35) | copy-start | bytes 2308
  19.6 54.4 %copy-start.32 = (f32[1,192]{1,0:T(1,128)}, f32[1,192]{1,0:T(1,128)S(1)}, u32[]{:S(2)}) copy-start(f32[1,192]{1,0:T(1,128)S(1)} %get-tuple-element.36) | copy-start | bytes 2308
  19.6 54.4 %copy-start.34 = (f32[1,192]{1,0:T(1,128)}, f32[1,192]{1,0:T(1,128)S(1)}, u32[]{:S(2)}) copy-start(f32[1,192]{1,0:T(1,128)S(1)} %get-tuple-element.37) | copy-start | bytes 2308
  19.6 54.4 %copy-start.36 = (f32[1,192]{1,0:T(1,128)}, f32[1,192]{1,0:T(1,128)S(1)}, u32[]{:S(2)}) copy-start(f32[1,192]{1,0:T(1,128)S(1)} %get-tuple-element.38) | copy-start | bytes 2308
  19.7 54.4 %copy-start.38 = (f32[1,192]{1,0:T(1,128)}, f32[1,192]{1,0:T(1,128)S(1)}, u32[]{:S(2)}) copy-start(f32[1,192]{1,0:T(1,128)S(1)} %get-tuple-element.39) | copy-start | bytes 2308
  19.7 54.4 %copy-start.40 = (f32[1,192]{1,0:T(1,128)}, f32[1,192]{1,0:T(1,128)S(1)}, u32[]{:S(2)}) copy-start(f32[1,192]{1,0:T(1,128)S(1)} %get-tuple-element.40) | copy-start | bytes 2308
  19.7 54.4 %copy-start.42 = (f32[1,192]{1,0:T(1,128)}, f32[1,192]{1,0:T(1,128)S(1)}, u32[]{:S(2)}) copy-start(f32[1,192]{1,0:T(1,128)S(1)} %get-tuple-element.41) | copy-start | bytes 2308
  19.7 54.4 %copy-start.44 = (f32[1,192]{1,0:T(1,128)}, f32[1,192]{1,0:T(1,128)S(1)}, u32[]{:S(2)}) copy-start(f32[1,192]{1,0:T(1,128)S(1)} %get-tuple-element.42) | copy-start | bytes 2308
  19.7 54.4 %copy-start.46 = (f32[1,192]{1,0:T(1,128)}, f32[1,192]{1,0:T(1,128)S(1)}, u32[]{:S(2)}) copy-start(f32[1,192]{1,0:T(1,128)S(1)} %get-tuple-element.43) | copy-start | bytes 2308
  19.7 54.4 %copy-start.48 = (f32[1,192]{1,0:T(1,128)}, f32[1,192]{1,0:T(1,128)S(1)}, u32[]{:S(2)}) copy-start(f32[1,192]{1,0:T(1,128)S(1)} %get-tuple-element.44) | copy-start | bytes 2308
  19.7 54.4 %copy-start.50 = (f32[1,192]{1,0:T(1,128)}, f32[1,192]{1,0:T(1,128)S(1)}, u32[]{:S(2)}) copy-start(f32[1,192]{1,0:T(1,128)S(1)} %get-tuple-element.45) | copy-start | bytes 2308
  19.7 54.4 %copy-start.52 = (f32[1,192]{1,0:T(1,128)}, f32[1,192]{1,0:T(1,128)S(1)}, u32[]{:S(2)}) copy-start(f32[1,192]{1,0:T(1,128)S(1)} %get-tuple-element.46) | copy-start | bytes 2308
  19.7 54.4 %copy-start.54 = (f32[1,192]{1,0:T(1,128)}, f32[1,192]{1,0:T(1,128)S(1)}, u32[]{:S(2)}) copy-start(f32[1,192]{1,0:T(1,128)S(1)} %get-tuple-element.47) | copy-start | bytes 2308
  19.8 54.4 %copy-start.56 = (f32[1,192]{1,0:T(1,128)}, f32[1,192]{1,0:T(1,128)S(1)}, u32[]{:S(2)}) copy-start(f32[1,192]{1,0:T(1,128)S(1)} %get-tuple-element.48) | copy-start | bytes 2308
  21.4 52.8 %copy-start.58 = (f32[1,192]{1,0:T(1,128)}, f32[1,192]{1,0:T(1,128)S(1)}, u32[]{:S(2)}) copy-start(f32[1,192]{1,0:T(1,128)S(1)} %get-tuple-element.49) | copy-start | bytes 2308
  21.4 52.8 %copy-start.60 = (f32[1,192]{1,0:T(1,128)}, f32[1,192]{1,0:T(1,128)S(1)}, u32[]{:S(2)}) copy-start(f32[1,192]{1,0:T(1,128)S(1)} %get-tuple-element.50) | copy-start | bytes 2308
  21.4 52.8 %copy-start.62 = (f32[1,192]{1,0:T(1,128)}, f32[1,192]{1,0:T(1,128)S(1)}, u32[]{:S(2)}) copy-start(f32[1,192]{1,0:T(1,128)S(1)} %get-tuple-element.51) | copy-start | bytes 2308
  21.4 52.8 %copy-start.64 = (f32[1,192]{1,0:T(1,128)}, f32[1,192]{1,0:T(1,128)S(1)}, u32[]{:S(2)}) copy-start(f32[1,192]{1,0:T(1,128)S(1)} %get-tuple-element.52) | copy-start | bytes 2308
  21.4 52.8 %copy-start.66 = (f32[1,192]{1,0:T(1,128)}, f32[1,192]{1,0:T(1,128)S(1)}, u32[]{:S(2)}) copy-start(f32[1,192]{1,0:T(1,128)S(1)} %get-tuple-element.53) | copy-start | bytes 2308
  21.4 52.8 %copy-start.68 = (f32[1,192]{1,0:T(1,128)}, f32[1,192]{1,0:T(1,128)S(1)}, u32[]{:S(2)}) copy-start(f32[1,192]{1,0:T(1,128)S(1)} %get-tuple-element.54) | copy-start | bytes 2308
  21.4 52.8 %copy-start.70 = (f32[1,192]{1,0:T(1,128)}, f32[1,192]{1,0:T(1,128)S(1)}, u32[]{:S(2)}) copy-start(f32[1,192]{1,0:T(1,128)S(1)} %get-tuple-element.55) | copy-start | bytes 2308
  21.4 52.8 %copy-start.72 = (f32[1,192]{1,0:T(1,128)}, f32[1,192]{1,0:T(1,128)S(1)}, u32[]{:S(2)}) copy-start(f32[1,192]{1,0:T(1,128)S(1)} %get-tuple-element.56) | copy-start | bytes 2308
  21.5 52.8 %copy-start.74 = (f32[1,192]{1,0:T(1,128)}, f32[1,192]{1,0:T(1,128)S(1)}, u32[]{:S(2)}) copy-start(f32[1,192]{1,0:T(1,128)S(1)} %get-tuple-element.57) | copy-start | bytes 2308
  21.5 52.8 %copy-start.75 = (f32[1,192]{1,0:T(1,128)}, f32[1,192]{1,0:T(1,128)S(1)}, u32[]{:S(2)}) copy-start(f32[1,192]{1,0:T(1,128)S(1)} %get-tuple-element.58) | copy-start | bytes 2308
  21.5 52.8 %copy-start.76 = (f32[1,192]{1,0:T(1,128)}, f32[1,192]{1,0:T(1,128)S(1)}, u32[]{:S(2)}) copy-start(f32[1,192]{1,0:T(1,128)S(1)} %get-tuple-element.59) | copy-start | bytes 2308
  21.5 52.8 %copy-start.77 = (f32[1,192]{1,0:T(1,128)}, f32[1,192]{1,0:T(1,128)S(1)}, u32[]{:S(2)}) copy-start(f32[1,192]{1,0:T(1,128)S(1)} %get-tuple-element.60) | copy-start | bytes 2308
  21.5 52.8 %copy-start.78 = (f32[1,192]{1,0:T(1,128)}, f32[1,192]{1,0:T(1,128)S(1)}, u32[]{:S(2)}) copy-start(f32[1,192]{1,0:T(1,128)S(1)} %get-tuple-element.61) | copy-start | bytes 2308
  25.1 46.7 %copy-start.5 = (f32[64,64]{0,1:T(8,128)}, f32[64,64]{0,1:T(8,128)S(1)}, u32[]{:S(2)}) copy-start(f32[64,64]{0,1:T(8,128)S(1)} %add.560) | copy-start | bytes 49156
  25.4 2.5 %copy-start.84 = (bf16[192]{0:T(256)(128)(2,1)S(1)}, bf16[192]{0:T(256)(128)(2,1)}, u32[]{:S(2)}) copy-start(bf16[192]{0:T(256)(128)(2,1)} %param.13) | copy-start | bytes 1156
  25.6 46.9 %copy-start.7 = (f32[64,64]{0,1:T(8,128)}, f32[64,64]{0,1:T(8,128)S(1)}, u32[]{:S(2)}) copy-start(f32[64,64]{0,1:T(8,128)S(1)} %add.569) | copy-start | bytes 49156
  25.9 2.4 copy-start.81
  25.9 2.4 copy-start.82
  27.4 44.2 %copy-start.11 = (f32[64,64]{0,1:T(8,128)}, f32[64,64]{0,1:T(8,128)S(1)}, u32[]{:S(2)}) copy-start(f32[64,64]{0,1:T(8,128)S(1)} %add.577) | copy-start | bytes 49156
  28.1 43.6 %copy-start.14 = (pred[3,8]{0,1:T(8,128)(4,1)}, pred[3,8]{0,1:T(8,128)(4,1)S(1)}, u32[]{:S(2)}) copy-start(pred[3,8]{0,1:T(8,128)(4,1)S(1)} %get-tuple-element.113) | copy-start | bytes 76
  28.2 43.4 %copy-start.18 = (pred[3,8]{0,1:T(8,128)(4,1)}, pred[3,8]{0,1:T(8,128)(4,1)S(1)}, u32[]{:S(2)}) copy-start(pred[3,8]{0,1:T(8,128)(4,1)S(1)} %get-tuple-element.116) | copy-start | bytes 76
  28.2 44.7 %copy-start.16 = (pred[3,8]{0,1:T(8,128)(4,1)}, pred[3,8]{0,1:T(8,128)(4,1)S(1)}, u32[]{:S(2)}) copy-start(pred[3,8]{0,1:T(8,128)(4,1)S(1)} %get-tuple-element.115) | copy-start | bytes 76
  112.5 1.6 copy-start.13
  112.5 1.7 copy-start.85
  112.5 29.4 %copy-start.3 = (bf16[192,512]{1,0:T(8,128)(2,1)S(1)}, bf16[192,512]{1,0:T(8,128)(2,1)}, u32[]{:S(2)}) copy-start(bf16[192,512]{1,0:T(8,128)(2,1)} %param.11) | copy-start | bytes 589828
  112.5 29.4 %copy-start.4 = (bf16[192,512]{1,0:T(8,128)(2,1)S(1)}, bf16[192,512]{1,0:T(8,128)(2,1)}, u32[]{:S(2)}) copy-start(bf16[192,512]{1,0:T(8,128)(2,1)} %param.21) | copy-start | bytes 589828
  114.0 91.1 %reduce-scatter.5.cloned.1.call-start = ((), (), s32[]{:S(2)}) async-start(), calls=%async_computation.3 | async-start | bytes 983040 | tf_op jit(solution)/shard_map/reduce_scatter | solution.py:505
  114.2 29.5 %copy-start.79 = (bf16[512]{0:T(512)(128)(2,1)}, bf16[512]{0:T(512)(128)(2,1)S(1)}, u32[]{:S(2)}) copy-start(bf16[512]{0:T(512)(128)(2,1)S(1)} %convert_element_type.381) | copy-start | bytes 3076
  141.9 13.2 %copy-start.86 = (f32[512,384]{1,0:T(8,128)S(1)}, f32[512,384]{1,0:T(8,128)}, u32[]{:S(2)}) copy-start(f32[512,384]{1,0:T(8,128)} %get-tuple-element.118) | copy-start | bytes 2359300
  155.8 0.8 copy-start.1
  156.5 1.5 copy-start.80
  158.0 1.1 copy-start.2
  213.8 0.7 copy-start.55
  229.2 0.8 copy-start.8
  229.2 0.8 copy-start.17
  229.2 5.8 %copy-start.6 = (f32[64,64]{0,1:T(8,128)S(1)}, f32[64,64]{0,1:T(8,128)}, u32[]{:S(2)}) copy-start(f32[64,64]{0,1:T(8,128)} %copy-done.5) | copy-start | bytes 49156
  229.2 8.3 %copy-start.12 = (f32[64,64]{0,1:T(8,128)S(1)}, f32[64,64]{0,1:T(8,128)}, u32[]{:S(2)}) copy-start(f32[64,64]{0,1:T(8,128)} %copy-done.11) | copy-start | bytes 49156
  229.2 8.6 %copy-start.10 = (f32[64,64]{0,1:T(8,128)S(1)}, f32[64,64]{0,1:T(8,128)}, u32[]{:S(2)}) copy-start(f32[64,64]{0,1:T(8,128)} %copy-done.9) | copy-start | bytes 49156
  229.7 12.3 %copy-start = (f32[192,512]{0,1:T(8,128)S(1)}, f32[192,512]{0,1:T(8,128)}, u32[]{:S(2)}) copy-start(f32[192,512]{0,1:T(8,128)} %copy.38) | copy-start | bytes 1179652
  230.4 7.7 %collective-permute-start.2 = (bf16[1,3,192,8,8]{2,1,3,4,0:T(4,128)(2,1)S(1)}, bf16[1,3,192,8,8]{2,1,3,4,0:T(4,128)(2,1)S(1)}, u32[]{:S(2)}, u32[]{:S(2)}) collective-permute-start(bf16[1,3,192,8,8]{2,1,3,4,0:T(4,128)(2,1)S(1)} %bitcast.343), channel_id=1, source_target_pairs={{0,4},{4,8},{8,12},{12,16},{16,20},{20,24},{24,28},{28,32},{32,36}... | collective-permute-start | bytes 221192 | tf_op jit(solution)/shard_map/ppermute | solution.py:336
  235.5 6.3 %collective-permute-start.3 = (bf16[1,3,192,8,8]{2,1,3,4,0:T(4,128)(2,1)S(1)}, bf16[1,3,192,8,8]{2,1,3,4,0:T(4,128)(2,1)S(1)}, u32[]{:S(2)}, u32[]{:S(2)}) collective-permute-start(bf16[1,3,192,8,8]{2,1,3,4,0:T(4,128)(2,1)S(1)} %bitcast.345), channel_id=1, source_target_pairs={{4,0},{8,4},{12,8},{16,12},{20,16},{24,20},{28,24},{32,28},{36,32}... | collective-permute-start | bytes 221192 | tf_op jit(solution)/shard_map/ppermute | solution.py:339
  (29 other events, 19.3 us)
Sparse Core Ops, SparseCore 0:
  114.1 27.7 reduce-scatter.2
  158.2 32.7 reduce-scatter.4

commit v2 on v0

v2 whole, which is shorter than its diff:
```python
import functools
import math

import jax
import jax.numpy as jnp
from jax import lax
from jax.experimental import pallas as pl
from jax.experimental.pallas import tpu as pltpu
from jax.sharding import PartitionSpec as P

root_half = 1.0 / math.sqrt(2.0)
root_tau = 1.0 / math.sqrt(2.0 * math.pi)

N_Z, N_Y, N_CORE, N_X = 16, 4, 2, 4
N_FAR, N_NEAR = 4, 4
N_DP = N_Z * N_Y * N_CORE
MESH = pl.DeviceIdType.MESH
F32, B16 = jnp.float32, jnp.bfloat16
SIDE, TILE, TAPS = 8, 8, 7
HALF_ROWS = 256


def dp_index(z, y, core):
    return (z * N_Y + y) * N_CORE + core


def dot(a, b):
    return jnp.dot(a, b, preferred_element_type=F32)


def dot_nt(a, b):
    return lax.dot_general(a, b, (((1,), (1,)), ((), ())), preferred_element_type=F32)


def dot_tn(a, b):
    return lax.dot_general(a, b, (((0,), (0,)), ((), ())), preferred_element_type=F32)


def block_kernel(
    rows, width,
    x_ref, cot_ref, land_ref, taps_ref, gain_ref, scale_ref, links_ref, shard_ref,
    block_ref, grad_ref, wgrad_ref,
    perm, widen, picks, taps, xt, go, east_in, west_in, pad, gains,
    gma, gmb, cva, cvb, cen, inv, nrm, gmx, hid, gpre,
    pga, pgb, pgin_a, pgin_b, mxa, mxb, mxin_a, mxin_b, sums, sums_in, sum_cols,
    gcv, gpad, ret_w, ret_e, ret_w_in, ret_e_in, tg,
    unit, unit_in, full, dense,
    st, st_in, ysum, y_in, nsum, n_in, fsum, f_in, last, last_in,
    halo_s, halo_r, gain_s, gain_r, gm_s, gm_r, cv_s, cv_r, pg_s, pg_r, mx_s, mx_r, sum_s, sum_r,
    ret_s, ret_r, wsib_s, wsib_r, wfar_s, wfar_r, wnear_s, wnear_r, wy_s, wy_r, wsh_s, wsh_r,
    gsib_s, gsib_r, gy_s, gy_r, gnear_s, gnear_r, gfar_s, gfar_r, gend_s, gend_r,
):
    channels = x_ref.shape[0]
    low, high = 128, channels - 128
    cells = x_ref.shape[1]
    me = lax.axis_index("dp")
    x = lax.axis_index("fsdp")
    z, y, core = me // (N_Y * N_CORE), (me // N_CORE) % N_Y, me % N_CORE
    far, near = z // N_NEAR, z % N_NEAR
    east, west = (me + 1) % N_DP, (me + N_DP - 1) % N_DP
    sibling = dp_index(z, y, 1 - core)

    def at_z(step):
        return dp_index((z + step + N_Z) % N_Z, y, core)

    def at_y(k):
        return dp_index(z, (y + k) % N_Y, core)

    def copy(src, dst, send, recv, dp, fs=None):
        return pltpu.make_async_remote_copy(
            src_ref=src, dst_ref=dst, send_sem=send, recv_sem=recv,
            device_id=(dp, x if fs is None else fs), device_id_type=MESH,
        )

    barrier = pltpu.get_barrier_semaphore()
    greeted = [(east, x), (west, x), (sibling, x)]
    greeted += [(me, (x + k) % N_X) for k in range(1, N_X)]
    greeted += [(at_z(s), x) for s in (4, 8, 12, 1, -1, 2, -2)]
    greeted += [(at_y(k), x) for k in range(1, N_Y)]
    for other in greeted:
        pl.semaphore_signal(barrier, inc=1, device_id=other, device_id_type=MESH)

    out_cell = lax.broadcasted_iota(jnp.int32, (cells, cells), 0)
    in_cell = lax.broadcasted_iota(jnp.int32, (cells, cells), 1)
    wanted = (out_cell % 8) * 64 + ((out_cell // 8) % 8) * 8 + out_cell // 64
    perm[...] = jnp.where(in_cell == wanted, 1.0, 0.0).astype(B16)
    xt[...] = dot_nt(perm[...], x_ref[...]).astype(B16)
    go[...] = dot_nt(perm[...], cot_ref[...] * land_ref[...]).astype(B16)
    grad_mixed = (go[...].astype(F32) * scale_ref[...]).astype(B16)
    gma[x] = grad_mixed[:, :low]
    gmb[x] = jnp.concatenate([grad_mixed[:HALF_ROWS, low:], grad_mixed[HALF_ROWS:, low:]], axis=1)
    gains[x] = gain_ref[...]

    pl.semaphore_wait(barrier, len(greeted))

    halo_west = copy(xt.at[pl.ds(0, 192)], east_in, halo_s.at[0], halo_r.at[0], west)
    halo_east = copy(xt.at[pl.ds(cells - 192, 192)], west_in, halo_s.at[1], halo_r.at[1], east)
    halo_west.start()
    halo_east.start()
    unit_in[core] = shard_ref[...]
    wsib = copy(shard_ref, unit_in.at[core], wsib_s, wsib_r, sibling)
    wsib.start()

    def x_copies(src, dst, send, recv, scatter):
        made = []
        for k in range(1, N_X):
            other = (x + k) % N_X
            if scatter:
                pair = (src.at[other], dst.at[k - 1])
            else:
                pair = (src.at[x], dst.at[x])
            made.append(copy(*pair, send.at[k - 1], recv.at[k - 1], me, other))
        return made

    gain_copies = x_copies(gains, gains, gain_s, gain_r, False)
    gm_copies = x_copies(gma, gma, gm_s.at[0], gm_r.at[0], False)
    gm_copies += x_copies(gmb, gmb, gm_s.at[1], gm_r.at[1], False)
    for c in gain_copies + gm_copies:
        c.start()

    edge_row = lax.broadcasted_iota(jnp.int32, (64, 64), 0)
    edge_col = lax.broadcasted_iota(jnp.int32, (64, 64), 1)
    links = jnp.concatenate([links_ref[...]] * 8, axis=0)
    for face in range(4):
        chosen = jnp.zeros((64, 64), F32)
        for entry in range(2):
            c = face * 2 + entry
            owner = links[:, c : c + 1]
            shift = links[:, 8 + c : 9 + c]
            target = jnp.where(owner >= 0, owner % TILE + TILE * shift, -4096)
            target = target + (edge_row // 8) * 8
            chosen = chosen + jnp.where(target == edge_col, 1.0, 0.0)
        for layer in range(3):
            depth = 3 - layer if face in (0, 2) else layer + 1
            keep = links[:, 16 + face : 17 + face] >= depth
            picks[face * 3 + layer] = jnp.where(keep, chosen, 0.0).astype(B16)

    kernel_taps = taps_ref[...].astype(F32)
    for a in range(TAPS):
        for b in range(TAPS):
            k = a * TAPS + b
            taps[b, a] = jnp.broadcast_to(kernel_taps[k : k + 1], (8, channels))

    pad[...] = jnp.zeros_like(pad)
    cells_f = xt[...].astype(F32).reshape(SIDE, SIDE, TILE, channels)
    pad[3 : 3 + SIDE, 3 : 3 + SIDE] = cells_f
    for layer in range(3):
        north = cells_f[:, 5 + layer].reshape(64, channels).astype(B16)
        south = cells_f[:, layer].reshape(64, channels).astype(B16)
        pad[3 : 3 + SIDE, layer] = dot(picks[layer], north).astype(B16).astype(F32).reshape(SIDE, TILE, channels)
        pad[3 : 3 + SIDE, 11 + layer] = (
            dot(picks[3 + layer], south).astype(B16).astype(F32).reshape(SIDE, TILE, channels)
        )

    wsib.wait_recv()
    both = unit_in[...].reshape(N_CORE * 16, width)
    u_row = lax.broadcasted_iota(jnp.int32, (16, N_CORE * 16), 0)
    u_col = lax.broadcasted_iota(jnp.int32, (16, N_CORE * 16), 1)
    first = (u_row < rows) & (u_col == u_row + 8 * core)
    second = (u_row >= rows) & (u_row < 2 * rows) & (u_col == 16 + u_row - rows + 8 * core)
    joined = dot(jnp.where(first | second, 1.0, 0.0).astype(B16), both).astype(B16)
    full[core, y, near, far] = joined

    def far_copy(k):
        place = full.at[core, y, near, far]
        return copy(place, place, wfar_s.at[k - 1], wfar_r.at[k - 1], at_z(4 * k))

    for k in range(1, N_FAR):
        far_copy(k).start()

    halo_west.wait_recv()
    halo_east.wait_recv()
    for layer in range(3):
        part = pl.ds(layer * 64, 64)
        pad[layer, 3 : 3 + SIDE] = (
            dot(picks[6 + layer], west_in[part]).astype(B16).astype(F32).reshape(SIDE, TILE, channels)
        )
        pad[11 + layer, 3 : 3 + SIDE] = (
            dot(picks[9 + layer], east_in[part]).astype(B16).astype(F32).reshape(SIDE, TILE, channels)
        )

    def conv_column(j, start, size):
        total = jnp.zeros((SIDE, TILE, size), F32)
        for b in range(TAPS):
            source = pad[j + b, :, :, start : start + size]
            for a in range(TAPS):
                total = total + source[a : a + SIDE] * taps[b, a, :, start : start + size][None]
        return total.reshape(64, size).astype(B16)

    def conv_low(j, carry):
        cva[x, pl.ds(pl.multiple_of(j * 64, 64), 64)] = conv_column(j, 0, low)
        return carry

    def conv_high(j, carry):
        cvb[x, pl.ds(pl.multiple_of(j * 64, 64), 64)] = jnp.concatenate(
            [conv_column(j, low, high), conv_column(j + 4, low, high)], axis=1
        )
        return carry

    lax.fori_loop(0, SIDE, conv_low, 0)
    cv_copies = x_copies(cva, cva, cv_s.at[0], cv_r.at[0], False)
    for c in cv_copies:
        c.start()

    for k in range(1, N_FAR):
        far_copy(k).wait_recv()

    near_steps = (1, -1, -2)

    def near_copy(k):
        place = full.at[core, y, near]
        return copy(place, place, wnear_s.at[k], wnear_r.at[k], at_z(near_steps[k]))

    for k in range(3):
        near_copy(k).start()

    lax.fori_loop(0, 4, conv_high, 0)
    high_copies = x_copies(cvb, cvb, cv_s.at[1], cv_r.at[1], False)
    for c in high_copies:
        c.start()

    w_row = lax.broadcasted_iota(jnp.int32, (256, 256), 0)
    w_col = lax.broadcasted_iota(jnp.int32, (256, 256), 1)
    span = N_CORE * rows
    w_from = ((w_row // span) % N_Y) * 64 + (w_row // (span * N_Y)) * 16 + w_row % span
    widen[...] = jnp.where((w_col == w_from) & (w_row < channels), 1.0, 0.0).astype(B16)

    for k in range(3):
        near_copy(k).wait_recv()

    def y_copy(k):
        place = full.at[core, y]
        return copy(place, place, wy_s.at[k - 1], wy_r.at[k - 1], at_y(k))

    def share(k):
        place = full.at[core, (y + N_Y - k) % N_Y]
        return copy(place, place, wsh_s.at[k], wsh_r.at[k], sibling)

    for k in range(1, N_Y):
        y_copy(k).start()
    share(0).start()

    for c in gain_copies + gm_copies:
        c.wait_recv()
    nrm[...] = jnp.zeros_like(nrm)
    gmx[...] = jnp.zeros_like(gmx)
    for b in range(N_X):
        gmx[:, b * 256 : b * 256 + low] = gma[b]
        packed = gmb[b]
        gmx[:HALF_ROWS, b * 256 + low : b * 256 + channels] = packed[:, :high]
        gmx[HALF_ROWS:, b * 256 + low : b * 256 + channels] = packed[:, high:]

    for c in cv_copies + high_copies:
        c.wait_recv()

    wide = float(channels * N_X)
    for half in range(2):

        def norm_rows(i, carry, half=half):
            part = pl.ds(pl.multiple_of(i * 64, 64), 64)
            here = pl.ds(pl.multiple_of(half * HALF_ROWS + i * 64, 64), 64)
            lows = [cva[b, here].astype(F32) for b in range(N_X)]
            highs = [cvb[b, part, half * high : (half + 1) * high].astype(F32) for b in range(N_X)]
            total = jnp.sum(sum(lows), axis=1, keepdims=True) + jnp.sum(sum(highs), axis=1, keepdims=True)
            square = jnp.sum(sum(v * v for v in lows), axis=1, keepdims=True) + jnp.sum(
                sum(v * v for v in highs), axis=1, keepdims=True
            )
            mean = total / wide
            scale = lax.rsqrt(square / wide - mean * mean + 1e-06)
            inv[here] = jnp.broadcast_to(scale, (64, 128))
            for b in range(N_X):
                centered = (lows[b] - mean) * scale
                cen[b, here, 0:low] = centered
                nrm[here, b * 256 : b * 256 + low] = (centered * gains[b, 0:1, 0:low]).astype(B16)
                centered = (highs[b] - mean) * scale
                cen[b, here, low:channels] = centered
                nrm[here, b * 256 + low : b * 256 + channels] = (
                    centered * gains[b, 0:1, low:channels]
                ).astype(B16)
            return carry

        lax.fori_loop(0, 4, norm_rows, 0)

    for k in range(1, N_Y):
        y_copy(k).wait_recv()
        share(k).start()

    def unit_rows(m, b):
        return jnp.concatenate(
            [full[m, yy, nn, b] for yy in range(N_Y) for nn in range(N_NEAR)], axis=0
        )

    for k in range(N_Y):
        share(k).wait_recv()
    for m in range(2):
        for b in range(N_X):
            dense[m, b * 256 : (b + 1) * 256] = dot(widen[...], unit_rows(m, b)).astype(B16)

    for half in range(2):

        def mlp_rows(i, carry, half=half):
            part = pl.ds(pl.multiple_of(i * 128, 128), 128)
            here = pl.ds(pl.multiple_of(half * HALF_ROWS + i * 128, 128), 128)
            pre = dot(nrm[here], dense[0])
            edge = 0.5 * (1.0 + lax.erf(pre * root_half))
            hidden = (pre * edge).astype(B16)
            hid[here] = hidden
            slope = edge + pre * jnp.exp(-0.5 * pre * pre) * root_tau
            grad_pre = (dot_nt_rows(gmx[here], dense[1]) * slope).astype(B16)
            gpre[here] = grad_pre
            back = dot_nt(grad_pre, dense[0]).astype(B16)
            first_sum = jnp.zeros((128, 128), F32)
            second_sum = jnp.zeros((128, 128), F32)
            first_high = jnp.zeros((128, high), F32)
            second_high = jnp.zeros((128, high), F32)
            for b in range(N_X):
                low_part = back[:, b * 256 : b * 256 + low]
                high_part = back[:, b * 256 + low : b * 256 + channels]
                pga[b, here] = low_part
                pgb[b, part, half * high : (half + 1) * high] = high_part
                g = low_part.astype(F32) * gains[b, 0:1, 0:low]
                first_sum += g
                second_sum += g * cen[b, here, 0:low]
                g = high_part.astype(F32) * gains[b, 0:1, low:channels]
                first_high += g
                second_high += g * cen[b, here, low:channels]
            one = jnp.sum(first_sum, axis=1, keepdims=True) + jnp.sum(first_high, axis=1, keepdims=True)
            two = jnp.sum(second_sum, axis=1, keepdims=True) + jnp.sum(second_high, axis=1, keepdims=True)
            lane = lax.broadcasted_iota(jnp.int32, (128, 128), 1)
            columns = jnp.where(lane == 0, one, jnp.where(lane == 1, two, 0.0))
            sums[i + 2 * half] = jnp.transpose(columns)[0:8]
            return carry

        def dot_nt_rows(a, b):
            return dot(a, b)

        lax.fori_loop(0, 2, mlp_rows, 0)

    pg_copies = x_copies(pga, pgin_a, pg_s.at[0], pg_r.at[0], True)
    pg_copies += x_copies(pgb, pgin_b, pg_s.at[1], pg_r.at[1], True)
    sum_copies = []
    for k in range(1, N_X):
        sum_copies.append(
            copy(sums, sums_in.at[k - 1], sum_s.at[k - 1], sum_r.at[k - 1], me, (x + k) % N_X)
        )
    for c in sum_copies + pg_copies:
        c.start()

    for b in range(N_X):
        for m, left, right in ((0, nrm, gpre), (1, gmx, hid)):
            local = dot_tn(left[:, b * 256 : (b + 1) * 256], right[...]).astype(B16)
            units = dot_tn(widen[...], local).astype(B16)
            for yy in range(N_Y):
                for nn in range(N_NEAR):
                    r = (yy * N_NEAR + nn) * 16
                    st[m, yy, nn, b] = units[r : r + 16]

    def gsib_copy(k):
        yy = (y + k) % N_Y
        return copy(st.at[1 - core, yy], st_in.at[yy], gsib_s.at[k], gsib_r.at[k], sibling)

    for k in (1, 2, 3, 0):
        gsib_copy(k).start()

    for half in range(2):

        def out_rows(i, carry, half=half):
            part = pl.ds(pl.multiple_of(i * 128, 128), 128)
            here = pl.ds(pl.multiple_of(half * HALF_ROWS + i * 128, 128), 128)
            mixed = dot_nt(hid[here], dense[1]).astype(B16)
            for b in range(N_X):
                mxa[b, here] = mixed[:, b * 256 : b * 256 + low]
                mxb[b, part, half * high : (half + 1) * high] = mixed[:, b * 256 + low : b * 256 + channels]
            return carry

        lax.fori_loop(0, 2, out_rows, 0)

    mx_copies = x_copies(mxa, mxin_a, mx_s.at[0], mx_r.at[0], True)
    mx_copies += x_copies(mxb, mxin_b, mx_s.at[1], mx_r.at[1], True)
    for c in mx_copies:
        c.start()

    def gy_copy(k):
        return copy(ysum.at[k], y_in.at[k - 1], gy_s.at[k - 1], gy_r.at[k - 1], at_y(k))

    for k in (1, 2, 3, 0):
        gsib_copy(k).wait_recv()
        yy = (y + k) % N_Y
        ysum[k] = (st[core, yy].astype(F32) + st_in[yy].astype(F32)).astype(B16)
        if k > 0:
            gy_copy(k).start()

    for c in sum_copies + pg_copies:
        c.wait_recv()
    for q in range(4):
        total = sums[q]
        for k in range(1, N_X):
            total = total + sums_in[k - 1, q]
        spread = jnp.concatenate([total / wide, jnp.zeros((120, 128), F32)], axis=0)
        sum_cols[q * 128 : (q + 1) * 128] = jnp.transpose(spread)

    gcv[...] = jnp.zeros_like(gcv)
    for half in range(2):

        def back_rows(i, carry, half=half):
            part = pl.ds(pl.multiple_of(i * 64, 64), 64)
            here = pl.ds(pl.multiple_of(half * HALF_ROWS + i * 64, 64), 64)
            lanes = slice(half * high, (half + 1) * high)
            low_part = pga[x, here].astype(F32)
            high_part = pgb[x, part, lanes].astype(F32)
            for k in range(N_X - 1):
                low_part = low_part + pgin_a[k, here].astype(F32)
                high_part = high_part + pgin_b[k, part, lanes].astype(F32)
            e1 = sum_cols[here, 0:1]
            e2 = sum_cols[here, 1:2]
            scale = inv[here]
            g = low_part * gains[x, 0:1, 0:low]
            g = scale * (g - e1 - cen[x, here, 0:low] * e2)
            gcv[half * 4 + i, :, :, 0:low] = g.astype(B16).astype(F32).reshape(SIDE, TILE, low)
            g = high_part * gains[x, 0:1, low:channels]
            g = scale[:, :high] * (g - e1 - cen[x, here, low:channels] * e2)
            gcv[half * 4 + i, :, :, low:channels] = g.astype(B16).astype(F32).reshape(SIDE, TILE, high)
            return carry

        lax.fori_loop(0, 4, back_rows, 0)

    def spread_column(j, start, size):
        def add_tap(b, totals):
            totals = list(totals)
            source = gcv[j - b, :, :, start : start + size]
            for a in range(TAPS):
                tap = taps[b, a, :, start : start + size]
                for i in range(SIDE):
                    totals[i + a] = totals[i + a] + source[i] * tap
            return tuple(totals)

        empty = tuple(jnp.zeros((TILE, size), F32) for _ in range(SIDE + 6))
        first_tap = jnp.maximum(0, j - (SIDE - 1))
        end_tap = jnp.minimum(TAPS, j + 1)
        totals = lax.fori_loop(first_tap, end_tap, add_tap, empty)
        for i in range(SIDE + 6):
            gpad[j, i, :, start : start + size] = totals[i]

    def spread_edge(j, carry):
        for k in (j, j + 11):
            spread_column(k, 0, low)
            spread_column(k, low, high)
        return carry

    def spread_inner(j, carry):
        spread_column(j, 0, low)
        spread_column(j, low, high)
        return carry

    lax.fori_loop(0, 3, spread_edge, 0)
    for layer in range(3):
        part = pl.ds(layer * 64, 64)
        for face, column, held in ((2, layer, ret_w), (3, 11 + layer, ret_e)):
            edge = gpad[column, 3 : 3 + SIDE].reshape(64, channels).astype(B16)
            held[part] = dot_tn(picks[face * 3 + layer], edge).astype(B16)
    ret_west = copy(ret_w, ret_w_in, ret_s.at[0], ret_r.at[0], west)
    ret_east = copy(ret_e, ret_e_in, ret_s.at[1], ret_r.at[1], east)
    ret_west.start()
    ret_east.start()

    for k in range(1, N_Y):
        gy_copy(k).wait_recv()
    for nn in range(N_NEAR):
        total = ysum[0, nn].astype(F32)
        for k in range(1, N_Y):
            total = total + y_in[k - 1, nn].astype(F32)
        nsum[nn] = total.astype(B16)

    back_steps = (-1, 1, 2)

    def gnear_copy(k):
        target = (near + back_steps[k] + N_NEAR) % N_NEAR
        return copy(nsum.at[target], n_in.at[k], gnear_s.at[k], gnear_r.at[k], at_z(back_steps[k]))

    for k in range(3):
        gnear_copy(k).start()

    lax.fori_loop(3, 11, spread_inner, 0)

    for k in range(3):
        gnear_copy(k).wait_recv()
    total = nsum[near].astype(F32)
    for k in range(3):
        total = total + n_in[k].astype(F32)
    fsum[...] = total

    def gfar_copy(k):
        return copy(
            fsum.at[(far + k) % N_FAR], f_in.at[k - 1], gfar_s.at[k - 1], gfar_r.at[k - 1], at_z(4 * k)
        )

    for k in range(1, N_FAR):
        gfar_copy(k).start()

    tg[...] = go[...].astype(F32).reshape(SIDE, SIDE, TILE, channels) + gpad[3 : 3 + SIDE, 3 : 3 + SIDE]
    for layer in range(3):
        for face, row, target in ((0, layer, 5 + layer), (1, 11 + layer, layer)):
            edge = gpad[3 : 3 + SIDE, row].reshape(64, channels).astype(B16)
            back = dot_tn(picks[face * 3 + layer], edge)
            tg[:, target] = tg[:, target] + back.reshape(SIDE, TILE, channels)

    for c in mx_copies:
        c.wait_recv()
    low_part = mxa[x].astype(F32)
    packed = mxb[x].astype(F32)
    for k in range(N_X - 1):
        low_part = low_part + mxin_a[k].astype(F32)
        packed = packed + mxin_b[k].astype(F32)
    high_part = jnp.concatenate([packed[:, :high], packed[:, high:]], axis=0)
    mixed = jnp.concatenate([low_part, high_part], axis=1)
    out = (xt[...].astype(F32) + scale_ref[...] * mixed).astype(B16)
    block_ref[...] = dot_tn(out, perm[...]).astype(B16)

    for k in range(1, N_FAR):
        gfar_copy(k).wait_recv()
    total = fsum[far]
    for k in range(1, N_FAR):
        total = total + f_in[k - 1]
    last[0, 0:8] = total[0:8]
    last[1, 0:8] = total[rows : rows + 8]
    gend = copy(last.at[1 - core], last_in, gend_s, gend_r, sibling)
    gend.start()
    wgrad_ref[core] = last[core]

    ret_west.wait_recv()
    ret_east.wait_recv()
    for layer in range(3):
        part = pl.ds(layer * 64, 64)
        tg[5 + layer] = tg[5 + layer] + ret_w_in[part].astype(F32).reshape(SIDE, TILE, channels)
        tg[layer] = tg[layer] + ret_e_in[part].astype(F32).reshape(SIDE, TILE, channels)
    grad_ref[...] = dot_tn(tg[...].reshape(cells, channels).astype(B16), perm[...]).astype(B16)

    gend.wait_recv()
    wgrad_ref[1 - core] = last_in[...]

    sent = [halo_west, halo_east, wsib, ret_west, ret_east, gend]
    sent += gain_copies + gm_copies + cv_copies + high_copies + pg_copies + sum_copies + mx_copies
    sent += [far_copy(k) for k in range(1, N_FAR)] + [near_copy(k) for k in range(3)]
    sent += [y_copy(k) for k in range(1, N_Y)] + [share(k) for k in range(N_Y)]
    sent += [gsib_copy(k) for k in range(N_Y)] + [gy_copy(k) for k in range(1, N_Y)]
    sent += [gnear_copy(k) for k in range(3)] + [gfar_copy(k) for k in range(1, N_FAR)]
    for c in sent:
        c.wait_send()


def per_device(
    tiles, kernel, norm_gain, w_up, w_down, layer_scale, neighbors, shifts, halo_widths, land, cotangent
):
    channels, cells = tiles.shape
    rows, width = w_up.shape
    gap = jnp.zeros((8 - rows, width), w_up.dtype)
    shard = jnp.concatenate([w_up, gap, w_down, gap], axis=0)
    links = jnp.concatenate(
        [neighbors.reshape(TILE, 8), shifts.reshape(TILE, 8), halo_widths], axis=1
    )
    land_row = land.reshape(1, cells).astype(B16)
    gain = jnp.broadcast_to(norm_gain.astype(F32)[None], (8, channels))
    scale = layer_scale.astype(F32)[None]
    high = channels - 128
    vmem = pl.BlockSpec(memory_space=pltpu.VMEM)
    dma = pltpu.SemaphoreType.DMA

    def v(dtype, *shape):
        return pltpu.VMEM(shape, dtype)

    quarter = (N_NEAR, N_FAR, 16, width)
    scratch = [
        v(B16, cells, cells), v(B16, 256, 256), v(B16, 12, 64, 64), v(F32, TAPS, TAPS, 8, channels),
        v(B16, cells, channels), v(B16, cells, channels), v(B16, 192, channels), v(B16, 192, channels),
        v(F32, SIDE + 6, SIDE + 6, TILE, channels), v(F32, N_X, 8, channels),
        v(B16, N_X, cells, 128), v(B16, N_X, HALF_ROWS, 128), v(B16, N_X, cells, 128), v(B16, N_X, HALF_ROWS, 128),
        v(F32, N_X, cells, channels), v(F32, cells, 128), v(B16, cells, N_X * 256), v(B16, cells, N_X * 256),
        v(B16, cells, width), v(B16, cells, width),
        v(B16, N_X, cells, 128), v(B16, N_X, HALF_ROWS, 128), v(B16, 3, cells, 128), v(B16, 3, HALF_ROWS, 128),
        v(B16, N_X, cells, 128), v(B16, N_X, HALF_ROWS, 128), v(B16, 3, cells, 128), v(B16, 3, HALF_ROWS, 128),
        v(F32, 4, 8, 128), v(F32, 3, 4, 8, 128), v(F32, cells, 128),
        v(F32, SIDE, SIDE, TILE, channels), v(F32, SIDE + 6, SIDE + 6, TILE, channels),
        v(B16, 192, channels), v(B16, 192, channels), v(B16, 192, channels), v(B16, 192, channels),
        v(F32, SIDE, SIDE, TILE, channels),
        v(B16, 16, width), v(B16, 2, 16, width), v(B16, 2, N_Y, *quarter), v(B16, 2, N_X * 256, width),
        v(B16, 2, N_Y, *quarter), v(B16, N_Y, *quarter), v(B16, N_Y, *quarter), v(B16, 3, *quarter),
        v(B16, *quarter), v(B16, 3, N_FAR, 16, width), v(F32, N_FAR, 16, width), v(F32, 3, 16, width),
        v(F32, 2, 8, width), v(F32, 8, width),
    ]
    pairs = [(2,), (3,), (2, 3), (2, 3), (2, 3), (2, 3), (3,), (2,), None, (3,), (3,), (3,), (4,)]
    pairs += [(4,), (3,), (3,), (3,), None]
    for p in pairs:
        scratch += [dma if p is None else dma(p)] * 2
    block_out, tile_grad, both = pl.pallas_call(
        functools.partial(block_kernel, rows, width),
        out_shape=[
            jax.ShapeDtypeStruct((channels, cells), B16),
            jax.ShapeDtypeStruct((channels, cells), B16),
            jax.ShapeDtypeStruct((2, 8, width), F32),
        ],
        in_specs=[vmem] * 8,
        out_specs=[vmem] * 3,
        scratch_shapes=scratch,
        compiler_params=pltpu.CompilerParams(
            collective_id=0, has_side_effects=True, vmem_limit_bytes=56 * 1024 * 1024
        ),
    )(tiles, cotangent, land_row, kernel, gain, scale, links, shard)
    return block_out, tile_grad, both[0, :rows], both[1, :rows]


def solution(mesh):
    return jax.shard_map(
        per_device,
        mesh=mesh,
        in_specs=(
            P("fsdp", "dp"),
            P(None, "fsdp"),
            P("fsdp"),
            P("dp", "fsdp"),
            P("dp", "fsdp"),
            P("fsdp"),
            P("dp", None, None),
            P("dp", None, None),
            P("dp", None),
            P("dp", None, None),
            P("fsdp", "dp"),
        ),
        out_specs=(P("fsdp", "dp"), P("fsdp", "dp"), P("dp", "fsdp"), P("dp", "fsdp")),
        check_vma=False,
    )
```

time: 740 us -> 92.5 us (0.12)
  waiting for transfers between devices: 401 us -> 0 us
  blocking collectives: 233 us -> 0 us
  Pallas kernels: 0 us -> 82.7 us
  other arithmetic: 38.2 us -> 2.53 us
  starting transfers between devices: 19.3 us -> 0 us
  local copies, waits for them, and re-layouts: 21.7 us -> 5.88 us
  between operations: 16 us -> 0.67 us
  matrix products: 8.83 us -> 0 us
    unnamed x5 -> x0, waiting for transfers between devices: 376 us -> none
    all_gather x4 -> x0, blocking collectives: 218 us -> none  [the longest x1 99.4 us: per_device(): lax.all_gather(w_up, 'dp', axis=0, tiled=True)]
    pallas_call x0 -> x1, Pallas kernels: none -> 82.7 us  [per_device(): pl.pallas_call(functools.partial(block_kernel, rows, width), out_shape=[j...]
    reduce_scatter x1 -> x0, waiting for transfers between devices: 24 us -> none  [per_device(): lax.psum_scatter(partial_out.astype(jnp.bfloat16), 'fsdp', scatter_dimens...]
    ppermute x4 -> x0, starting transfers between devices: 19 us -> none  [the longest x2 11.6 us: padded_2(): lax.ppermute(lax.slice_in_dim(block, 0, width, axis=dim), axis, backward)]
    another operation x1 -> x0, other arithmetic: 16.6 us -> none
    add x14 -> x0, other arithmetic: 15.7 us -> none  [the longest x1 14.7 us: depthwise_back_flat(): summed + placed[:, lead - offset:lead - offset + total] * taps[row_tap *...]
    psum x2 -> x0, blocking collectives: 14.5 us -> none  [the longest x1 8.47 us: per_device(): lax.psum((jnp.sum(values, axis=0), jnp.sum(values * values, axis=0)), 'fs...]
  transfers between devices with their start and end apart: 7 -> 0, of which waited for: 5 -> 0; matrix products, arithmetic and copies ran while one was open for 2% -> 0% of each run, Pallas kernels for 0% -> 0%
where the time goes in v2:
time: 92.5 us; the launch traced here: 91.8 us
  Pallas kernels  82.7 us (89%)
  local copies, waits for them, and re-layouts  5.88 us (6%)
  other arithmetic  2.53 us (3%)
    pallas_call x1, Pallas kernels, per_device(): pl.pallas_call(functools.partial(block_kernel, rows, width), out_shape=[j...  82.7 us
    unnamed x19, local copies, waits for them, and re-layouts  3.13 us

profile of v2, /device:TPU:1, one launch (start us, length us, event | category | flops | bytes accessed | tf_op | source)
XLA Modules:
  0.0 91.8 jit_solution(6622852048519565531)
XLA Ops:
  0.6 0.0 copy-start.4
  0.6 0.0 copy-start.7
  0.7 1.2 %broadcast_in_dim.18 = f32[192]{0:T(256)} convert(bf16[192]{0:T(256)(128)(2,1)} %param.16) | non-fusion elementwise | flops 192 | bytes 1152 | tf_op jit(solution)/shard_map/broadcast_in_dim | solution.py:563
  1.9 0.0 copy-start.5
  1.9 0.0 copy-done.4
  1.9 0.0 copy-start.6
  1.9 0.0 copy-start.3
  1.9 0.1 copy.15
  2.0 0.6 copy-done.5
  2.6 0.0 copy-start.1
  2.6 0.1 copy.16
  2.7 0.0 copy-done.6
  2.7 0.1 copy.17
  2.7 0.7 pad_add_fusion.links_ref
  3.4 0.0 copy-done.7
  3.4 0.0 copy-start.2
  3.4 0.6 broadcast_in_dim.14.gain_ref
  4.0 0.0 copy-done.3
  4.0 0.1 copy-done.2
  4.1 0.6 pad_maximum_fusion.shard_ref
  4.7 0.0 copy-done.1
  4.7 0.7 convert_element_type.10.land_ref
  5.4 82.7 %shard_map.138 = (bf16[192,512]{1,0:T(8,128)(2,1)}, bf16[192,512]{1,0:T(8,128)(2,1)}, f32[2,8,384]{2,1,0:T(8,128)}) custom-call(bf16[192,512]{1,0:T(8,128)(2,1)} %x_ref.1, bf16[192,512]{1,0:T(8,128)(2,1)} %cot_ref.1, bf16[1,512]{1,0:T(2,128)(2,1)} %convert_element_type.10.land_ref, bf16[49,192]{1,0:T(8,128)(2,1)} %taps_ref.1, ...), custom_call_target="tpu_custom_call" | custom-call | tf_op jit(solution)/shard_map/pallas_call | solution.py:594
  88.1 1.3 %slice_bitcast_fusion = (f32[6,384]{1,0:T(8,128)}, f32[6,384]{1,0:T(8,128)}) fusion(f32[2,8,384]{2,1,0:T(8,128)} %get-tuple-element.9), kind=kLoop, calls=%fused_computation.1 | loop fusion | bytes 36864 | tf_op jit(solution)/shard_map/squeeze | solution.py:608
  89.4 0.0 copy-start
  89.5 1.7 %copy.20 = bf16[192,512]{1,0:T(8,128)(2,1)} copy(bf16[192,512]{1,0:T(8,128)(2,1)} %get-tuple-element.16) | data formatting | bytes 393216
  91.1 0.0 copy-done
  91.1 0.7 copy.21
  (2 shorter events, 0.0 us)
Async XLA Ops:
  0.6 1.3 %copy-start.4 = (s32[8,4,2]{0,2,1:T(2,128)S(1)}, s32[8,4,2]{0,2,1:T(2,128)}, u32[]{:S(2)}) copy-start(s32[8,4,2]{0,2,1:T(2,128)} %param.17) | copy-start | bytes 772
  0.6 2.8 %copy-start.7 = (bf16[192]{0:T(256)(128)(2,1)S(1)}, bf16[192]{0:T(256)(128)(2,1)}, u32[]{:S(2)}) copy-start(bf16[192]{0:T(256)(128)(2,1)} %param.13) | copy-start | bytes 1156
  1.9 0.7 copy-start.5
  1.9 0.8 copy-start.6
  1.9 2.1 %copy-start.3 = (bf16[6,384]{1,0:T(8,128)(2,1)S(1)}, bf16[6,384]{1,0:T(8,128)(2,1)}, u32[]{:S(2)}) copy-start(bf16[6,384]{1,0:T(8,128)(2,1)} %param.14) | copy-start | bytes 13828
  2.6 2.1 %copy-start.1 = (s32[8,8,8]{2,1,0:T(8,128)S(1)}, s32[8,8,8]{2,1,0:T(8,128)}, u32[]{:S(2)}) copy-start(s32[8,8,8]{2,1,0:T(8,128)} %param.20) | copy-start | bytes 6148
  3.4 0.7 copy-start.2
  89.4 1.7 %copy-start = (bf16[192,512]{1,0:T(8,128)(2,1)S(1)}, bf16[192,512]{1,0:T(8,128)(2,1)}, u32[]{:S(2)}) copy-start(bf16[192,512]{1,0:T(8,128)(2,1)} %get-tuple-element.17) | copy-start | bytes 589828

commit v3 on v2

--- a/solution.py
+++ b/solution.py
@@ -38,17 +38,18 @@
 
 def block_kernel(
     rows, width,
-    x_ref, cot_ref, land_ref, taps_ref, gain_ref, scale_ref, links_ref, shard_ref,
-    block_ref, grad_ref, wgrad_ref,
-    perm, widen, picks, taps, xt, go, east_in, west_in, pad, gains,
+    x_ref, cot_ref, land_ref, taps_ref, gain_ref, scale_ref, owner_ref, shift_ref, depth_ref, up_ref, down_ref,
+    block_ref, grad_ref, up_grad_ref, down_grad_ref,
+    perm, order, picks, taps, xt, go, east_in, west_in, pad, gains,
     gma, gmb, cva, cvb, cen, inv, nrm, gmx, hid, gpre,
     pga, pgb, pgin_a, pgin_b, mxa, mxb, mxin_a, mxin_b, sums, sums_in, sum_cols,
     gcv, gpad, ret_w, ret_e, ret_w_in, ret_e_in, tg,
-    unit, unit_in, full, dense,
-    st, st_in, ysum, y_in, nsum, n_in, fsum, f_in, last, last_in,
+    unit_in, wfar, wone_a, wone_b, wtwo_a, wtwo_b, dense,
+    st_a, st_b, st_in_a, st_in_b, one_a, one_b, one_in_a, one_in_b, two_a, two_b, two_in_a, two_in_b,
+    fsum, f_in, last, last_in,
     halo_s, halo_r, gain_s, gain_r, gm_s, gm_r, cv_s, cv_r, pg_s, pg_r, mx_s, mx_r, sum_s, sum_r,
-    ret_s, ret_r, wsib_s, wsib_r, wfar_s, wfar_r, wnear_s, wnear_r, wy_s, wy_r, wsh_s, wsh_r,
-    gsib_s, gsib_r, gy_s, gy_r, gnear_s, gnear_r, gfar_s, gfar_r, gend_s, gend_r,
+    ret_s, ret_r, wsib_s, wsib_r, wfar_s, wfar_r, wone_s, wone_r, wtwo_s, wtwo_r, wsh_s, wsh_r,
+    gsib_s, gsib_r, gone_s, gone_r, gtwo_s, gtwo_r, gfar_s, gfar_r, gend_s, gend_r,
 ):
     channels = x_ref.shape[0]
     low, high = 128, channels - 128
@@ -85,11 +86,27 @@
     wanted = (out_cell % 8) * 64 + ((out_cell // 8) % 8) * 8 + out_cell // 64
     perm[...] = jnp.where(in_cell == wanted, 1.0, 0.0).astype(B16)
     xt[...] = dot_nt(perm[...], x_ref[...]).astype(B16)
-    go[...] = dot_nt(perm[...], cot_ref[...] * land_ref[...]).astype(B16)
-    grad_mixed = (go[...].astype(F32) * scale_ref[...]).astype(B16)
+    j_row = lax.broadcasted_iota(jnp.int32, (SIDE, cells), 0)
+    j_col = lax.broadcasted_iota(jnp.int32, (SIDE, cells), 1)
+    spread_j = jnp.where(j_row == j_col % SIDE, 1.0, 0.0).astype(B16)
+    land = land_ref[...].astype(F32).reshape(TILE * SIDE, SIDE).astype(B16)
+    ti_row = lax.broadcasted_iota(jnp.int32, (TILE * SIDE, cells), 0)
+    ti_col = lax.broadcasted_iota(jnp.int32, (TILE * SIDE, cells), 1)
+    land_row = jnp.sum(
+        jnp.where(ti_row == ti_col // SIDE, dot(land, spread_j), 0.0), axis=0, keepdims=True
+    ).astype(B16)
+    go[...] = dot_nt(perm[...], cot_ref[...] * land_row).astype(B16)
+    scale_row = scale_ref[...].astype(F32)
+    grad_mixed = (go[...].astype(F32) * scale_row).astype(B16)
     gma[x] = grad_mixed[:, :low]
     gmb[x] = jnp.concatenate([grad_mixed[:HALF_ROWS, low:], grad_mixed[HALF_ROWS:, low:]], axis=1)
-    gains[x] = gain_ref[...]
+    gains[x] = jnp.broadcast_to(gain_ref[...].astype(F32), (8, channels))
+    s_row = lax.broadcasted_iota(jnp.int32, (16, rows), 0)
+    s_col = lax.broadcasted_iota(jnp.int32, (16, rows), 1)
+    unit_in[core] = (
+        dot(jnp.where(s_row == s_col, 1.0, 0.0).astype(B16), up_ref[...])
+        + dot(jnp.where(s_row == s_col + 8, 1.0, 0.0).astype(B16), down_ref[...])
+    ).astype(B16)
 
     pl.semaphore_wait(barrier, len(greeted))
 
@@ -97,8 +114,7 @@
     halo_east = copy(xt.at[pl.ds(cells - 192, 192)], west_in, halo_s.at[1], halo_r.at[1], east)
     halo_west.start()
     halo_east.start()
-    unit_in[core] = shard_ref[...]
-    wsib = copy(shard_ref, unit_in.at[core], wsib_s, wsib_r, sibling)
+    wsib = copy(unit_in.at[core], unit_in.at[core], wsib_s, wsib_r, sibling)
     wsib.start()
 
     def x_copies(src, dst, send, recv, scatter):
@@ -120,19 +136,21 @@
 
     edge_row = lax.broadcasted_iota(jnp.int32, (64, 64), 0)
     edge_col = lax.broadcasted_iota(jnp.int32, (64, 64), 1)
-    links = jnp.concatenate([links_ref[...]] * 8, axis=0)
+    owners = jnp.concatenate([owner_ref[...]] * 8, axis=0)
+    moves = jnp.concatenate([shift_ref[...]] * 8, axis=0)
+    depths = jnp.concatenate([depth_ref[...]] * 8, axis=0)
     for face in range(4):
         chosen = jnp.zeros((64, 64), F32)
         for entry in range(2):
             c = face * 2 + entry
-            owner = links[:, c : c + 1]
-            shift = links[:, 8 + c : 9 + c]
+            owner = owners[:, c : c + 1]
+            shift = moves[:, c : c + 1]
             target = jnp.where(owner >= 0, owner % TILE + TILE * shift, -4096)
             target = target + (edge_row // 8) * 8
             chosen = chosen + jnp.where(target == edge_col, 1.0, 0.0)
         for layer in range(3):
             depth = 3 - layer if face in (0, 2) else layer + 1
-            keep = links[:, 16 + face : 17 + face] >= depth
+            keep = depths[:, face : face + 1] >= depth
             picks[face * 3 + layer] = jnp.where(keep, chosen, 0.0).astype(B16)
 
     kernel_taps = taps_ref[...].astype(F32)
@@ -159,10 +177,10 @@
     first = (u_row < rows) & (u_col == u_row + 8 * core)
     second = (u_row >= rows) & (u_row < 2 * rows) & (u_col == 16 + u_row - rows + 8 * core)
     joined = dot(jnp.where(first | second, 1.0, 0.0).astype(B16), both).astype(B16)
-    full[core, y, near, far] = joined
+    wfar[far] = joined
 
     def far_copy(k):
-        place = full.at[core, y, near, far]
+        place = wfar.at[far]
         return copy(place, place, wfar_s.at[k - 1], wfar_r.at[k - 1], at_z(4 * k))
 
     for k in range(1, N_FAR):
@@ -207,48 +225,77 @@
 
     near_steps = (1, -1, -2)
 
-    def near_copy(k):
-        place = full.at[core, y, near]
-        return copy(place, place, wnear_s.at[k], wnear_r.at[k], at_z(near_steps[k]))
-
-    for k in range(3):
-        near_copy(k).start()
+    def one_copies():
+        made = []
+        for k in range(3):
+            made.append(
+                copy(wone_a.at[near], wone_a.at[near], wone_s.at[0, k], wone_r.at[0, k], at_z(near_steps[k]))
+            )
+            made.append(copy(wone_b.at[y], wone_b.at[y], wone_s.at[1, k], wone_r.at[1, k], at_y(k + 1)))
+        return made
+
+    wone_a[near] = wfar[0:2]
+    wone_b[y] = wfar[2:4]
+    for c in one_copies():
+        c.start()
 
     lax.fori_loop(0, 4, conv_high, 0)
     high_copies = x_copies(cvb, cvb, cv_s.at[1], cv_r.at[1], False)
     for c in high_copies:
         c.start()
 
-    w_row = lax.broadcasted_iota(jnp.int32, (256, 256), 0)
-    w_col = lax.broadcasted_iota(jnp.int32, (256, 256), 1)
     span = N_CORE * rows
-    w_from = ((w_row // span) % N_Y) * 64 + (w_row // (span * N_Y)) * 16 + w_row % span
-    widen[...] = jnp.where((w_col == w_from) & (w_row < channels), 1.0, 0.0).astype(B16)
-
-    for k in range(3):
-        near_copy(k).wait_recv()
-
-    def y_copy(k):
-        place = full.at[core, y]
-        return copy(place, place, wy_s.at[k - 1], wy_r.at[k - 1], at_y(k))
-
-    def share(k):
-        place = full.at[core, (y + N_Y - k) % N_Y]
-        return copy(place, place, wsh_s.at[k], wsh_r.at[k], sibling)
-
-    for k in range(1, N_Y):
-        y_copy(k).start()
-    share(0).start()
+    w_row = lax.broadcasted_iota(jnp.int32, (256, channels), 0)
+    w_col = lax.broadcasted_iota(jnp.int32, (256, channels), 1)
+    w_from = ((w_row // span) % N_Y) * (span * N_NEAR) + (w_row // (span * N_Y)) * span + w_row % span
+    order[...] = jnp.where((w_col == w_from) & (w_row < channels), 1.0, 0.0).astype(B16)
+    p_row = lax.broadcasted_iota(jnp.int32, (4 * span, 64), 0)
+    p_col = lax.broadcasted_iota(jnp.int32, (4 * span, 64), 1)
+    close = jnp.where(p_col == (p_row // span) * 16 + p_row % span, 1.0, 0.0).astype(B16)
+    gap_row = lax.broadcasted_iota(jnp.int32, (64, 4 * span), 0)
+    gap_col = lax.broadcasted_iota(jnp.int32, (64, 4 * span), 1)
+    reopen = jnp.where(gap_row == (gap_col // span) * 16 + gap_col % span, 1.0, 0.0).astype(B16)
 
     for c in gain_copies + gm_copies:
         c.wait_recv()
-    nrm[...] = jnp.zeros_like(nrm)
-    gmx[...] = jnp.zeros_like(gmx)
     for b in range(N_X):
+        gap = jnp.zeros((cells, 256 - channels), B16)
+        nrm[:, b * 256 + channels : (b + 1) * 256] = gap
+        gmx[:, b * 256 + channels : (b + 1) * 256] = gap
         gmx[:, b * 256 : b * 256 + low] = gma[b]
         packed = gmb[b]
         gmx[:HALF_ROWS, b * 256 + low : b * 256 + channels] = packed[:, :high]
         gmx[HALF_ROWS:, b * 256 + low : b * 256 + channels] = packed[:, high:]
+
+    def two_copies():
+        made = []
+        for k in range(3):
+            place = wtwo_a.at[core, y]
+            made.append(copy(place, place, wtwo_s.at[0, k], wtwo_r.at[0, k], at_y(k + 1)))
+            place = wtwo_b.at[core, near]
+            made.append(copy(place, place, wtwo_s.at[1, k], wtwo_r.at[1, k], at_z(near_steps[k])))
+        return made
+
+    def share_a(k):
+        place = wtwo_a.at[core, (y + N_Y - k) % N_Y]
+        return copy(place, place, wsh_s.at[0, k], wsh_r.at[0, k], sibling)
+
+    def share_b(k):
+        step = 0 if k == 0 else near_steps[k - 1]
+        place = wtwo_b.at[core, (near - step + N_NEAR) % N_NEAR]
+        return copy(place, place, wsh_s.at[1, k], wsh_r.at[1, k], sibling)
+
+    for c in one_copies():
+        c.wait_recv()
+    for f in range(2):
+        rows_a = jnp.concatenate([wone_a[nn, f] for nn in range(N_NEAR)], axis=0)
+        wtwo_a[core, y, f] = dot(close, rows_a).astype(B16)
+        rows_b = jnp.concatenate([wone_b[yy, f] for yy in range(N_Y)], axis=0)
+        wtwo_b[core, near, f] = dot(close, rows_b).astype(B16)
+    for c in two_copies():
+        c.start()
+    share_a(0).start()
+    share_b(0).start()
 
     for c in cv_copies + high_copies:
         c.wait_recv()
@@ -280,33 +327,37 @@
             return carry
 
         lax.fori_loop(0, 4, norm_rows, 0)
-
-    for k in range(1, N_Y):
-        y_copy(k).wait_recv()
-        share(k).start()
-
-    def unit_rows(m, b):
-        return jnp.concatenate(
-            [full[m, yy, nn, b] for yy in range(N_Y) for nn in range(N_NEAR)], axis=0
-        )
-
-    for k in range(N_Y):
-        share(k).wait_recv()
+        if half == 0:
+            arrived = two_copies()
+            for k in range(1, 4):
+                arrived[2 * k - 2].wait_recv()
+                share_a(k).start()
+                arrived[2 * k - 1].wait_recv()
+                share_b(k).start()
+
+    for k in range(4):
+        share_a(k).wait_recv()
+        share_b(k).wait_recv()
     for m in range(2):
-        for b in range(N_X):
-            dense[m, b * 256 : (b + 1) * 256] = dot(widen[...], unit_rows(m, b)).astype(B16)
-
+        for f in range(2):
+            rows_a = jnp.concatenate([wtwo_a[m, yy, f] for yy in range(N_Y)], axis=0)
+            dense[m, f * 256 : (f + 1) * 256] = dot(order[...], rows_a).astype(B16)
+            for nn in range(N_NEAR):
+                r = (f + 2) * 256 + nn * 4 * span
+                dense[m, r : r + 4 * span] = wtwo_b[m, nn, f]
+            dense[m, (f + 2) * 256 + channels : (f + 3) * 256] = jnp.zeros((256 - channels, width), B16)
+
+    pg_copies, sum_copies = [], []
     for half in range(2):
-
-        def mlp_rows(i, carry, half=half):
-            part = pl.ds(pl.multiple_of(i * 128, 128), 128)
-            here = pl.ds(pl.multiple_of(half * HALF_ROWS + i * 128, 128), 128)
+        for i in range(2):
+            start = half * HALF_ROWS + i * 128
+            here = slice(start, start + 128)
+            part = slice(half * 128, half * 128 + 128)
             pre = dot(nrm[here], dense[0])
             edge = 0.5 * (1.0 + lax.erf(pre * root_half))
-            hidden = (pre * edge).astype(B16)
-            hid[here] = hidden
+            hid[here] = (pre * edge).astype(B16)
             slope = edge + pre * jnp.exp(-0.5 * pre * pre) * root_tau
-            grad_pre = (dot_nt_rows(gmx[here], dense[1]) * slope).astype(B16)
+            grad_pre = (dot(gmx[here], dense[1]) * slope).astype(B16)
             gpre[here] = grad_pre
             back = dot_nt(grad_pre, dense[0]).astype(B16)
             first_sum = jnp.zeros((128, 128), F32)
@@ -317,7 +368,7 @@
                 low_part = back[:, b * 256 : b * 256 + low]
                 high_part = back[:, b * 256 + low : b * 256 + channels]
                 pga[b, here] = low_part
-                pgb[b, part, half * high : (half + 1) * high] = high_part
+                pgb[b, part, i * high : (i + 1) * high] = high_part
                 g = low_part.astype(F32) * gains[b, 0:1, 0:low]
                 first_sum += g
                 second_sum += g * cen[b, here, 0:low]
@@ -328,39 +379,73 @@
             two = jnp.sum(second_sum, axis=1, keepdims=True) + jnp.sum(second_high, axis=1, keepdims=True)
             lane = lax.broadcasted_iota(jnp.int32, (128, 128), 1)
             columns = jnp.where(lane == 0, one, jnp.where(lane == 1, two, 0.0))
-            sums[i + 2 * half] = jnp.transpose(columns)[0:8]
-            return carry
-
-        def dot_nt_rows(a, b):
-            return dot(a, b)
-
-        lax.fori_loop(0, 2, mlp_rows, 0)
-
-    pg_copies = x_copies(pga, pgin_a, pg_s.at[0], pg_r.at[0], True)
-    pg_copies += x_copies(pgb, pgin_b, pg_s.at[1], pg_r.at[1], True)
-    sum_copies = []
-    for k in range(1, N_X):
-        sum_copies.append(
-            copy(sums, sums_in.at[k - 1], sum_s.at[k - 1], sum_r.at[k - 1], me, (x + k) % N_X)
-        )
-    for c in sum_copies + pg_copies:
-        c.start()
+            sums[half, i] = jnp.transpose(columns)[0:8]
+        made = []
+        for k in range(1, N_X):
+            other = (x + k) % N_X
+            part = pl.ds(half * HALF_ROWS, HALF_ROWS)
+            made.append(
+                copy(pga.at[other, part], pgin_a.at[k - 1, part], pg_s.at[half, 0, k - 1], pg_r.at[half, 0, k - 1], me, other)
+            )
+            part = pl.ds(half * 128, 128)
+            made.append(
+                copy(pgb.at[other, part], pgin_b.at[k - 1, part], pg_s.at[half, 1, k - 1], pg_r.at[half, 1, k - 1], me, other)
+            )
+            made.append(
+                copy(sums.at[half], sums_in.at[k - 1, half], sum_s.at[half, k - 1], sum_r.at[half, k - 1], me, other)
+            )
+        for c in made:
+            c.start()
+        pg_copies.append(made)
 
     for b in range(N_X):
         for m, left, right in ((0, nrm, gpre), (1, gmx, hid)):
             local = dot_tn(left[:, b * 256 : (b + 1) * 256], right[...]).astype(B16)
-            units = dot_tn(widen[...], local).astype(B16)
-            for yy in range(N_Y):
-                for nn in range(N_NEAR):
-                    r = (yy * N_NEAR + nn) * 16
-                    st[m, yy, nn, b] = units[r : r + 16]
-
-    def gsib_copy(k):
-        yy = (y + k) % N_Y
-        return copy(st.at[1 - core, yy], st_in.at[yy], gsib_s.at[k], gsib_r.at[k], sibling)
+            if b < 2:
+                local = dot_tn(order[...], local).astype(B16)
+            for q in range(4):
+                r = q * 4 * span
+                if b < 2:
+                    st_a[m, q, b] = local[r : r + 4 * span]
+                else:
+                    st_b[m, q, b - 2] = local[r : r + 4 * span]
+
+    back_steps = (-1, 1, 2)
+
+    def one_place(k):
+        step = 0 if k == 0 else back_steps[k - 1]
+        return (y + k) % N_Y, (near + step + N_NEAR) % N_NEAR
+
+    def gsib_copies(k):
+        yy, nn = one_place(k)
+        return (
+            copy(st_a.at[1 - core, yy], st_in_a.at[yy], gsib_s.at[0, k], gsib_r.at[0, k], sibling),
+            copy(st_b.at[1 - core, nn], st_in_b.at[nn], gsib_s.at[1, k], gsib_r.at[1, k], sibling),
+        )
 
     for k in (1, 2, 3, 0):
-        gsib_copy(k).start()
+        for c in gsib_copies(k):
+            c.start()
+
+    def gone_copies(k):
+        return (
+            copy(one_a.at[k], one_in_a.at[k - 1], gone_s.at[0, k - 1], gone_r.at[0, k - 1], at_y(k)),
+            copy(
+                one_b.at[k], one_in_b.at[k - 1], gone_s.at[1, k - 1], gone_r.at[1, k - 1], at_z(back_steps[k - 1])
+            ),
+        )
+
+    for k in (1, 2, 3, 0):
+        yy, nn = one_place(k)
+        over_y, over_z = gsib_copies(k)
+        over_y.wait_recv()
+        one_a[k] = (st_a[core, yy].astype(F32) + st_in_a[yy].astype(F32)).astype(B16)
+        if k > 0:
+            gone_copies(k)[0].start()
+        over_z.wait_recv()
+        one_b[k] = (st_b[core, nn].astype(F32) + st_in_b[nn].astype(F32)).astype(B16)
+        if k > 0:
+            gone_copies(k)[1].start()
 
     for half in range(2):
 
@@ -380,49 +465,40 @@
     for c in mx_copies:
         c.start()
 
-    def gy_copy(k):
-        return copy(ysum.at[k], y_in.at[k - 1], gy_s.at[k - 1], gy_r.at[k - 1], at_y(k))
-
-    for k in (1, 2, 3, 0):
-        gsib_copy(k).wait_recv()
-        yy = (y + k) % N_Y
-        ysum[k] = (st[core, yy].astype(F32) + st_in[yy].astype(F32)).astype(B16)
-        if k > 0:
-            gy_copy(k).start()
-
-    for c in sum_copies + pg_copies:
-        c.wait_recv()
-    for q in range(4):
-        total = sums[q]
-        for k in range(1, N_X):
-            total = total + sums_in[k - 1, q]
-        spread = jnp.concatenate([total / wide, jnp.zeros((120, 128), F32)], axis=0)
-        sum_cols[q * 128 : (q + 1) * 128] = jnp.transpose(spread)
-
     gcv[...] = jnp.zeros_like(gcv)
     for half in range(2):
-
-        def back_rows(i, carry, half=half):
-            part = pl.ds(pl.multiple_of(i * 64, 64), 64)
-            here = pl.ds(pl.multiple_of(half * HALF_ROWS + i * 64, 64), 64)
-            lanes = slice(half * high, (half + 1) * high)
-            low_part = pga[x, here].astype(F32)
-            high_part = pgb[x, part, lanes].astype(F32)
+        for c in pg_copies[half]:
+            c.wait_recv()
+        for i in range(2):
+            total = sums[half, i]
             for k in range(N_X - 1):
-                low_part = low_part + pgin_a[k, here].astype(F32)
-                high_part = high_part + pgin_b[k, part, lanes].astype(F32)
-            e1 = sum_cols[here, 0:1]
-            e2 = sum_cols[here, 1:2]
-            scale = inv[here]
-            g = low_part * gains[x, 0:1, 0:low]
-            g = scale * (g - e1 - cen[x, here, 0:low] * e2)
-            gcv[half * 4 + i, :, :, 0:low] = g.astype(B16).astype(F32).reshape(SIDE, TILE, low)
-            g = high_part * gains[x, 0:1, low:channels]
-            g = scale[:, :high] * (g - e1 - cen[x, here, low:channels] * e2)
-            gcv[half * 4 + i, :, :, low:channels] = g.astype(B16).astype(F32).reshape(SIDE, TILE, high)
-            return carry
-
-        lax.fori_loop(0, 4, back_rows, 0)
+                total = total + sums_in[k, half, i]
+            spread = jnp.concatenate([total / wide, jnp.zeros((120, 128), F32)], axis=0)
+            sum_cols[...] = jnp.transpose(spread)
+            lanes = slice(i * high, (i + 1) * high)
+
+            def back_rows(n, carry, half=half, i=i, lanes=lanes):
+                column = half * 4 + i * 2 + n
+                part = pl.ds(pl.multiple_of(half * 128 + n * 64, 64), 64)
+                here = pl.ds(pl.multiple_of(column * 64, 64), 64)
+                low_part = pga[x, here].astype(F32)
+                high_part = pgb[x, part, lanes].astype(F32)
+                for k in range(N_X - 1):
+                    low_part = low_part + pgin_a[k, here].astype(F32)
+                    high_part = high_part + pgin_b[k, part, lanes].astype(F32)
+                local = pl.ds(pl.multiple_of(n * 64, 64), 64)
+                e1 = sum_cols[local, 0:1]
+                e2 = sum_cols[local, 1:2]
+                scale = inv[here]
+                g = low_part * gains[x, 0:1, 0:low]
+                g = scale * (g - e1 - cen[x, here, 0:low] * e2)
+                gcv[column, :, :, 0:low] = g.astype(B16).astype(F32).reshape(SIDE, TILE, low)
+                g = high_part * gains[x, 0:1, low:channels]
+                g = scale[:, :high] * (g - e1 - cen[x, here, low:channels] * e2)
+                gcv[column, :, :, low:channels] = g.astype(B16).astype(F32).reshape(SIDE, TILE, high)
+                return carry
+
+            lax.fori_loop(0, 2, back_rows, 0)
 
     def spread_column(j, start, size):
         def add_tap(b, totals):
@@ -463,31 +539,40 @@
     ret_west.start()
     ret_east.start()
 
-    for k in range(1, N_Y):
-        gy_copy(k).wait_recv()
-    for nn in range(N_NEAR):
-        total = ysum[0, nn].astype(F32)
-        for k in range(1, N_Y):
-            total = total + y_in[k - 1, nn].astype(F32)
-        nsum[nn] = total.astype(B16)
-
-    back_steps = (-1, 1, 2)
-
-    def gnear_copy(k):
-        target = (near + back_steps[k] + N_NEAR) % N_NEAR
-        return copy(nsum.at[target], n_in.at[k], gnear_s.at[k], gnear_r.at[k], at_z(back_steps[k]))
-
+    def gtwo_copies(k):
+        yy, nn = one_place(k)
+        return (
+            copy(two_a.at[nn], two_in_a.at[k - 1], gtwo_s.at[0, k - 1], gtwo_r.at[0, k - 1], at_z(back_steps[k - 1])),
+            copy(two_b.at[yy], two_in_b.at[k - 1], gtwo_s.at[1, k - 1], gtwo_r.at[1, k - 1], at_y(k)),
+        )
+
+    for k in range(1, 4):
+        for c in gone_copies(k):
+            c.wait_recv()
+    for f in range(2):
+        for mine, came, units in ((one_a, one_in_a, two_a), (one_b, one_in_b, two_b)):
+            total = mine[0, f].astype(F32)
+            for k in range(3):
+                total = total + came[k, f].astype(F32)
+            opened = dot(reopen, total.astype(B16)).astype(B16)
+            for q in range(4):
+                units[q, f] = opened[q * 16 : (q + 1) * 16]
+    for k in range(1, 4):
+        for c in gtwo_copies(k):
+            c.start()
+
+    lax.fori_loop(3, 11, spread_inner, 0)
+
+    for k in range(1, 4):
+        for c in gtwo_copies(k):
+            c.wait_recv()
+    total = two_a[near].astype(F32)
+    other_total = two_b[y].astype(F32)
     for k in range(3):
-        gnear_copy(k).start()
-
-    lax.fori_loop(3, 11, spread_inner, 0)
-
-    for k in range(3):
-        gnear_copy(k).wait_recv()
-    total = nsum[near].astype(F32)
-    for k in range(3):
-        total = total + n_in[k].astype(F32)
-    fsum[...] = total
+        total = total + two_in_a[k].astype(F32)
+        other_total = other_total + two_in_b[k].astype(F32)
+    fsum[0:2] = total
+    fsum[2:4] = other_total
 
     def gfar_copy(k):
         return copy(
@@ -513,7 +598,7 @@
         packed = packed + mxin_b[k].astype(F32)
     high_part = jnp.concatenate([packed[:, :high], packed[:, high:]], axis=0)
     mixed = jnp.concatenate([low_part, high_part], axis=1)
-    out = (xt[...].astype(F32) + scale_ref[...] * mixed).astype(B16)
+    out = (xt[...].astype(F32) + scale_row * mixed).astype(B16)
     block_ref[...] = dot_tn(out, perm[...]).astype(B16)
 
     for k in range(1, N_FAR):
@@ -523,9 +608,9 @@
         total = total + f_in[k - 1]
     last[0, 0:8] = total[0:8]
     last[1, 0:8] = total[rows : rows + 8]
-    gend = copy(last.at[1 - core], last_in, gend_s, gend_r, sibling)
+    gend = copy(last.at[1 - core], last_in.at[core], gend_s, gend_r, sibling)
     gend.start()
-    wgrad_ref[core] = last[core]
+    last_in[core] = last[core]
 
     ret_west.wait_recv()
     ret_east.wait_recv()
@@ -536,14 +621,18 @@
     grad_ref[...] = dot_tn(tg[...].reshape(cells, channels).astype(B16), perm[...]).astype(B16)
 
     gend.wait_recv()
-    wgrad_ref[1 - core] = last_in[...]
+    up_grad_ref[...] = last_in[0, 0:rows]
+    down_grad_ref[...] = last_in[1, 0:rows]
 
     sent = [halo_west, halo_east, wsib, ret_west, ret_east, gend]
-    sent += gain_copies + gm_copies + cv_copies + high_copies + pg_copies + sum_copies + mx_copies
-    sent += [far_copy(k) for k in range(1, N_FAR)] + [near_copy(k) for k in range(3)]
-    sent += [y_copy(k) for k in range(1, N_Y)] + [share(k) for k in range(N_Y)]
-    sent += [gsib_copy(k) for k in range(N_Y)] + [gy_copy(k) for k in range(1, N_Y)]
-    sent += [gnear_copy(k) for k in range(3)] + [gfar_copy(k) for k in range(1, N_FAR)]
+    sent += gain_copies + gm_copies + cv_copies + high_copies + mx_copies + pg_copies[0] + pg_copies[1]
+    sent += [far_copy(k) for k in range(1, N_FAR)] + one_copies() + two_copies()
+    sent += [share_a(k) for k in range(4)] + [share_b(k) for k in range(4)]
+    for k in range(4):
+        sent += gsib_copies(k)
+    for k in range(1, 4):
+        sent += gone_copies(k) + gtwo_copies(k)
+    sent += [gfar_copy(k) for k in range(1, N_FAR)]
     for c in sent:
         c.wait_send()
 
@@ -553,24 +642,16 @@
 ):
     channels, cells = tiles.shape
     rows, width = w_up.shape
-    gap = jnp.zeros((8 - rows, width), w_up.dtype)
-    shard = jnp.concatenate([w_up, gap, w_down, gap], axis=0)
-    links = jnp.concatenate(
-        [neighbors.reshape(TILE, 8), shifts.reshape(TILE, 8), halo_widths], axis=1
-    )
-    land_row = land.reshape(1, cells).astype(B16)
-    gain = jnp.broadcast_to(norm_gain.astype(F32)[None], (8, channels))
-    scale = layer_scale.astype(F32)[None]
-    high = channels - 128
     vmem = pl.BlockSpec(memory_space=pltpu.VMEM)
     dma = pltpu.SemaphoreType.DMA
 
     def v(dtype, *shape):
         return pltpu.VMEM(shape, dtype)
 
-    quarter = (N_NEAR, N_FAR, 16, width)
+    strip = (2, 8 * rows, width)
+    units = (2, 16, width)
     scratch = [
-        v(B16, cells, cells), v(B16, 256, 256), v(B16, 12, 64, 64), v(F32, TAPS, TAPS, 8, channels),
+        v(B16, cells, cells), v(B16, 256, channels), v(B16, 12, 64, 64), v(F32, TAPS, TAPS, 8, channels),
         v(B16, cells, channels), v(B16, cells, channels), v(B16, 192, channels), v(B16, 192, channels),
         v(F32, SIDE + 6, SIDE + 6, TILE, channels), v(F32, N_X, 8, channels),
         v(B16, N_X, cells, 128), v(B16, N_X, HALF_ROWS, 128), v(B16, N_X, cells, 128), v(B16, N_X, HALF_ROWS, 128),
@@ -578,34 +659,39 @@
         v(B16, cells, width), v(B16, cells, width),
         v(B16, N_X, cells, 128), v(B16, N_X, HALF_ROWS, 128), v(B16, 3, cells, 128), v(B16, 3, HALF_ROWS, 128),
         v(B16, N_X, cells, 128), v(B16, N_X, HALF_ROWS, 128), v(B16, 3, cells, 128), v(B16, 3, HALF_ROWS, 128),
-        v(F32, 4, 8, 128), v(F32, 3, 4, 8, 128), v(F32, cells, 128),
+        v(F32, 2, 2, 8, 128), v(F32, 3, 2, 2, 8, 128), v(F32, 128, 128),
         v(F32, SIDE, SIDE, TILE, channels), v(F32, SIDE + 6, SIDE + 6, TILE, channels),
         v(B16, 192, channels), v(B16, 192, channels), v(B16, 192, channels), v(B16, 192, channels),
         v(F32, SIDE, SIDE, TILE, channels),
-        v(B16, 16, width), v(B16, 2, 16, width), v(B16, 2, N_Y, *quarter), v(B16, 2, N_X * 256, width),
-        v(B16, 2, N_Y, *quarter), v(B16, N_Y, *quarter), v(B16, N_Y, *quarter), v(B16, 3, *quarter),
-        v(B16, *quarter), v(B16, 3, N_FAR, 16, width), v(F32, N_FAR, 16, width), v(F32, 3, 16, width),
-        v(F32, 2, 8, width), v(F32, 8, width),
+        v(B16, 2, 16, width), v(B16, N_FAR, 16, width), v(B16, 4, *units), v(B16, 4, *units),
+        v(B16, 2, 4, *strip), v(B16, 2, 4, *strip), v(B16, 2, N_X * 256, width),
+        v(B16, 2, 4, *strip), v(B16, 2, 4, *strip), v(B16, 4, *strip), v(B16, 4, *strip),
+        v(B16, 4, *strip), v(B16, 4, *strip), v(B16, 3, *strip), v(B16, 3, *strip),
+        v(B16, 4, *units), v(B16, 4, *units), v(B16, 3, *units), v(B16, 3, *units),
+        v(F32, N_FAR, 16, width), v(F32, 3, 16, width), v(F32, 2, 8, width), v(F32, 2, 8, width),
     ]
-    pairs = [(2,), (3,), (2, 3), (2, 3), (2, 3), (2, 3), (3,), (2,), None, (3,), (3,), (3,), (4,)]
-    pairs += [(4,), (3,), (3,), (3,), None]
+    pairs = [(2,), (3,), (2, 3), (2, 3), (2, 2, 3), (2, 3), (2, 3), (2,), None, (3,), (2, 3), (2, 3), (2, 4)]
+    pairs += [(2, 4), (2, 3), (2, 3), (3,), None]
     for p in pairs:
         scratch += [dma if p is None else dma(p)] * 2
-    block_out, tile_grad, both = pl.pallas_call(
+    return pl.pallas_call(
         functools.partial(block_kernel, rows, width),
         out_shape=[
             jax.ShapeDtypeStruct((channels, cells), B16),
             jax.ShapeDtypeStruct((channels, cells), B16),
-            jax.ShapeDtypeStruct((2, 8, width), F32),
+            jax.ShapeDtypeStruct((rows, width), F32),
+            jax.ShapeDtypeStruct((rows, width), F32),
         ],
-        in_specs=[vmem] * 8,
-        out_specs=[vmem] * 3,
+        in_specs=[vmem] * 11,
+        out_specs=[vmem] * 4,
         scratch_shapes=scratch,
         compiler_params=pltpu.CompilerParams(
             collective_id=0, has_side_effects=True, vmem_limit_bytes=56 * 1024 * 1024
         ),
-    )(tiles, cotangent, land_row, kernel, gain, scale, links, shard)
-    return block_out, tile_grad, both[0, :rows], both[1, :rows]
+    )(
+        tiles, cotangent, land, kernel, norm_gain.reshape(1, channels), layer_scale.reshape(1, channels),
+        neighbors.reshape(TILE, 8), shifts.reshape(TILE, 8), halo_widths, w_up, w_down,
+    )
 
 
 def solution(mesh):

time: 92.5 us -> 82.2 us (0.89)
  Pallas kernels: 82.7 us -> 73.6 us
  other arithmetic: 2.53 us -> 0 us
  local copies, waits for them, and re-layouts: 5.88 us -> 7.54 us
    pallas_call x1, Pallas kernels: 82.7 us -> 73.6 us  [per_device(): pl.pallas_call(functools.partial(block_kernel, rows, width), out_shape=[j...]
    reshape x0 -> x2, local copies, waits for them, and re-layouts: none -> 1.81 us  [the longest x1 1.23 us: per_device(): norm_gain.reshape(1, channels)]
    squeeze x1 -> x0, local copies, waits for them, and re-layouts: 1.33 us -> none  [per_device(): return (block_out, tile_grad, both[0, :rows], both[1, :rows])]
    concatenate x2 -> x0, other arithmetic: 1.28 us -> none  [the longest x1 0.67 us: per_device(): jnp.concatenate([neighbors.reshape(TILE, 8), shifts.reshape(TILE, 8), hal...]
    unnamed x19, local copies, waits for them, and re-layouts: 3.13 us -> 4.4 us
    broadcast_in_dim x1 -> x0, other arithmetic: 1.25 us -> none  [per_device(): scale = layer_scale.astype(F32)[None]]
where the time goes in v3:
time: 82.2 us; the launch traced here: 81.9 us
  Pallas kernels  73.6 us (90%)
  local copies, waits for them, and re-layouts  7.54 us (9%)
    pallas_call x1, Pallas kernels, per_device(): pl.pallas_call(functools.partial(block_kernel, rows, width), out_shape=[j...  73.6 us
    unnamed x19, local copies, waits for them, and re-layouts  4.4 us

profile of v3, /device:TPU:1, one launch (start us, length us, event | category | flops | bytes accessed | tf_op | source)
XLA Modules:
  0.0 81.9 jit_solution(11609323306961185179)
XLA Ops:
  0.6 0.0 copy-start.3
  0.6 0.0 copy-start.6
  0.7 1.2 %reshape.20.gain_ref = bf16[1,192]{1,0:T(2,128)(2,1)} reshape(bf16[192]{0:T(256)(128)(2,1)} %param.13) | data formatting | bytes 768 | tf_op jit(solution)/shard_map/reshape | solution.py:692
  1.9 0.0 copy-done.6
  1.9 0.6 reshape.21.scale_ref
  2.5 0.0 copy-done.3
  2.5 0.0 copy-start.4
  2.5 0.7 copy.15.owner_ref
  3.1 0.0 copy-done.4
  3.2 0.0 copy-start.5
  3.2 0.7 copy.16.shift_ref
  3.8 0.0 copy-done.5
  3.8 0.7 copy.17.depth_ref
  4.5 73.6 %shard_map.138 = (bf16[192,512]{1,0:T(8,128)(2,1)}, bf16[192,512]{1,0:T(8,128)(2,1)}, f32[6,384]{1,0:T(8,128)}, f32[6,384]{1,0:T(8,128)}) custom-call(bf16[192,512]{1,0:T(8,128)(2,1)} %x_ref.1, bf16[192,512]{1,0:T(8,128)(2,1)} %cot_ref.1, s32[8,8,8]{2,1,0:T(8,128)} %land_ref.1, bf16[49,192]{1,0:T(8,128)(2,1)} %taps_ref.1, bf16[1,192]{1,0:T(2,128)(2,1)} %reshape.20.gain_ref, ...), custom_call_target="tpu_custom_call" | custom-call | tf_op jit(solution)/shard_map/pallas_call | solution.py:677
  78.2 0.0 copy-start
  78.2 1.7 %copy.22 = bf16[192,512]{1,0:T(8,128)(2,1)} copy(bf16[192,512]{1,0:T(8,128)(2,1)} %get-tuple-element.8) | data formatting | bytes 393216
  79.8 0.0 copy-done
  79.8 0.0 copy-start.2
  79.8 0.7 copy.23
  80.5 0.0 copy-done.2
  80.5 0.0 copy-start.1
  80.5 0.6 copy.24
  81.1 0.1 copy-done.1
  81.3 0.6 copy.25
Async XLA Ops:
  0.6 1.8 %copy-start.3 = (s32[8,4,2]{0,2,1:T(2,128)S(1)}, s32[8,4,2]{0,2,1:T(2,128)}, u32[]{:S(2)}) copy-start(s32[8,4,2]{0,2,1:T(2,128)} %param.17) | copy-start | bytes 772
  0.6 1.2 %copy-start.6 = (bf16[192]{0:T(256)(128)(2,1)S(1)}, bf16[192]{0:T(256)(128)(2,1)}, u32[]{:S(2)}) copy-start(bf16[192]{0:T(256)(128)(2,1)} %param.16) | copy-start | bytes 1156
  2.5 0.7 copy-start.4
  3.2 0.7 copy-start.5
  78.2 1.7 %copy-start = (bf16[192,512]{1,0:T(8,128)(2,1)S(1)}, bf16[192,512]{1,0:T(8,128)(2,1)}, u32[]{:S(2)}) copy-start(bf16[192,512]{1,0:T(8,128)(2,1)} %get-tuple-element.9) | copy-start | bytes 589828
  79.8 0.7 copy-start.2
  80.5 0.7 copy-start.1

commit v4 on v3

--- a/solution.py
+++ b/solution.py
@@ -42,12 +42,12 @@
     block_ref, grad_ref, up_grad_ref, down_grad_ref,
     perm, order, picks, taps, xt, go, east_in, west_in, pad, gains,
     gma, gmb, cva, cvb, cen, inv, nrm, gmx, hid, gpre,
-    pga, pgb, pgin_a, pgin_b, mxa, mxb, mxin_a, mxin_b, sums, sums_in, sum_cols,
+    pga, pgb, pgin_a, pgin_b, pgre_a, pgre_b, mxa, mxb, mxin_a, mxin_b, mxre_a, mxre_b, sums, sums_in, sum_cols,
     gcv, gpad, ret_w, ret_e, ret_w_in, ret_e_in, tg,
     unit_in, wfar, wone_a, wone_b, wtwo_a, wtwo_b, dense,
     st_a, st_b, st_in_a, st_in_b, one_a, one_b, one_in_a, one_in_b, two_a, two_b, two_in_a, two_in_b,
     fsum, f_in, last, last_in,
-    halo_s, halo_r, gain_s, gain_r, gm_s, gm_r, cv_s, cv_r, pg_s, pg_r, mx_s, mx_r, sum_s, sum_r,
+    x_in, cot_in, in_sem, halo_s, halo_r, gain_s, gain_r, gm_s, gm_r, cv_s, cv_r, pg_s, pg_r, mx_s, mx_r, sum_s, sum_r,
     ret_s, ret_r, wsib_s, wsib_r, wfar_s, wfar_r, wone_s, wone_r, wtwo_s, wtwo_r, wsh_s, wsh_r,
     gsib_s, gsib_r, gone_s, gone_r, gtwo_s, gtwo_r, gfar_s, gfar_r, gend_s, gend_r,
 ):
@@ -80,12 +80,18 @@
     greeted += [(at_y(k), x) for k in range(1, N_Y)]
     for other in greeted:
         pl.semaphore_signal(barrier, inc=1, device_id=other, device_id_type=MESH)
+    x_load = pltpu.make_async_copy(x_ref, x_in, in_sem.at[0])
+    cot_load = pltpu.make_async_copy(cot_ref, cot_in, in_sem.at[1])
+    x_load.start()
+    cot_load.start()
 
     out_cell = lax.broadcasted_iota(jnp.int32, (cells, cells), 0)
     in_cell = lax.broadcasted_iota(jnp.int32, (cells, cells), 1)
     wanted = (out_cell % 8) * 64 + ((out_cell // 8) % 8) * 8 + out_cell // 64
     perm[...] = jnp.where(in_cell == wanted, 1.0, 0.0).astype(B16)
-    xt[...] = dot_nt(perm[...], x_ref[...]).astype(B16)
+    x_load.wait()
+    xt[...] = dot_nt(perm[...], x_in[...]).astype(B16)
+    cot_load.wait()
     j_row = lax.broadcasted_iota(jnp.int32, (SIDE, cells), 0)
     j_col = lax.broadcasted_iota(jnp.int32, (SIDE, cells), 1)
     spread_j = jnp.where(j_row == j_col % SIDE, 1.0, 0.0).astype(B16)
@@ -95,12 +101,12 @@
     land_row = jnp.sum(
         jnp.where(ti_row == ti_col // SIDE, dot(land, spread_j), 0.0), axis=0, keepdims=True
     ).astype(B16)
-    go[...] = dot_nt(perm[...], cot_ref[...] * land_row).astype(B16)
-    scale_row = scale_ref[...].astype(F32)
+    go[...] = dot_nt(perm[...], cot_in[...] * land_row).astype(B16)
+    scale_row = scale_ref[...].astype(F32).reshape(1, channels)
     grad_mixed = (go[...].astype(F32) * scale_row).astype(B16)
     gma[x] = grad_mixed[:, :low]
     gmb[x] = jnp.concatenate([grad_mixed[:HALF_ROWS, low:], grad_mixed[HALF_ROWS:, low:]], axis=1)
-    gains[x] = jnp.broadcast_to(gain_ref[...].astype(F32), (8, channels))
+    gains[x] = jnp.broadcast_to(gain_ref[...].astype(F32).reshape(1, channels), (8, channels))
     s_row = lax.broadcasted_iota(jnp.int32, (16, rows), 0)
     s_col = lax.broadcasted_iota(jnp.int32, (16, rows), 1)
     unit_in[core] = (
@@ -117,41 +123,79 @@
     wsib = copy(unit_in.at[core], unit_in.at[core], wsib_s, wsib_r, sibling)
     wsib.start()
 
-    def x_copies(src, dst, send, recv, scatter):
+    right, left, across = (x + 1) % N_X, (x + N_X - 1) % N_X, (x + 2) % N_X
+
+    def gather_first(buffer, send, recv):
+        return [
+            copy(buffer.at[x], buffer.at[x], send.at[0], recv.at[0], me, right),
+            copy(buffer.at[x], buffer.at[x], send.at[1], recv.at[1], me, left),
+        ]
+
+    def gather_next(buffer, send, recv):
+        count = buffer.shape[1] // 2
+        head, tail = pl.ds(0, count), pl.ds(count, count)
+        return [
+            copy(buffer.at[left, head], buffer.at[left, head], send.at[2], recv.at[2], me, right),
+            copy(buffer.at[right, tail], buffer.at[right, tail], send.at[3], recv.at[3], me, left),
+        ]
+
+    def forward(first, later):
+        for c, n in zip(first, later):
+            c.wait_recv()
+            n.start()
+
+    gain_copies = []
+    for k in range(1, N_X):
+        gain_copies.append(
+            copy(gains.at[x], gains.at[x], gain_s.at[k - 1], gain_r.at[k - 1], me, (x + k) % N_X)
+        )
+    gm_first = gather_first(gma, gm_s.at[0], gm_r.at[0]), gather_first(gmb, gm_s.at[1], gm_r.at[1])
+    gm_next = gather_next(gma, gm_s.at[0], gm_r.at[0]), gather_next(gmb, gm_s.at[1], gm_r.at[1])
+    for c in gm_first[0] + gm_first[1] + gain_copies:
+        c.start()
+
+    def scatter_copies(held, came, relay, send, recv, half):
+        toward, away = (right, left) if half == 0 else (left, right)
         made = []
-        for k in range(1, N_X):
-            other = (x + k) % N_X
-            if scatter:
-                pair = (src.at[other], dst.at[k - 1])
-            else:
-                pair = (src.at[x], dst.at[x])
-            made.append(copy(*pair, send.at[k - 1], recv.at[k - 1], me, other))
+        for p in range(2):
+            count = held[p].shape[1] // 2
+            part = pl.ds(half * count, count)
+            made.append((
+                copy(held[p].at[across, part], relay[p].at[half], send.at[half, 0, p], recv.at[half, 0, p], me, toward),
+                copy(
+                    held[p].at[away, part], came[p].at[1 - half, part], send.at[half, 1, p], recv.at[half, 1, p], me, away
+                ),
+                copy(
+                    held[p].at[toward, part], came[p].at[half, part], send.at[half, 2, p], recv.at[half, 2, p], me, toward
+                ),
+            ))
         return made
 
-    gain_copies = x_copies(gains, gains, gain_s, gain_r, False)
-    gm_copies = x_copies(gma, gma, gm_s.at[0], gm_r.at[0], False)
-    gm_copies += x_copies(gmb, gmb, gm_s.at[1], gm_r.at[1], False)
-    for c in gain_copies + gm_copies:
-        c.start()
+    def relay_on(held, relay, made, half):
+        toward = right if half == 0 else left
+        for p in range(2):
+            count = held[p].shape[1] // 2
+            part = pl.ds(half * count, count)
+            made[p][0].wait_recv()
+            held[p][toward, part] = (held[p][toward, part].astype(F32) + relay[p][half].astype(F32)).astype(B16)
+            made[p][2].start()
+
+    pg_made = [scatter_copies((pga, pgb), (pgin_a, pgin_b), (pgre_a, pgre_b), pg_s, pg_r, h) for h in range(2)]
+    mx_made = [scatter_copies((mxa, mxb), (mxin_a, mxin_b), (mxre_a, mxre_b), mx_s, mx_r, h) for h in range(2)]
 
     edge_row = lax.broadcasted_iota(jnp.int32, (64, 64), 0)
-    edge_col = lax.broadcasted_iota(jnp.int32, (64, 64), 1)
-    owners = jnp.concatenate([owner_ref[...]] * 8, axis=0)
-    moves = jnp.concatenate([shift_ref[...]] * 8, axis=0)
-    depths = jnp.concatenate([depth_ref[...]] * 8, axis=0)
     for face in range(4):
         chosen = jnp.zeros((64, 64), F32)
         for entry in range(2):
-            c = face * 2 + entry
-            owner = owners[:, c : c + 1]
-            shift = moves[:, c : c + 1]
+            owner = owner_ref[face, entry : entry + 1, :]
+            shift = shift_ref[face, entry : entry + 1, :]
             target = jnp.where(owner >= 0, owner % TILE + TILE * shift, -4096)
-            target = target + (edge_row // 8) * 8
-            chosen = chosen + jnp.where(target == edge_col, 1.0, 0.0)
+            target = jnp.concatenate([target + TILE * p for p in range(SIDE)], axis=1)
+            chosen = chosen + jnp.where(target == edge_row, 1.0, 0.0)
+        widths = jnp.concatenate([depth_ref[face : face + 1, :]] * SIDE, axis=1)
         for layer in range(3):
             depth = 3 - layer if face in (0, 2) else layer + 1
-            keep = depths[:, face : face + 1] >= depth
-            picks[face * 3 + layer] = jnp.where(keep, chosen, 0.0).astype(B16)
+            picks[face * 3 + layer] = jnp.where(widths >= depth, chosen, 0.0).astype(B16)
 
     kernel_taps = taps_ref[...].astype(F32)
     for a in range(TAPS):
@@ -165,9 +209,9 @@
     for layer in range(3):
         north = cells_f[:, 5 + layer].reshape(64, channels).astype(B16)
         south = cells_f[:, layer].reshape(64, channels).astype(B16)
-        pad[3 : 3 + SIDE, layer] = dot(picks[layer], north).astype(B16).astype(F32).reshape(SIDE, TILE, channels)
+        pad[3 : 3 + SIDE, layer] = dot_tn(picks[layer], north).astype(B16).astype(F32).reshape(SIDE, TILE, channels)
         pad[3 : 3 + SIDE, 11 + layer] = (
-            dot(picks[3 + layer], south).astype(B16).astype(F32).reshape(SIDE, TILE, channels)
+            dot_tn(picks[3 + layer], south).astype(B16).astype(F32).reshape(SIDE, TILE, channels)
         )
 
     wsib.wait_recv()
@@ -191,10 +235,10 @@
     for layer in range(3):
         part = pl.ds(layer * 64, 64)
         pad[layer, 3 : 3 + SIDE] = (
-            dot(picks[6 + layer], west_in[part]).astype(B16).astype(F32).reshape(SIDE, TILE, channels)
+            dot_tn(picks[6 + layer], west_in[part]).astype(B16).astype(F32).reshape(SIDE, TILE, channels)
         )
         pad[11 + layer, 3 : 3 + SIDE] = (
-            dot(picks[9 + layer], east_in[part]).astype(B16).astype(F32).reshape(SIDE, TILE, channels)
+            dot_tn(picks[9 + layer], east_in[part]).astype(B16).astype(F32).reshape(SIDE, TILE, channels)
         )
 
     def conv_column(j, start, size):
@@ -216,8 +260,9 @@
         return carry
 
     lax.fori_loop(0, SIDE, conv_low, 0)
-    cv_copies = x_copies(cva, cva, cv_s.at[0], cv_r.at[0], False)
-    for c in cv_copies:
+    cv_first = gather_first(cva, cv_s.at[0], cv_r.at[0])
+    cv_next = gather_next(cva, cv_s.at[0], cv_r.at[0])
+    for c in cv_first:
         c.start()
 
     for k in range(1, N_FAR):
@@ -240,9 +285,12 @@
         c.start()
 
     lax.fori_loop(0, 4, conv_high, 0)
-    high_copies = x_copies(cvb, cvb, cv_s.at[1], cv_r.at[1], False)
-    for c in high_copies:
+    high_first = gather_first(cvb, cv_s.at[1], cv_r.at[1])
+    high_next = gather_next(cvb, cv_s.at[1], cv_r.at[1])
+    for c in high_first:
         c.start()
+    forward(gm_first[0], gm_next[0])
+    forward(gm_first[1], gm_next[1])
 
     span = N_CORE * rows
     w_row = lax.broadcasted_iota(jnp.int32, (256, channels), 0)
@@ -256,17 +304,6 @@
     gap_col = lax.broadcasted_iota(jnp.int32, (64, 4 * span), 1)
     reopen = jnp.where(gap_row == (gap_col // span) * 16 + gap_col % span, 1.0, 0.0).astype(B16)
 
-    for c in gain_copies + gm_copies:
-        c.wait_recv()
-    for b in range(N_X):
-        gap = jnp.zeros((cells, 256 - channels), B16)
-        nrm[:, b * 256 + channels : (b + 1) * 256] = gap
-        gmx[:, b * 256 + channels : (b + 1) * 256] = gap
-        gmx[:, b * 256 : b * 256 + low] = gma[b]
-        packed = gmb[b]
-        gmx[:HALF_ROWS, b * 256 + low : b * 256 + channels] = packed[:, :high]
-        gmx[HALF_ROWS:, b * 256 + low : b * 256 + channels] = packed[:, high:]
-
     def two_copies():
         made = []
         for k in range(3):
@@ -297,7 +334,20 @@
     share_a(0).start()
     share_b(0).start()
 
-    for c in cv_copies + high_copies:
+    forward(cv_first, cv_next)
+    forward(high_first, high_next)
+    for c in gm_next[0] + gm_next[1]:
+        c.wait_recv()
+    for b in range(N_X):
+        gap = jnp.zeros((cells, 256 - channels), B16)
+        nrm[:, b * 256 + channels : (b + 1) * 256] = gap
+        gmx[:, b * 256 + channels : (b + 1) * 256] = gap
+        gmx[:, b * 256 : b * 256 + low] = gma[b]
+        packed = gmb[b]
+        gmx[:HALF_ROWS, b * 256 + low : b * 256 + channels] = packed[:, :high]
+        gmx[HALF_ROWS:, b * 256 + low : b * 256 + channels] = packed[:, high:]
+
+    for c in gain_copies + cv_next + high_next:
         c.wait_recv()
 
     wide = float(channels * N_X)
@@ -347,7 +397,7 @@
                 dense[m, r : r + 4 * span] = wtwo_b[m, nn, f]
             dense[m, (f + 2) * 256 + channels : (f + 3) * 256] = jnp.zeros((256 - channels, width), B16)
 
-    pg_copies, sum_copies = [], []
+    sum_copies = []
     for half in range(2):
         for i in range(2):
             start = half * HALF_ROWS + i * 128
@@ -383,24 +433,21 @@
         made = []
         for k in range(1, N_X):
             other = (x + k) % N_X
-            part = pl.ds(half * HALF_ROWS, HALF_ROWS)
-            made.append(
-                copy(pga.at[other, part], pgin_a.at[k - 1, part], pg_s.at[half, 0, k - 1], pg_r.at[half, 0, k - 1], me, other)
-            )
-            part = pl.ds(half * 128, 128)
-            made.append(
-                copy(pgb.at[other, part], pgin_b.at[k - 1, part], pg_s.at[half, 1, k - 1], pg_r.at[half, 1, k - 1], me, other)
-            )
             made.append(
                 copy(sums.at[half], sums_in.at[k - 1, half], sum_s.at[half, k - 1], sum_r.at[half, k - 1], me, other)
             )
+        for p in range(2):
+            pg_made[half][p][0].start()
+        for p in range(2):
+            pg_made[half][p][1].start()
         for c in made:
             c.start()
-        pg_copies.append(made)
+        sum_copies.append(made)
+    relay_on((pga, pgb), (pgre_a, pgre_b), pg_made[0], 0)
 
     for b in range(N_X):
-        for m, left, right in ((0, nrm, gpre), (1, gmx, hid)):
-            local = dot_tn(left[:, b * 256 : (b + 1) * 256], right[...]).astype(B16)
+        for m, inner, outer in ((0, nrm, gpre), (1, gmx, hid)):
+            local = dot_tn(inner[:, b * 256 : (b + 1) * 256], outer[...]).astype(B16)
             if b < 2:
                 local = dot_tn(order[...], local).astype(B16)
             for q in range(4):
@@ -427,6 +474,8 @@
         for c in gsib_copies(k):
             c.start()
 
+    relay_on((pga, pgb), (pgre_a, pgre_b), pg_made[1], 1)
+
     def gone_copies(k):
         return (
             copy(one_a.at[k], one_in_a.at[k - 1], gone_s.at[0, k - 1], gone_r.at[0, k - 1], at_y(k)),
@@ -441,34 +490,33 @@
         over_y.wait_recv()
         one_a[k] = (st_a[core, yy].astype(F32) + st_in_a[yy].astype(F32)).astype(B16)
         if k > 0:
-            gone_copies(k)[0].start()
+            to_y, to_z = gone_copies(k)
+            to_y.start()
         over_z.wait_recv()
         one_b[k] = (st_b[core, nn].astype(F32) + st_in_b[nn].astype(F32)).astype(B16)
         if k > 0:
-            gone_copies(k)[1].start()
+            to_z.start()
 
     for half in range(2):
-
-        def out_rows(i, carry, half=half):
-            part = pl.ds(pl.multiple_of(i * 128, 128), 128)
-            here = pl.ds(pl.multiple_of(half * HALF_ROWS + i * 128, 128), 128)
-            mixed = dot_nt(hid[here], dense[1]).astype(B16)
+        for i in range(2):
+            start = half * HALF_ROWS + i * 128
+            mixed = dot_nt(hid[start : start + 128], dense[1]).astype(B16)
             for b in range(N_X):
-                mxa[b, here] = mixed[:, b * 256 : b * 256 + low]
-                mxb[b, part, half * high : (half + 1) * high] = mixed[:, b * 256 + low : b * 256 + channels]
-            return carry
-
-        lax.fori_loop(0, 2, out_rows, 0)
-
-    mx_copies = x_copies(mxa, mxin_a, mx_s.at[0], mx_r.at[0], True)
-    mx_copies += x_copies(mxb, mxin_b, mx_s.at[1], mx_r.at[1], True)
-    for c in mx_copies:
-        c.start()
+                mxa[b, start : start + 128] = mixed[:, b * 256 : b * 256 + low]
+                mxb[b, half * 128 : half * 128 + 128, i * high : (i + 1) * high] = mixed[
+                    :, b * 256 + low : b * 256 + channels
+                ]
+        for p in range(2):
+            mx_made[half][p][0].start()
+            mx_made[half][p][1].start()
 
     gcv[...] = jnp.zeros_like(gcv)
     for half in range(2):
-        for c in pg_copies[half]:
+        for c in sum_copies[half]:
             c.wait_recv()
+        for p in range(2):
+            pg_made[half][p][1].wait_recv()
+            pg_made[half][p][2].wait_recv()
         for i in range(2):
             total = sums[half, i]
             for k in range(N_X - 1):
@@ -483,7 +531,7 @@
                 here = pl.ds(pl.multiple_of(column * 64, 64), 64)
                 low_part = pga[x, here].astype(F32)
                 high_part = pgb[x, part, lanes].astype(F32)
-                for k in range(N_X - 1):
+                for k in range(2):
                     low_part = low_part + pgin_a[k, here].astype(F32)
                     high_part = high_part + pgin_b[k, part, lanes].astype(F32)
                 local = pl.ds(pl.multiple_of(n * 64, 64), 64)
@@ -528,12 +576,14 @@
         spread_column(j, low, high)
         return carry
 
+    for half in range(2):
+        relay_on((mxa, mxb), (mxre_a, mxre_b), mx_made[half], half)
     lax.fori_loop(0, 3, spread_edge, 0)
     for layer in range(3):
         part = pl.ds(layer * 64, 64)
         for face, column, held in ((2, layer, ret_w), (3, 11 + layer, ret_e)):
             edge = gpad[column, 3 : 3 + SIDE].reshape(64, channels).astype(B16)
-            held[part] = dot_tn(picks[face * 3 + layer], edge).astype(B16)
+            held[part] = dot(picks[face * 3 + layer], edge).astype(B16)
     ret_west = copy(ret_w, ret_w_in, ret_s.at[0], ret_r.at[0], west)
     ret_east = copy(ret_e, ret_e_in, ret_s.at[1], ret_r.at[1], east)
     ret_west.start()
@@ -586,17 +636,20 @@
     for layer in range(3):
         for face, row, target in ((0, layer, 5 + layer), (1, 11 + layer, layer)):
             edge = gpad[3 : 3 + SIDE, row].reshape(64, channels).astype(B16)
-            back = dot_tn(picks[face * 3 + layer], edge)
+            back = dot(picks[face * 3 + layer], edge)
             tg[:, target] = tg[:, target] + back.reshape(SIDE, TILE, channels)
 
-    for c in mx_copies:
-        c.wait_recv()
+    for half in range(2):
+        for p in range(2):
+            mx_made[half][p][1].wait_recv()
+            mx_made[half][p][2].wait_recv()
     low_part = mxa[x].astype(F32)
     packed = mxb[x].astype(F32)
-    for k in range(N_X - 1):
+    for k in range(2):
         low_part = low_part + mxin_a[k].astype(F32)
         packed = packed + mxin_b[k].astype(F32)
-    high_part = jnp.concatenate([packed[:, :high], packed[:, high:]], axis=0)
+    tops, ends = packed[:128], packed[128:]
+    high_part = jnp.concatenate([tops[:, :high], tops[:, high:], ends[:, :high], ends[:, high:]], axis=0)
     mixed = jnp.concatenate([low_part, high_part], axis=1)
     out = (xt[...].astype(F32) + scale_row * mixed).astype(B16)
     block_ref[...] = dot_tn(out, perm[...]).astype(B16)
@@ -625,7 +678,10 @@
     down_grad_ref[...] = last_in[1, 0:rows]
 
     sent = [halo_west, halo_east, wsib, ret_west, ret_east, gend]
-    sent += gain_copies + gm_copies + cv_copies + high_copies + mx_copies + pg_copies[0] + pg_copies[1]
+    sent += gain_copies + gm_first[0] + gm_first[1] + gm_next[0] + gm_next[1]
+    sent += cv_first + cv_next + high_first + high_next + sum_copies[0] + sum_copies[1]
+    for made in pg_made + mx_made:
+        sent += made[0] + made[1]
     sent += [far_copy(k) for k in range(1, N_FAR)] + one_copies() + two_copies()
     sent += [share_a(k) for k in range(4)] + [share_b(k) for k in range(4)]
     for k in range(4):
@@ -637,6 +693,11 @@
         c.wait_send()
 
 
+def hand_over(*refs):
+    for i in range(4):
+        refs[4 + i][...] = refs[i][...]
+
+
 def per_device(
     tiles, kernel, norm_gain, w_up, w_down, layer_scale, neighbors, shifts, halo_widths, land, cotangent
 ):
@@ -657,8 +718,10 @@
         v(B16, N_X, cells, 128), v(B16, N_X, HALF_ROWS, 128), v(B16, N_X, cells, 128), v(B16, N_X, HALF_ROWS, 128),
         v(F32, N_X, cells, channels), v(F32, cells, 128), v(B16, cells, N_X * 256), v(B16, cells, N_X * 256),
         v(B16, cells, width), v(B16, cells, width),
-        v(B16, N_X, cells, 128), v(B16, N_X, HALF_ROWS, 128), v(B16, 3, cells, 128), v(B16, 3, HALF_ROWS, 128),
-        v(B16, N_X, cells, 128), v(B16, N_X, HALF_ROWS, 128), v(B16, 3, cells, 128), v(B16, 3, HALF_ROWS, 128),
+        v(B16, N_X, cells, 128), v(B16, N_X, HALF_ROWS, 128), v(B16, 2, cells, 128), v(B16, 2, HALF_ROWS, 128),
+        v(B16, 2, HALF_ROWS, 128), v(B16, 2, 128, 128),
+        v(B16, N_X, cells, 128), v(B16, N_X, HALF_ROWS, 128), v(B16, 2, cells, 128), v(B16, 2, HALF_ROWS, 128),
+        v(B16, 2, HALF_ROWS, 128), v(B16, 2, 128, 128),
         v(F32, 2, 2, 8, 128), v(F32, 3, 2, 2, 8, 128), v(F32, 128, 128),
         v(F32, SIDE, SIDE, TILE, channels), v(F32, SIDE + 6, SIDE + 6, TILE, channels),
         v(B16, 192, channels), v(B16, 192, channels), v(B16, 192, channels), v(B16, 192, channels),
@@ -670,28 +733,36 @@
         v(B16, 4, *units), v(B16, 4, *units), v(B16, 3, *units), v(B16, 3, *units),
         v(F32, N_FAR, 16, width), v(F32, 3, 16, width), v(F32, 2, 8, width), v(F32, 2, 8, width),
     ]
-    pairs = [(2,), (3,), (2, 3), (2, 3), (2, 2, 3), (2, 3), (2, 3), (2,), None, (3,), (2, 3), (2, 3), (2, 4)]
+    scratch += [v(B16, channels, cells), v(B16, channels, cells), dma((2,))]
+    pairs = [(2,), (3,), (2, 4), (2, 4), (2, 3, 2), (2, 3, 2), (2, 3), (2,), None, (3,), (2, 3), (2, 3), (2, 4)]
     pairs += [(2, 4), (2, 3), (2, 3), (3,), None]
     for p in pairs:
         scratch += [dma if p is None else dma(p)] * 2
-    return pl.pallas_call(
+    shapes = [
+        jax.ShapeDtypeStruct((channels, cells), B16),
+        jax.ShapeDtypeStruct((channels, cells), B16),
+        jax.ShapeDtypeStruct((rows, width), F32),
+        jax.ShapeDtypeStruct((rows, width), F32),
+    ]
+    made = pl.pallas_call(
         functools.partial(block_kernel, rows, width),
-        out_shape=[
-            jax.ShapeDtypeStruct((channels, cells), B16),
-            jax.ShapeDtypeStruct((channels, cells), B16),
-            jax.ShapeDtypeStruct((rows, width), F32),
-            jax.ShapeDtypeStruct((rows, width), F32),
-        ],
-        in_specs=[vmem] * 11,
+        out_shape=shapes,
+        in_specs=[pl.BlockSpec(memory_space=pl.ANY)] * 2 + [vmem] * 9,
         out_specs=[vmem] * 4,
         scratch_shapes=scratch,
         compiler_params=pltpu.CompilerParams(
             collective_id=0, has_side_effects=True, vmem_limit_bytes=56 * 1024 * 1024
         ),
     )(
-        tiles, cotangent, land, kernel, norm_gain.reshape(1, channels), layer_scale.reshape(1, channels),
-        neighbors.reshape(TILE, 8), shifts.reshape(TILE, 8), halo_widths, w_up, w_down,
+        tiles, cotangent, land, kernel, norm_gain, layer_scale,
+        jnp.transpose(neighbors, (1, 2, 0)), jnp.transpose(shifts, (1, 2, 0)), halo_widths.T, w_up, w_down,
     )
+    return pl.pallas_call(
+        hand_over,
+        out_shape=shapes,
+        in_specs=[vmem] * 4,
+        out_specs=[vmem] * 4,
+    )(*made)
 
 
 def solution(mesh):

time: 82.2 us -> 77.9 us (0.948)
  local copies, waits for them, and re-layouts: 7.54 us -> 0 us
  Pallas kernels: 73.6 us -> 77 us
    unnamed x19 -> x0, local copies, waits for them, and re-layouts: 4.4 us -> none
    pallas_call x1 -> x2, Pallas kernels: 73.6 us -> 77 us  [the longest x1 75.3 us: per_device(): pl.pallas_call(functools.partial(block_kernel, rows, width), out_shape=sh...]
    reshape x4 -> x0, local copies, waits for them, and re-layouts: 3.13 us -> none  [the longest x1 1.23 us: per_device(): norm_gain.reshape(1, channels)]
where the time goes in v4:
time: 77.9 us; the launch traced here: 77.7 us
  Pallas kernels  77 us (99%)
    pallas_call x1, Pallas kernels, per_device(): pl.pallas_call(functools.partial(block_kernel, rows, width), out_shape=sh...  75.3 us
    pallas_call x1, Pallas kernels, per_device(): pl.pallas_call(hand_over, out_shape=shapes, in_specs=[vmem] * 4, out_spec...  1.79 us

profile of v4, /device:TPU:1, one launch (start us, length us, event | category | flops | bytes accessed | tf_op | source)
XLA Modules:
  0.0 77.7 jit_solution(13958059124573360214)
XLA Ops:
  0.6 75.3 %shard_map.138 = (bf16[192,512]{1,0:T(8,128)(2,1)}, bf16[192,512]{1,0:T(8,128)(2,1)}, f32[6,384]{1,0:T(8,128)}, f32[6,384]{1,0:T(8,128)}) custom-call(bf16[192,512]{1,0:T(8,128)(2,1)} %x_ref.1, bf16[192,512]{1,0:T(8,128)(2,1)} %cot_ref.1, s32[8,8,8]{2,1,0:T(8,128)} %land_ref.1, bf16[49,192]{1,0:T(8,128)(2,1)} %taps_ref.1, bf16[192]{0:T(256)(128)(2,1)} %gain_ref.1, ...), custom_call_target="tpu_custom_call" | custom-call | tf_op jit(solution)/shard_map/pallas_call | solution.py:747
  75.9 1.8 %shard_map.139 = (bf16[192,512]{1,0:T(8,128)(2,1)}, bf16[192,512]{1,0:T(8,128)(2,1)}, f32[6,384]{1,0:T(8,128)}, f32[6,384]{1,0:T(8,128)}) custom-call(bf16[192,512]{1,0:T(8,128)(2,1)} %get-tuple-element.8.refs_0_, bf16[192,512]{1,0:T(8,128)(2,1)} %get-tuple-element.9.refs_1_, f32[6,384]{1,0:T(8,128)} %get-tuple-element.10.refs_2_, ...), custom_call_target="tpu_custom_call" | custom-call | tf_op jit(solution)/shard_map/pallas_call | solution.py:760

commit v5 on v4

--- a/solution.py
+++ b/solution.py
@@ -85,21 +85,22 @@
     x_load.start()
     cot_load.start()
 
-    out_cell = lax.broadcasted_iota(jnp.int32, (cells, cells), 0)
-    in_cell = lax.broadcasted_iota(jnp.int32, (cells, cells), 1)
-    wanted = (out_cell % 8) * 64 + ((out_cell // 8) % 8) * 8 + out_cell // 64
-    perm[...] = jnp.where(in_cell == wanted, 1.0, 0.0).astype(B16)
+    out_cell = lax.broadcasted_iota(jnp.int32, (cells, 128), 0)
+    in_cell = lax.broadcasted_iota(jnp.int32, (cells, 128), 1)
+    wanted = ((out_cell & 7) << 6) + (((out_cell >> 3) & 7) << 3) + (out_cell >> 6)
+    for start in range(0, cells, 128):
+        perm[:, start : start + 128] = jnp.where(in_cell + start == wanted, 1.0, 0.0).astype(B16)
     x_load.wait()
     xt[...] = dot_nt(perm[...], x_in[...]).astype(B16)
     cot_load.wait()
     j_row = lax.broadcasted_iota(jnp.int32, (SIDE, cells), 0)
     j_col = lax.broadcasted_iota(jnp.int32, (SIDE, cells), 1)
-    spread_j = jnp.where(j_row == j_col % SIDE, 1.0, 0.0).astype(B16)
+    spread_j = jnp.where(j_row == (j_col & 7), 1.0, 0.0).astype(B16)
     land = land_ref[...].astype(F32).reshape(TILE * SIDE, SIDE).astype(B16)
     ti_row = lax.broadcasted_iota(jnp.int32, (TILE * SIDE, cells), 0)
     ti_col = lax.broadcasted_iota(jnp.int32, (TILE * SIDE, cells), 1)
     land_row = jnp.sum(
-        jnp.where(ti_row == ti_col // SIDE, dot(land, spread_j), 0.0), axis=0, keepdims=True
+        jnp.where(ti_row == (ti_col >> 3), dot(land, spread_j), 0.0), axis=0, keepdims=True
     ).astype(B16)
     go[...] = dot_nt(perm[...], cot_in[...] * land_row).astype(B16)
     scale_row = scale_ref[...].astype(F32).reshape(1, channels)
@@ -189,13 +190,26 @@
         for entry in range(2):
             owner = owner_ref[face, entry : entry + 1, :]
             shift = shift_ref[face, entry : entry + 1, :]
-            target = jnp.where(owner >= 0, owner % TILE + TILE * shift, -4096)
+            target = jnp.where(owner >= 0, (owner & 7) + TILE * shift, -4096)
             target = jnp.concatenate([target + TILE * p for p in range(SIDE)], axis=1)
             chosen = chosen + jnp.where(target == edge_row, 1.0, 0.0)
         widths = jnp.concatenate([depth_ref[face : face + 1, :]] * SIDE, axis=1)
         for layer in range(3):
             depth = 3 - layer if face in (0, 2) else layer + 1
             picks[face * 3 + layer] = jnp.where(widths >= depth, chosen, 0.0).astype(B16)
+
+    span = N_CORE * rows
+    w_row = lax.broadcasted_iota(jnp.int32, (256, channels), 0)
+    w_col = lax.broadcasted_iota(jnp.int32, (256, channels), 1)
+    w_strip = (w_row * 171) >> 11
+    w_from = (w_strip & 3) * (span * N_NEAR) + (w_strip >> 2) * span + (w_row - w_strip * span)
+    order[...] = jnp.where((w_col == w_from) & (w_row < channels), 1.0, 0.0).astype(B16)
+    p_row = lax.broadcasted_iota(jnp.int32, (4 * span, 64), 0)
+    p_col = lax.broadcasted_iota(jnp.int32, (4 * span, 64), 1)
+    close = jnp.where(p_col == p_row + 4 * ((p_row * 171) >> 11), 1.0, 0.0).astype(B16)
+    gap_row = lax.broadcasted_iota(jnp.int32, (64, 4 * span), 0)
+    gap_col = lax.broadcasted_iota(jnp.int32, (64, 4 * span), 1)
+    reopen = jnp.where(gap_row == gap_col + 4 * ((gap_col * 171) >> 11), 1.0, 0.0).astype(B16)
 
     kernel_taps = taps_ref[...].astype(F32)
     for a in range(TAPS):
@@ -291,18 +305,6 @@
         c.start()
     forward(gm_first[0], gm_next[0])
     forward(gm_first[1], gm_next[1])
-
-    span = N_CORE * rows
-    w_row = lax.broadcasted_iota(jnp.int32, (256, channels), 0)
-    w_col = lax.broadcasted_iota(jnp.int32, (256, channels), 1)
-    w_from = ((w_row // span) % N_Y) * (span * N_NEAR) + (w_row // (span * N_Y)) * span + w_row % span
-    order[...] = jnp.where((w_col == w_from) & (w_row < channels), 1.0, 0.0).astype(B16)
-    p_row = lax.broadcasted_iota(jnp.int32, (4 * span, 64), 0)
-    p_col = lax.broadcasted_iota(jnp.int32, (4 * span, 64), 1)
-    close = jnp.where(p_col == (p_row // span) * 16 + p_row % span, 1.0, 0.0).astype(B16)
-    gap_row = lax.broadcasted_iota(jnp.int32, (64, 4 * span), 0)
-    gap_col = lax.broadcasted_iota(jnp.int32, (64, 4 * span), 1)
-    reopen = jnp.where(gap_row == (gap_col // span) * 16 + gap_col % span, 1.0, 0.0).astype(B16)
 
     def two_copies():
         made = []

time: 77.9 us -> 78.6 us (level)
  no operation moved by 1% of the time
where the time goes in v5:
time: 78.6 us; the launch traced here: 78.4 us
  Pallas kernels  77.7 us (99%)
    pallas_call x1, Pallas kernels, per_device(): pl.pallas_call(functools.partial(block_kernel, rows, width), out_shape=sh...  75.9 us
    pallas_call x1, Pallas kernels, per_device(): pl.pallas_call(hand_over, out_shape=shapes, in_specs=[vmem] * 4, out_spec...  1.79 us

profile of v5, /device:TPU:1, one launch (start us, length us, event | category | flops | bytes accessed | tf_op | source)
XLA Modules:
  0.0 78.4 jit_solution(3176052268569323605)
XLA Ops:
  0.6 75.9 %shard_map.138 = (bf16[192,512]{1,0:T(8,128)(2,1)}, bf16[192,512]{1,0:T(8,128)(2,1)}, f32[6,384]{1,0:T(8,128)}, f32[6,384]{1,0:T(8,128)}) custom-call(bf16[192,512]{1,0:T(8,128)(2,1)} %x_ref.1, bf16[192,512]{1,0:T(8,128)(2,1)} %cot_ref.1, s32[8,8,8]{2,1,0:T(8,128)} %land_ref.1, bf16[49,192]{1,0:T(8,128)(2,1)} %taps_ref.1, bf16[192]{0:T(256)(128)(2,1)} %gain_ref.1, ...), custom_call_target="tpu_custom_call" | custom-call | tf_op jit(solution)/shard_map/pallas_call | solution.py:749
  76.6 1.8 %shard_map.139 = (bf16[192,512]{1,0:T(8,128)(2,1)}, bf16[192,512]{1,0:T(8,128)(2,1)}, f32[6,384]{1,0:T(8,128)}, f32[6,384]{1,0:T(8,128)}) custom-call(bf16[192,512]{1,0:T(8,128)(2,1)} %get-tuple-element.8.refs_0_, bf16[192,512]{1,0:T(8,128)(2,1)} %get-tuple-element.9.refs_1_, f32[6,384]{1,0:T(8,128)} %get-tuple-element.10.refs_2_, ...), custom_call_target="tpu_custom_call" | custom-call | tf_op jit(solution)/shard_map/pallas_call | solution.py:762

commit v6 on v4

--- a/solution.py
+++ b/solution.py
@@ -576,19 +576,6 @@
         spread_column(j, low, high)
         return carry
 
-    for half in range(2):
-        relay_on((mxa, mxb), (mxre_a, mxre_b), mx_made[half], half)
-    lax.fori_loop(0, 3, spread_edge, 0)
-    for layer in range(3):
-        part = pl.ds(layer * 64, 64)
-        for face, column, held in ((2, layer, ret_w), (3, 11 + layer, ret_e)):
-            edge = gpad[column, 3 : 3 + SIDE].reshape(64, channels).astype(B16)
-            held[part] = dot(picks[face * 3 + layer], edge).astype(B16)
-    ret_west = copy(ret_w, ret_w_in, ret_s.at[0], ret_r.at[0], west)
-    ret_east = copy(ret_e, ret_e_in, ret_s.at[1], ret_r.at[1], east)
-    ret_west.start()
-    ret_east.start()
-
     def gtwo_copies(k):
         yy, nn = one_place(k)
         return (
@@ -611,6 +598,19 @@
         for c in gtwo_copies(k):
             c.start()
 
+    lax.fori_loop(0, 3, spread_edge, 0)
+    for layer in range(3):
+        part = pl.ds(layer * 64, 64)
+        for face, column, held in ((2, layer, ret_w), (3, 11 + layer, ret_e)):
+            edge = gpad[column, 3 : 3 + SIDE].reshape(64, channels).astype(B16)
+            held[part] = dot(picks[face * 3 + layer], edge).astype(B16)
+    ret_west = copy(ret_w, ret_w_in, ret_s.at[0], ret_r.at[0], west)
+    ret_east = copy(ret_e, ret_e_in, ret_s.at[1], ret_r.at[1], east)
+    ret_west.start()
+    ret_east.start()
+
+    for half in range(2):
+        relay_on((mxa, mxb), (mxre_a, mxre_b), mx_made[half], half)
     lax.fori_loop(3, 11, spread_inner, 0)
 
     for k in range(1, 4):
@@ -638,6 +638,14 @@
             edge = gpad[3 : 3 + SIDE, row].reshape(64, channels).astype(B16)
             back = dot(picks[face * 3 + layer], edge)
             tg[:, target] = tg[:, target] + back.reshape(SIDE, TILE, channels)
+
+    ret_west.wait_recv()
+    ret_east.wait_recv()
+    for layer in range(3):
+        part = pl.ds(layer * 64, 64)
+        tg[5 + layer] = tg[5 + layer] + ret_w_in[part].astype(F32).reshape(SIDE, TILE, channels)
+        tg[layer] = tg[layer] + ret_e_in[part].astype(F32).reshape(SIDE, TILE, channels)
+    grad_ref[...] = dot_tn(tg[...].reshape(cells, channels).astype(B16), perm[...]).astype(B16)
 
     for half in range(2):
         for p in range(2):
@@ -664,14 +672,6 @@
     gend = copy(last.at[1 - core], last_in.at[core], gend_s, gend_r, sibling)
     gend.start()
     last_in[core] = last[core]
-
-    ret_west.wait_recv()
-    ret_east.wait_recv()
-    for layer in range(3):
-        part = pl.ds(layer * 64, 64)
-        tg[5 + layer] = tg[5 + layer] + ret_w_in[part].astype(F32).reshape(SIDE, TILE, channels)
-        tg[layer] = tg[layer] + ret_e_in[part].astype(F32).reshape(SIDE, TILE, channels)
-    grad_ref[...] = dot_tn(tg[...].reshape(cells, channels).astype(B16), perm[...]).astype(B16)
 
     gend.wait_recv()
     up_grad_ref[...] = last_in[0, 0:rows]

time: 77.9 us -> 77.8 us (level)
  no operation moved by 1% of the time
where the time goes in v6:
time: 77.8 us; the launch traced here: 77.5 us
  Pallas kernels  76.9 us (99%)
    pallas_call x1, Pallas kernels, per_device(): pl.pallas_call(functools.partial(block_kernel, rows, width), out_shape=sh...  75.1 us
    pallas_call x1, Pallas kernels, per_device(): pl.pallas_call(hand_over, out_shape=shapes, in_specs=[vmem] * 4, out_spec...  1.79 us

profile of v6, /device:TPU:1, one launch (start us, length us, event | category | flops | bytes accessed | tf_op | source)
XLA Modules:
  0.0 77.5 jit_solution(14342247087066707646)
XLA Ops:
  0.6 75.1 %shard_map.138 = (bf16[192,512]{1,0:T(8,128)(2,1)}, bf16[192,512]{1,0:T(8,128)(2,1)}, f32[6,384]{1,0:T(8,128)}, f32[6,384]{1,0:T(8,128)}) custom-call(bf16[192,512]{1,0:T(8,128)(2,1)} %x_ref.1, bf16[192,512]{1,0:T(8,128)(2,1)} %cot_ref.1, s32[8,8,8]{2,1,0:T(8,128)} %land_ref.1, bf16[49,192]{1,0:T(8,128)(2,1)} %taps_ref.1, bf16[192]{0:T(256)(128)(2,1)} %gain_ref.1, ...), custom_call_target="tpu_custom_call" | custom-call | tf_op jit(solution)/shard_map/pallas_call | solution.py:747
  75.8 1.8 %shard_map.139 = (bf16[192,512]{1,0:T(8,128)(2,1)}, bf16[192,512]{1,0:T(8,128)(2,1)}, f32[6,384]{1,0:T(8,128)}, f32[6,384]{1,0:T(8,128)}) custom-call(bf16[192,512]{1,0:T(8,128)(2,1)} %get-tuple-element.8.refs_0_, bf16[192,512]{1,0:T(8,128)(2,1)} %get-tuple-element.9.refs_1_, f32[6,384]{1,0:T(8,128)} %get-tuple-element.10.refs_2_, ...), custom_call_target="tpu_custom_call" | custom-call | tf_op jit(solution)/shard_map/pallas_call | solution.py:760

commit v7 on v6

--- a/solution.py
+++ b/solution.py
@@ -443,7 +443,19 @@
         for c in made:
             c.start()
         sum_copies.append(made)
-    relay_on((pga, pgb), (pgre_a, pgre_b), pg_made[0], 0)
+
+    back_steps = (-1, 1, 2)
+
+    def one_place(k):
+        step = 0 if k == 0 else back_steps[k - 1]
+        return (y + k) % N_Y, (near + step + N_NEAR) % N_NEAR
+
+    def gsib_copies(k):
+        yy, nn = one_place(k)
+        return (
+            copy(st_a.at[1 - core, yy], st_in_a.at[yy], gsib_s.at[0, k], gsib_r.at[0, k], sibling),
+            copy(st_b.at[1 - core, nn], st_in_b.at[nn], gsib_s.at[1, k], gsib_r.at[1, k], sibling),
+        )
 
     for b in range(N_X):
         for m, inner, outer in ((0, nrm, gpre), (1, gmx, hid)):
@@ -457,22 +469,11 @@
                 else:
                     st_b[m, q, b - 2] = local[r : r + 4 * span]
 
-    back_steps = (-1, 1, 2)
-
-    def one_place(k):
-        step = 0 if k == 0 else back_steps[k - 1]
-        return (y + k) % N_Y, (near + step + N_NEAR) % N_NEAR
-
-    def gsib_copies(k):
-        yy, nn = one_place(k)
-        return (
-            copy(st_a.at[1 - core, yy], st_in_a.at[yy], gsib_s.at[0, k], gsib_r.at[0, k], sibling),
-            copy(st_b.at[1 - core, nn], st_in_b.at[nn], gsib_s.at[1, k], gsib_r.at[1, k], sibling),
-        )
-
-    for k in (1, 2, 3, 0):
-        for c in gsib_copies(k):
-            c.start()
+        if b % 2 == 1:
+            for k in (1, 2, 3, 0):
+                gsib_copies(k)[b // 2].start()
+        if b == 1:
+            relay_on((pga, pgb), (pgre_a, pgre_b), pg_made[0], 0)
 
     relay_on((pga, pgb), (pgre_a, pgre_b), pg_made[1], 1)
 

time: 77.8 us -> 76.5 us (0.983)
  Pallas kernels: 76.9 us -> 75.6 us
    pallas_call x1, Pallas kernels: 75.1 us -> 73.8 us  [per_device(): pl.pallas_call(functools.partial(block_kernel, rows, width), out_shape=sh...]
where the time goes in v7:
time: 76.5 us; the launch traced here: 76.3 us
  Pallas kernels  75.6 us (99%)
    pallas_call x1, Pallas kernels, per_device(): pl.pallas_call(functools.partial(block_kernel, rows, width), out_shape=sh...  73.8 us
    pallas_call x1, Pallas kernels, per_device(): pl.pallas_call(hand_over, out_shape=shapes, in_specs=[vmem] * 4, out_spec...  1.79 us

profile of v7, /device:TPU:1, one launch (start us, length us, event | category | flops | bytes accessed | tf_op | source)
XLA Modules:
  0.0 76.3 jit_solution(10290018946786599229)
XLA Ops:
  0.6 73.8 %shard_map.138 = (bf16[192,512]{1,0:T(8,128)(2,1)}, bf16[192,512]{1,0:T(8,128)(2,1)}, f32[6,384]{1,0:T(8,128)}, f32[6,384]{1,0:T(8,128)}) custom-call(bf16[192,512]{1,0:T(8,128)(2,1)} %x_ref.1, bf16[192,512]{1,0:T(8,128)(2,1)} %cot_ref.1, s32[8,8,8]{2,1,0:T(8,128)} %land_ref.1, bf16[49,192]{1,0:T(8,128)(2,1)} %taps_ref.1, bf16[192]{0:T(256)(128)(2,1)} %gain_ref.1, ...), custom_call_target="tpu_custom_call" | custom-call | tf_op jit(solution)/shard_map/pallas_call | solution.py:748
  74.5 1.8 %shard_map.139 = (bf16[192,512]{1,0:T(8,128)(2,1)}, bf16[192,512]{1,0:T(8,128)(2,1)}, f32[6,384]{1,0:T(8,128)}, f32[6,384]{1,0:T(8,128)}) custom-call(bf16[192,512]{1,0:T(8,128)(2,1)} %get-tuple-element.8.refs_0_, bf16[192,512]{1,0:T(8,128)(2,1)} %get-tuple-element.9.refs_1_, f32[6,384]{1,0:T(8,128)} %get-tuple-element.10.refs_2_, ...), custom_call_target="tpu_custom_call" | custom-call | tf_op jit(solution)/shard_map/pallas_call | solution.py:761
